TPU v7x, 32 devices: a whole 2x2x4 slice. The times are simulated.
32 devices in a mesh: dp: 2 (over y), row: 4 (over z), col: 4 (over x, core).
Axes of the slice: x: 2, y: 2, z: 4, core: 2. Of those that a mesh axis runs over, the one named last changes fastest.
Arguments:
- block_input: bfloat16 [2048, 2048], P(('dp', 'row'), 'col'), may hold values from -6 to 6
- mixer_gain: float32 [2048], P('col'), may hold values from 0.25 to 1.75
- ssm_gate_weight: bfloat16 [2048, 3072], P('col', 'row'), may hold values from -0.125 to 0.125
- ssm_input_weight: bfloat16 [2048, 3072], P('col', 'row'), may hold values from -0.125 to 0.125
- ssm_bc_weight: bfloat16 [2048, 512], P('col', 'row'), may hold values from -0.125 to 0.125
- ssm_step_weight: bfloat16 [2048, 48], P('col', 'row'), may hold values from -0.125 to 0.125
- query_weight: bfloat16 [2048, 1024], P('col', 'row'), may hold values from -0.125 to 0.125
- keyval_weight: bfloat16 [2048, 512], P('col', 'row'), may hold values from -0.125 to 0.125
- conv_input: float32 [4, 3072], P(None, ('row', 'col')), may hold values from -0.5 to 0.5
- conv_states: float32 [4, 512], P(None, ('row', 'col')), may hold values from -0.5 to 0.5
- step_bias: float32 [48], P(('row', 'col')), may hold values from -6 to -2
- decay_log: float32 [48], P(('row', 'col')), may hold values from 0 to 2.8
- skip_gain: float32 [48], P(('row', 'col')), may hold values from 0.5 to 4
- ssm_norm_gain: float32 [3072], P(('row', 'col')), may hold values from 0.25 to 1.75
- ssm_out_weight: bfloat16 [3072, 2048], P('row', 'col'), may hold values from -0.109375 to 0.109375
- attn_out_weight: bfloat16 [1024, 2048], P('row', 'col'), may hold values from -3 to 3
- ffn_gain: float32 [2048], P('col'), may hold values from 0.25 to 1.75
- gate_up_weight: bfloat16 [2048, 2, 4096], P('col', None, 'row'), may hold values from -0.125 to 0.125
- down_weight: bfloat16 [4096, 2048], P('row', 'col'), may hold values from -0.09375 to 0.09375
- cotangent: float32 [2048, 2048], P(('dp', 'row'), 'col'), may hold values from -6 to 6
Outputs:
- output: bfloat16 [2048, 2048], P(('dp', 'row'), 'col')
- input_grad: float32 [2048, 2048], P(('dp', 'row'), 'col')
- mixer_gain_grad: float32 [2048], P('col')
- ssm_gate_grad: float32 [2048, 3072], P('col', 'row')
- ssm_input_grad: float32 [2048, 3072], P('col', 'row')
- ssm_bc_grad: float32 [2048, 512], P('col', 'row')
- ssm_step_grad: float32 [2048, 48], P('col', 'row')
- query_grad: float32 [2048, 1024], P('col', 'row')
- keyval_grad: float32 [2048, 512], P('col', 'row')
- conv_input_grad: float32 [4, 3072], P(None, ('row', 'col'))
- conv_states_grad: float32 [4, 512], P(None, ('row', 'col'))
- step_bias_grad: float32 [48], P(('row', 'col'))
- decay_log_grad: float32 [48], P(('row', 'col'))
- skip_gain_grad: float32 [48], P(('row', 'col'))
- ssm_norm_gain_grad: float32 [3072], P(('row', 'col'))
- ssm_out_grad: float32 [3072, 2048], P('row', 'col')
- attn_out_grad: float32 [1024, 2048], P('row', 'col')
- ffn_gain_grad: float32 [2048], P('col')
- gate_up_grad: float32 [2048, 2, 4096], P('col', None, 'row')
- down_grad: float32 [4096, 2048], P('row', 'col')
All inputs are finite; a program needn't handle non-finite values.
Results may differ from a plain program's by a relative error of at most 0.012.
Values may be sent and summed in bfloat16 or wider, within the bound.
A program may use at most 192 MiB of HBM per device.

v0:
```python
from functools import partial

import jax
import jax.numpy as jnp
from jax import lax
from jax.sharding import PartitionSpec as P

D = 2048
HEADS = 48
HDIM = 64
QHEADS = 8
KVHEADS = 2
ADIM = 128
LEN = 1024
SPAN = 256


EPSILON = 1e-05
ROPE_BASE = 100000000000.0
HIGHEST = lax.Precision.HIGHEST
NEGATIVE = -1e30


def softplus(values):
    return jnp.maximum(values, 0.0) + jnp.log1p(jnp.exp(-jnp.abs(values)))


def causal_conv(series, kernel):
    taps = kernel.shape[0]
    length = series.shape[1]
    padded = jnp.pad(series, ((0, 0), (taps - 1, 0), (0, 0)))
    total = jnp.zeros(series.shape, jnp.float32)
    for kernel_row in range(taps):
        total = total + padded[:, kernel_row : kernel_row + length, :] * kernel[kernel_row]
    return total


def conv_piece(raw_cols, kernel, seq_count):
    tokens = raw_cols.shape[0]
    shaped = raw_cols.reshape(seq_count, tokens // seq_count, raw_cols.shape[1])
    return jax.nn.silu(causal_conv(shaped, kernel)).reshape(tokens, raw_cols.shape[1])


def ssd_block(state, block):
    xdt, b_rows, c_rows, rates = block
    size_q = rates.shape[1]
    within = jnp.cumsum(rates, axis=1)
    rows_i = lax.broadcasted_iota(jnp.int32, (size_q, size_q), 0)
    cols_j = lax.broadcasted_iota(jnp.int32, (size_q, size_q), 1)
    lower = (cols_j <= rows_i)[None, :, :, None]
    gaps = within[:, :, None, :] - within[:, None, :, :]
    decay = jnp.where(lower, jnp.exp(jnp.where(lower, gaps, 0.0)), 0.0)
    scores = jnp.einsum("sin,sjn->sij", c_rows, b_rows, precision=HIGHEST)
    inner = jnp.einsum("sijh,sjhp->sihp", scores[..., None] * decay, xdt, precision=HIGHEST)
    carried = (
        jnp.einsum("sin,shpn->sihp", c_rows, state, precision=HIGHEST) * jnp.exp(within)[..., None]
    )
    last_sum = within[:, -1, :]
    weights = jnp.exp(last_sum[:, None, :] - within)
    fresh = jnp.einsum("sjhp,sjn->shpn", xdt * weights[..., None], b_rows, precision=HIGHEST)
    new_state = state * jnp.exp(last_sum)[:, :, None, None] + fresh
    return (new_state, inner + carried)


def ssd_scan(xdt, b_rows, c_rows, rates):
    seq_count, length, heads, head_dim = xdt.shape
    blocks = length // SPAN

    def split_blocks(values):
        shaped = values.reshape((seq_count, blocks, SPAN) + values.shape[2:])
        return jnp.moveaxis(shaped, 1, 0)

    state = jnp.zeros((seq_count, heads, head_dim, b_rows.shape[2]), jnp.float32)
    _, outputs = lax.scan(
        jax.checkpoint(ssd_block),
        state,
        (split_blocks(xdt), split_blocks(b_rows), split_blocks(c_rows), split_blocks(rates)),
    )
    return jnp.moveaxis(outputs, 0, 1).reshape(seq_count, length, heads, head_dim)


def mamba_core(
    seq_count, x_raw, z_cols, step_raw, bc_full, conv_input, step_bias, decay_log, skip_gain
):
    tokens, breadth = x_raw.shape
    heads = step_raw.shape[1]
    head_dim = breadth // heads
    length = tokens // seq_count
    states_n = bc_full.shape[1] // 2
    mixed_x = conv_piece(x_raw, conv_input, seq_count).reshape(seq_count, length, heads, head_dim)
    steps_dt = softplus(step_raw + step_bias).reshape(seq_count, length, heads)
    rates = -steps_dt * jnp.exp(decay_log)
    b_rows = bc_full[:, :states_n].reshape(seq_count, length, states_n)
    c_rows = bc_full[:, states_n:].reshape(seq_count, length, states_n)
    scanned = ssd_scan(mixed_x * steps_dt[..., None], b_rows, c_rows, rates)
    outputs = scanned + skip_gain[:, None] * mixed_x
    return outputs.reshape(tokens, breadth) * jax.nn.silu(z_cols)


def rope_turn(values, positions, direction):
    half_dim = values.shape[-1] // 2
    freqs = ROPE_BASE ** (-jnp.arange(half_dim, dtype=jnp.float32) / half_dim)
    angles = positions.astype(jnp.float32)[:, None] * freqs
    cosine = jnp.cos(angles)[:, None, :]
    sine = direction * jnp.sin(angles)[:, None, :]
    first = values[..., :half_dim]
    second = values[..., half_dim:]
    return jnp.concatenate(
        [first * cosine - second * sine, second * cosine + first * sine], axis=-1
    )


def dot_plain(left, right):
    return jnp.dot(left, right, preferred_element_type=jnp.float32)


def dot_right_t(left, right):
    return lax.dot_general(
        left, right, (((1,), (1,)), ((), ())), preferred_element_type=jnp.float32
    )


def dot_left_t(left, right):
    return lax.dot_general(
        left, right, (((0,), (0,)), ((), ())), preferred_element_type=jnp.float32
    )


def split_columns(values, widths):
    pieces = []
    offset = 0
    for breadth in widths:
        pieces.append(values[..., offset : offset + breadth])
        offset = offset + breadth
    return pieces


def col_total(values):
    return lax.psum(values, "col")


def grid_total(values):
    return lax.psum(values, ("row", "col"))


def row_gather(values):
    return lax.all_gather(values, "row", axis=0, tiled=True)


def col_gather(values):
    return lax.all_gather(values, "col", axis=1, tiled=True)


def col_scatter(values):
    return lax.psum_scatter(values, "col", scatter_dimension=1, tiled=True)


def to_tokens(values):
    return lax.all_to_all(values, ("row", "col"), split_axis=0, concat_axis=1, tiled=True)


def to_columns(values):
    return lax.all_to_all(values, ("row", "col"), split_axis=1, concat_axis=0, tiled=True)


def row_scatter(gathered, weight, transposed):

    def row_term():
        if transposed:
            return dot_right_t(gathered, weight)
        return dot_plain(gathered, weight)

    return lax.psum_scatter(row_term(), "row", scatter_dimension=0, tiled=True)


def project_in(gathered, joined):
    return col_scatter(dot_plain(gathered, joined))


def project_back(gathered, joined):
    return col_scatter(dot_right_t(gathered, joined))


def norm_scale(values, breadth, total_fn):
    return lax.rsqrt(total_fn(jnp.sum(values * values, axis=1)) / breadth + EPSILON)


def norm_back(grad_out, values, scales, gain, breadth, total_fn):
    normed = values * scales[:, None]
    gain_grad = jnp.sum(grad_out * normed, axis=0)
    grad_normed = grad_out * gain
    inner_sum = total_fn(jnp.sum(grad_normed * values, axis=1))
    grad_values = (
        scales[:, None] * grad_normed - values * (scales**3 * inner_sum / breadth)[:, None]
    )
    return (grad_values, gain_grad)


def head_rows(values, kv_heads):
    tok_count, q_heads, head_dim = values.shape
    shaped = values.reshape(tok_count, kv_heads, q_heads // kv_heads, head_dim)
    return shaped.transpose(1, 2, 0, 3).reshape(kv_heads, -1, head_dim)


def head_tokens(values, tok_count):
    kv_heads, row_total, head_dim = values.shape
    shaped = values.reshape(kv_heads, row_total // tok_count, tok_count, head_dim)
    return shaped.transpose(2, 0, 1, 3).reshape(tok_count, -1, head_dim)


def masked_scores(q_rows, keys, key_mask):
    scores = jnp.einsum("hra,kha->hrk", q_rows, keys, preferred_element_type=jnp.float32)
    scores = scores * q_rows.shape[-1] ** (-0.5)
    return jnp.where(key_mask[None], scores, NEGATIVE)


def on_device(
    block_input,
    mixer_gain,
    ssm_gate_weight,
    ssm_input_weight,
    ssm_bc_weight,
    ssm_step_weight,
    query_weight,
    keyval_weight,
    conv_input,
    conv_states,
    step_bias,
    decay_log,
    skip_gain,
    ssm_norm_gain,
    ssm_out_weight,
    attn_out_weight,
    ffn_gain,
    gate_up_weight,
    down_weight,
    cotangent,
):
    col_count = lax.axis_size("col")
    grid_count = lax.axis_size("row") * col_count
    my_group = lax.axis_index("row") * col_count + lax.axis_index("col")
    feat_cols = block_input.shape[1]
    residual = block_input.astype(jnp.float32)
    scale_mix = norm_scale(residual, D, col_total)
    normed_mix = (residual * scale_mix[:, None] * mixer_gain).astype(jnp.bfloat16)
    rows_mix = row_gather(normed_mix)
    tokens = rows_mix.shape[0]
    seq_count = tokens // LEN
    in_weights = (
        ssm_gate_weight,
        ssm_input_weight,
        ssm_bc_weight,
        ssm_step_weight,
        query_weight,
        keyval_weight,
    )
    widths = [weight_arg.shape[1] // col_count for weight_arg in in_weights]
    joined_in = jnp.concatenate(
        [weight_arg.reshape(feat_cols, col_count, -1) for weight_arg in in_weights], axis=2
    ).reshape(feat_cols, -1)
    projected = project_in(rows_mix, joined_in)
    z_cols, x_raw, bc_raw, step_raw, q_raw, kv_raw = split_columns(projected, widths)
    bc_post, bc_pull = jax.vjp(
        lambda raw_cols, kernel_w: conv_piece(raw_cols, kernel_w, seq_count), bc_raw, conv_states
    )
    bc_whole, kv_whole = (
        lax.all_gather(bc_post.astype(jnp.bfloat16), ("row", "col"), axis=1, tiled=True),
        lax.all_gather(kv_raw.astype(jnp.bfloat16), ("row", "col"), axis=1, tiled=True),
    )
    gated, mamba_pull = jax.vjp(
        partial(mamba_core, seq_count),
        x_raw,
        z_cols,
        step_raw,
        bc_whole.astype(jnp.float32),
        conv_input,
        step_bias,
        decay_log,
        skip_gain,
    )
    ssm_width = HEADS * HDIM
    scale_ssm = norm_scale(gated, ssm_width, grid_total)
    ssm_out = (gated * scale_ssm[:, None] * ssm_norm_gain).astype(jnp.bfloat16)
    tok_share = tokens // grid_count
    q_tokens = to_tokens(q_raw.astype(jnp.bfloat16))
    q_pos = my_group * tok_share + jnp.arange(tok_share, dtype=jnp.int32)
    k_pos = jnp.arange(tokens, dtype=jnp.int32)
    q_rot = rope_turn(
        q_tokens.astype(jnp.float32).reshape(tok_share, QHEADS, ADIM), q_pos % LEN, 1.0
    ).astype(jnp.bfloat16)
    key_width = kv_whole.shape[1] // 2
    k_rot = rope_turn(
        kv_whole[:, :key_width].astype(jnp.float32).reshape(tokens, KVHEADS, ADIM), k_pos % LEN, 1.0
    ).astype(jnp.bfloat16)
    v_whole = kv_whole[:, key_width:].reshape(tokens, KVHEADS, ADIM)
    q_rows = head_rows(q_rot, KVHEADS)
    row_pos = jnp.tile(q_pos, QHEADS // KVHEADS)
    key_mask = (row_pos[:, None] // LEN == k_pos[None, :] // LEN) & (
        k_pos[None, :] <= row_pos[:, None]
    )
    scores = masked_scores(q_rows, k_rot, key_mask)
    row_top = jnp.max(scores, axis=2, keepdims=True)
    log_total = row_top + jnp.log(jnp.sum(jnp.exp(scores - row_top), axis=2, keepdims=True))
    probs_low = jnp.exp(scores - log_total).astype(jnp.bfloat16)
    attn_rows = jnp.einsum("hrk,kha->hra", probs_low, v_whole, preferred_element_type=jnp.float32)
    attn_cols = to_columns(
        head_tokens(attn_rows, tok_share).reshape(tok_share, -1).astype(jnp.bfloat16)
    )
    mixer_cat = jnp.concatenate([ssm_out, attn_cols], axis=1)
    mixer_all = col_gather(mixer_cat)
    joined_out = jnp.concatenate(
        [
            ssm_out_weight.reshape(col_count, -1, feat_cols),
            attn_out_weight.reshape(col_count, -1, feat_cols),
        ],
        axis=1,
    ).reshape(-1, feat_cols)
    mixed = row_scatter(mixer_all, joined_out, False)
    after_mix = residual + mixed
    scale_ffn = norm_scale(after_mix, D, col_total)
    normed_ffn = (after_mix * scale_ffn[:, None] * ffn_gain).astype(jnp.bfloat16)
    rows_ffn = row_gather(normed_ffn)
    ff_share = gate_up_weight.shape[2] // col_count
    joined_gu = (
        gate_up_weight.reshape(feat_cols, 2, col_count, ff_share)
        .transpose(0, 2, 1, 3)
        .reshape(feat_cols, -1)
    )
    gate_up = project_in(rows_ffn, joined_gu)
    gate_val = gate_up[:, :ff_share]
    up_val = gate_up[:, ff_share:]
    sig_gate = jax.nn.sigmoid(gate_val)
    hidden = (gate_val * sig_gate * up_val).astype(jnp.bfloat16)
    hidden_all = col_gather(hidden)
    ffn_out = row_scatter(hidden_all, down_weight, False)
    output = (after_mix + ffn_out).astype(jnp.bfloat16)
    rows_dout = row_gather(cotangent.astype(jnp.bfloat16))
    grad_hidden = project_back(rows_dout, down_weight)
    grad_down = dot_left_t(hidden_all, rows_dout)
    grad_gate = grad_hidden * up_val * sig_gate * (1.0 + gate_val * (1.0 - sig_gate))
    grad_up = grad_hidden * gate_val * sig_gate
    gu_all = col_gather(jnp.concatenate([grad_gate, grad_up], axis=1).astype(jnp.bfloat16))
    grad_nffn = row_scatter(gu_all, joined_gu, True)
    grad_joined_gu = dot_left_t(rows_ffn, gu_all)
    grad_gate_up = (
        grad_joined_gu.reshape(feat_cols, col_count, 2, ff_share)
        .transpose(0, 2, 1, 3)
        .reshape(feat_cols, 2, -1)
    )
    grad_mid, grad_ffn_gain = norm_back(grad_nffn, after_mix, scale_ffn, ffn_gain, D, col_total)
    grad_mid = cotangent + grad_mid
    rows_dmix = row_gather(grad_mid.astype(jnp.bfloat16))
    grad_cat = project_back(rows_dmix, joined_out)
    grad_joined_out = dot_left_t(mixer_all, rows_dmix).reshape(col_count, -1, feat_cols)
    ssm_share = ssm_out.shape[1]
    grad_ssm_w = grad_joined_out[:, :ssm_share].reshape(-1, feat_cols)
    grad_attn_w = grad_joined_out[:, ssm_share:].reshape(-1, feat_cols)
    grad_ssm_out = grad_cat[:, :ssm_share]
    grad_attn_tok = to_tokens(grad_cat[:, ssm_share:].astype(jnp.bfloat16))
    grad_rows = head_rows(grad_attn_tok.reshape(tok_share, QHEADS, ADIM), KVHEADS)
    scores_again = masked_scores(q_rows, k_rot, key_mask)
    probs = jnp.exp(scores_again - log_total)
    probs_again = probs.astype(jnp.bfloat16)
    grad_v = jnp.einsum("hrk,hra->kha", probs_again, grad_rows, preferred_element_type=jnp.float32)
    grad_p = jnp.einsum("hra,kha->hrk", grad_rows, v_whole, preferred_element_type=jnp.float32)
    grad_s = probs * (grad_p - jnp.sum(grad_p * probs, axis=2, keepdims=True)) * ADIM ** (-0.5)
    grad_q_rows = jnp.einsum("hrk,kha->hra", grad_s, k_rot.astype(jnp.float32), precision=HIGHEST)
    grad_k = jnp.einsum("hrk,hra->kha", grad_s, q_rows.astype(jnp.float32), precision=HIGHEST)
    grad_q = rope_turn(head_tokens(grad_q_rows, tok_share), q_pos % LEN, -1.0).reshape(
        tok_share, -1
    )
    grad_q_cols = to_columns(grad_q.astype(jnp.bfloat16))
    grad_k_raw = rope_turn(grad_k, k_pos % LEN, -1.0).reshape(tokens, -1)
    grad_kv_part = jnp.concatenate([grad_k_raw, grad_v.reshape(tokens, -1)], axis=1)
    grad_gated, grad_ssm_gain = norm_back(
        grad_ssm_out, gated, scale_ssm, ssm_norm_gain, ssm_width, grid_total
    )
    (
        grad_x_raw,
        grad_z,
        grad_step,
        grad_bc_whole,
        grad_conv_in,
        grad_step_bias,
        grad_decay,
        grad_skip,
    ) = mamba_pull(grad_gated)
    grad_bc_own, grad_kv_own = (
        lax.psum_scatter(grad_bc_whole, ("row", "col"), scatter_dimension=1, tiled=True),
        lax.psum_scatter(grad_kv_part, ("row", "col"), scatter_dimension=1, tiled=True),
    )
    grad_bc_raw, grad_conv_bc = bc_pull(grad_bc_own)
    grad_in_cat = jnp.concatenate(
        [
            grad_z.astype(jnp.bfloat16),
            grad_x_raw.astype(jnp.bfloat16),
            grad_bc_raw.astype(jnp.bfloat16),
            grad_step.astype(jnp.bfloat16),
            grad_q_cols,
            grad_kv_own.astype(jnp.bfloat16),
        ],
        axis=1,
    )
    in_all = col_gather(grad_in_cat)
    grad_nmix = row_scatter(in_all, joined_in, True)
    grad_joined_in = dot_left_t(rows_mix, in_all).reshape(feat_cols, col_count, -1)
    in_grads = [segment.reshape(feat_cols, -1) for segment in split_columns(grad_joined_in, widths)]
    grad_res, grad_mixer_gain = norm_back(grad_nmix, residual, scale_mix, mixer_gain, D, col_total)
    grad_input = grad_mid + grad_res
    summed = lax.psum(
        (
            in_grads[0],
            in_grads[1],
            in_grads[2],
            in_grads[3],
            in_grads[4],
            in_grads[5],
            grad_conv_in,
            grad_conv_bc,
            grad_step_bias,
            grad_decay,
            grad_skip,
            grad_ssm_gain,
            grad_ssm_w,
            grad_attn_w,
            grad_gate_up,
            grad_down,
        ),
        "dp",
    )
    gains = lax.psum((grad_mixer_gain, grad_ffn_gain), ("dp", "row"))
    return (
        output,
        grad_input,
        gains[0],
        summed[0],
        summed[1],
        summed[2],
        summed[3],
        summed[4],
        summed[5],
        summed[6],
        summed[7],
        summed[8],
        summed[9],
        summed[10],
        summed[11],
        summed[12],
        summed[13],
        gains[1],
        summed[14],
        summed[15],
    )


def solution(mesh):
    placed = (
        P(("dp", "row"), "col"),
        P("col"),
        P("col", "row"),
        P("col", "row"),
        P("col", "row"),
        P("col", "row"),
        P("col", "row"),
        P("col", "row"),
        P(None, ("row", "col")),
        P(None, ("row", "col")),
        P(("row", "col")),
        P(("row", "col")),
        P(("row", "col")),
        P(("row", "col")),
        P("row", "col"),
        P("row", "col"),
        P("col"),
        P("col", None, "row"),
        P("row", "col"),
        P(("dp", "row"), "col"),
    )
    return jax.shard_map(
        on_device,
        mesh=mesh,
        in_specs=placed,
        out_specs=(
            P(("dp", "row"), "col"),
            P(("dp", "row"), "col"),
            P("col"),
            P("col", "row"),
            P("col", "row"),
            P("col", "row"),
            P("col", "row"),
            P("col", "row"),
            P("col", "row"),
            P(None, ("row", "col")),
            P(None, ("row", "col")),
            P(("row", "col")),
            P(("row", "col")),
            P(("row", "col")),
            P(("row", "col")),
            P("row", "col"),
            P("row", "col"),
            P("col"),
            P("col", None, "row"),
            P("row", "col"),
        ),
        check_vma=False,
    )
```

profile of v0, /device:TPU:0, one launch (start us, length us, event | category | flops | bytes accessed | tf_op | source)
XLA Modules:
  0.0 1626.0 jit_solution(6823961549924899481)
XLA Ops:
  25.1 9.7 concatenate.39
  36.8 11.5 all-gather.13.cloned.1.call-done
  60.7 148.8 %all-reduce.28.cloned.1.call-done = f32[1024,2060]{0,1:T(8,128)} async-done(((f32[1024,2060]{0,1:T(8,128)}), f32[1024,2060]{0,1:T(8,128)}) %all-reduce.28.cloned.1.call-update) | async-done | bytes 8437776
  256.6 51.1 %while.42 = (s32[]{:T(128)}, f32[1,3,64,256]{3,2,1,0:T(8,128)S(1)}, f32[4,1,256,3,64]{2,0,4,3,1:T(4,128)}, f32[4,1,3,64,256]{4,3,2,1,0:T(8,128)}, f32[4,1,256,3]...) while((s32[]{:T(128)}, f32[1,3,64,256]{3,2,1,0:T(8,128)S(1)}, ...), condition=%wide.region_6.7_spmd.clone.clone, body=%wide.region_3.6_spmd.clone.clone.sunk | while | flops 655590144 | bytes 4463589 | solution.py:74
  316.5 31.8 %psum.169 = f32[1024]{0:T(1024)S(1)} all-reduce(f32[1024]{0:T(1024)S(1)} %get-tuple-element.927), channel_id=1, replica_groups=mesh['dp'=2,'row'=4,'col'=4] {'row','col'}, use_global_device_ids=true, to_apply=%region_8.9 | all-reduce | flops 1024 | bytes 8192 | tf_op jit(solution)/shard_map/psum | solution.py:143
  377.7 18.3 %all-gather.17.cloned.1.call-done = bf16[1024,1024]{1,0:T(8,128)(2,1)} async-done(((bf16[1024,256]{1,0:T(8,128)(2,1)}), bf16[1024,1024]{1,0:T(8,128)(2,1)}) %all-gather.17.cloned.1.call-update) | async-done | bytes 2097168 | tf_op jit(solution)/shard_map/all_gather | solution.py:151
  402.3 42.1 %reduce-scatter.14.cloned.1.call-done = f32[256,512]{1,0:T(8,128)} async-done(((f32[1024,512]{1,0:T(8,128)}), f32[256,512]{1,0:T(8,128)}) %reduce-scatter.14.cloned.1.call-update) | async-done | bytes 524304 | tf_op jit(solution)/shard_map/reduce_scatter | solution.py:173
  455.1 18.9 %all-gather.23.cloned.1.call-done = bf16[1024,512]{1,0:T(8,128)(2,1)} async-done(((bf16[256,512]{1,0:T(8,128)(2,1)}), bf16[1024,512]{1,0:T(8,128)(2,1)}) %all-gather.23.cloned.1.call-update) | async-done | bytes 1048592 | tf_op jit(solution)/shard_map/all_gather | solution.py:147
  487.8 15.8 all-gather.19.cloned.1.call-done
  511.3 39.6 %reduce-scatter.20.cloned.1.call-done = f32[1024,256]{1,0:T(8,128)} async-done(((f32[1024,1024]{1,0:T(8,128)}), f32[1024,256]{1,0:T(8,128)}) %reduce-scatter.20.cloned.1.call-update) | async-done | bytes 1048592 | tf_op jit(solution)/shard_map/reduce_scatter | solution.py:155
  550.9 74.2 %reduce-scatter.16.cloned.1.call-done = f32[1024,512]{1,0:T(8,128)} async-done(((f32[1024,2048]{1,0:T(8,128)}), f32[1024,512]{1,0:T(8,128)}) %reduce-scatter.16.cloned.1.call-update) | async-done | bytes 2097168 | tf_op jit(solution)/shard_map/reduce_scatter | solution.py:155
  630.1 34.0 %all-gather.25.cloned.1.call-done = bf16[1024,2048]{1,0:T(8,128)(2,1)} async-done(((bf16[1024,512]{1,0:T(8,128)(2,1)}), bf16[1024,2048]{1,0:T(8,128)(2,1)}) %all-gather.25.cloned.1.call-update) | async-done | bytes 4194320 | tf_op jit(solution)/shard_map/all_gather | solution.py:151
  670.7 18.4 %all-gather.21.cloned.1.call-done = bf16[1024,1024]{1,0:T(8,128)(2,1)} async-done(((bf16[1024,256]{1,0:T(8,128)(2,1)}), bf16[1024,1024]{1,0:T(8,128)(2,1)}) %all-gather.21.cloned.1.call-update) | async-done | bytes 2097168 | tf_op jit(solution)/shard_map/all_gather | solution.py:151
  693.2 42.6 %reduce-scatter.22.cloned.1.call-done = f32[256,512]{1,0:T(8,128)} async-done(((f32[1024,512]{1,0:T(8,128)}), f32[256,512]{1,0:T(8,128)}) %reduce-scatter.22.cloned.1.call-update) | async-done | bytes 524304 | tf_op jit(solution)/shard_map/reduce_scatter | solution.py:173
  744.1 37.8 %reduce-scatter.18.cloned.1.call-done = f32[256,512]{1,0:T(8,128)} async-done(((f32[1024,512]{1,0:T(8,128)}), f32[256,512]{1,0:T(8,128)}) %reduce-scatter.18.cloned.1.call-update) | async-done | bytes 524304 | tf_op jit(solution)/shard_map/reduce_scatter | solution.py:173
  784.2 27.4 %all-gather.27.cloned.1.call-done = bf16[1024,512]{1,0:T(8,128)(2,1)} async-done(((bf16[256,512]{1,0:T(8,128)(2,1)}), bf16[1024,512]{1,0:T(8,128)(2,1)}) %all-gather.27.cloned.1.call-update) | async-done | bytes 1048592 | tf_op jit(solution)/shard_map/all_gather | solution.py:147
  816.5 44.1 %reduce-scatter.24.cloned.1.call-done = f32[1024,256]{1,0:T(8,128)} async-done(((f32[1024,1024]{1,0:T(8,128)}), f32[1024,256]{1,0:T(8,128)}) %reduce-scatter.24.cloned.1.call-update) | async-done | bytes 1048592 | tf_op jit(solution)/shard_map/reduce_scatter | solution.py:155
  863.2 32.4 %psum.172 = f32[1024]{0:T(1024)S(1)} all-reduce(f32[1024]{0:T(1024)S(1)} %get-tuple-element.840), channel_id=1, replica_groups=mesh['dp'=2,'row'=4,'col'=4] {'row','col'}, use_global_device_ids=true, to_apply=%region_22.23 | all-reduce | flops 1024 | bytes 8192 | tf_op jit(solution)/shard_map/psum | solution.py:143
  906.2 173.9 %while.41 = (s32[]{:T(128)}, f32[1,3,64,256]{3,2,1,0:T(8,128)}, f32[4,1,256,3,64]{2,0,4,3,1:T(4,128)}, f32[4,1,256,256]{3,2,0,1:T(8,128)}, f32[4,1,256,256]{3,2,...) while((s32[]{:T(128)}, f32[1,3,64,256]{3,2,1,0:T(8,128)}, ...), condition=%wide.region_35.36_spmd.clone, body=%wide.region_23.35_spmd.clone.sunk | while | flops 1664915456 | bytes 16544779 | solution.py:74
  1087.6 10.9 all_to_all.61
  1147.2 63.3 %reduce-scatter.30.cloned.1.call-done = f32[32,1024]{1,0:T(8,128)} async-done(((f32[512,1024]{1,0:T(8,128)}), f32[32,1024]{1,0:T(8,128)}) %reduce-scatter.30.cloned.1.call-update) | async-done | bytes 131088
  1214.1 33.9 %all-gather.31.cloned.1.call-done = bf16[4,515,1024]{2,1,0:T(8,128)(2,1)} async-done(((bf16[1,515,1024]{2,1,0:T(8,128)(2,1)}), bf16[4,515,1024]{2,1,0:T(8,128)(2,1)}) %all-gather.31.cloned.1.call-update) | async-done | bytes 4218896 | tf_op jit(solution)/shard_map/all_gather | solution.py:151
  1314.7 21.5 %all-reduce.22 = (f32[512]{0:T(512)}, f32[512]{0:T(512)}) all-reduce(f32[512]{0:T(512)S(1)} %get-tuple-element.850, f32[512]{0:T(512)S(1)} %copy-done.85), channel_id=1, replica_groups=mesh['dp'=2,'row'=4,'col'=4] {'dp','row'}, use_global_device_ids=true, to_apply=%region_44.45 | all-reduce | flops 1024 | bytes 8192 | tf_op jit(solution)/shard_map/psum | solution.py:431
  1338.1 264.0 %all-reduce.30.cloned.1.call-done = (f32[512,768]{0,1:T(8,128)}, f32[512,768]{0,1:T(8,128)}, f32[512,128]{0,1:T(8,128)}, f32[512,256]{0,1:T(8,128)}, f32[512,128...) async-done(((f32[512,768]{0,1:T(8,128)}, f32[512,768]{0,1:T(8,128)}, f32[512,128]{0,1:T(8,128)}, ...) | async-done | bytes 12582928 | tf_op jit(solution)/shard_map/psum | solution.py:410
  (784 shorter events, 567.6 us)
Async XLA Ops:
  7.2 41.0 %all-gather.13.cloned.1.call-start = ((), (), s32[]{:S(2)}) async-start(), calls=%async_computation.13 | async-start | bytes 1310720 | tf_op jit(solution)/shard_map/all_gather | solution.py:147
  19.8 189.7 %all-reduce.28.cloned.1.call-start = ((), (), s32[]{:S(2)}) async-start(), calls=%async_computation.32 | async-start | bytes 16908288
  55.9 195.2 %all-gather.29.cloned.1.call-start = ((), (), s32[]{:S(2)}) async-start(), calls=%async_computation.28 | async-start | bytes 1114112 | tf_op jit(solution)/shard_map/all_gather | solution.py:267
  229.7 14.1 all-to-all-start
  234.5 113.8 %all-gather.15.cloned.1.call-start = ((), (), s32[]{:S(2)}) async-start(), calls=%async_computation.14 | async-start | bytes 1114112 | tf_op jit(solution)/shard_map/all_gather | solution.py:268
  361.7 11.4 all-to-all-start.1
  365.2 30.8 %all-gather.17.cloned.1.call-start = ((), (), s32[]{:S(2)}) async-start(), calls=%async_computation.15 | async-start | bytes 2621440 | tf_op jit(solution)/shard_map/all_gather | solution.py:151
  375.3 69.1 %reduce-scatter.14.cloned.1.call-start = ((), (), s32[]{:S(2)}) async-start(), calls=%async_computation.16 | async-start | bytes 2621440 | tf_op jit(solution)/shard_map/reduce_scatter | solution.py:173
  400.4 73.5 %all-gather.23.cloned.1.call-start = ((), (), s32[]{:S(2)}) async-start(), calls=%async_computation.21 | async-start | bytes 1310720 | tf_op jit(solution)/shard_map/all_gather | solution.py:147
  402.3 101.3 %all-gather.19.cloned.1.call-start = ((), (), s32[]{:S(2)}) async-start(), calls=%async_computation.17 | async-start | bytes 1310720 | tf_op jit(solution)/shard_map/all_gather | solution.py:147
  455.0 95.9 %reduce-scatter.20.cloned.1.call-start = ((), (), s32[]{:S(2)}) async-start(), calls=%async_computation.22 | async-start | bytes 5242880 | tf_op jit(solution)/shard_map/reduce_scatter | solution.py:155
  478.5 146.6 %reduce-scatter.16.cloned.1.call-start = ((), (), s32[]{:S(2)}) async-start(), calls=%async_computation.18 | async-start | bytes 10485760 | tf_op jit(solution)/shard_map/reduce_scatter | solution.py:155
  511.2 152.8 %all-gather.25.cloned.1.call-start = ((), (), s32[]{:S(2)}) async-start(), calls=%async_computation.23 | async-start | bytes 5242880 | tf_op jit(solution)/shard_map/all_gather | solution.py:151
  629.4 59.6 %all-gather.21.cloned.1.call-start = ((), (), s32[]{:S(2)}) async-start(), calls=%async_computation.19 | async-start | bytes 2621440 | tf_op jit(solution)/shard_map/all_gather | solution.py:151
  630.0 105.9 %reduce-scatter.22.cloned.1.call-start = ((), (), s32[]{:S(2)}) async-start(), calls=%async_computation.24 | async-start | bytes 2621440 | tf_op jit(solution)/shard_map/reduce_scatter | solution.py:173
  670.6 111.2 %reduce-scatter.18.cloned.1.call-start = ((), (), s32[]{:S(2)}) async-start(), calls=%async_computation.20 | async-start | bytes 2621440 | tf_op jit(solution)/shard_map/reduce_scatter | solution.py:173
  693.2 118.4 %all-gather.27.cloned.1.call-start = ((), (), s32[]{:S(2)}) async-start(), calls=%async_computation.25 | async-start | bytes 1310720 | tf_op jit(solution)/shard_map/all_gather | solution.py:147
  784.2 76.4 %reduce-scatter.24.cloned.1.call-start = ((), (), s32[]{:S(2)}) async-start(), calls=%async_computation.26 | async-start | bytes 5242880 | tf_op jit(solution)/shard_map/reduce_scatter | solution.py:155
  816.5 328.6 %reduce-scatter.28.cloned.1.call-start = ((), (), s32[]{:S(2)}) async-start(), calls=%async_computation.30 | async-start | bytes 2228224
  1086.1 124.3 %reduce-scatter.30.cloned.1.call-start = ((), (), s32[]{:S(2)}) async-start(), calls=%async_computation.31 | async-start | bytes 2228224
  1129.3 12.8 all-to-all-start.3
  1132.8 115.3 %all-gather.31.cloned.1.call-start = ((), (), s32[]{:S(2)}) async-start(), calls=%async_computation.29 | async-start | bytes 5324800 | tf_op jit(solution)/shard_map/all_gather | solution.py:151
  1214.1 93.4 %reduce-scatter.26.cloned.1.call-start = ((), (), s32[]{:S(2)}) async-start(), calls=%async_computation.27 | async-start | bytes 2621440 | tf_op jit(solution)/shard_map/reduce_scatter | solution.py:173
  1259.6 342.6 %all-reduce.30.cloned.1.call-start = ((), (), s32[]{:S(2)}) async-start(), calls=%async_computation.33 | async-start | bytes 25165824 | tf_op jit(solution)/shard_map/psum | solution.py:410
  (127 other events, 3882.9 us)
Sparse Core Ops, SparseCore 0:
  19.9 28.2 all-gather.12
  56.1 153.4 all-reduce.27
  212.7 38.3 all-gather.28
  253.7 37.0 all-gather.14
  375.5 20.4 all-gather.16
  400.5 43.8 reduce-scatter.13
  446.7 27.2 all-gather.22
  476.2 27.3 all-gather.18
  506.9 44.0 reduce-scatter.19
  553.4 71.7 reduce-scatter.15
  629.5 34.4 all-gather.24
  666.1 22.8 all-gather.20
  692.0 43.8 reduce-scatter.21
  738.6 43.1 reduce-scatter.17
  784.3 27.2 all-gather.26
  816.6 44.0 reduce-scatter.23
  1086.2 58.7 reduce-scatter.27
  1149.1 61.2 reduce-scatter.29
  1214.2 33.8 all-gather.30
  1259.7 43.8 reduce-scatter.25
  1308.9 293.2 all-reduce.29
where the time goes:
time: 1640 us; the launch traced here: 1630 us
  waiting for transfers between devices  960 us (59%)
  local copies, waits for them, and re-layouts  251 us (15%)
  matrix products  138 us (8%)
  blocking collectives  133 us (8%)
  other arithmetic  114 us (7%)
  between operations  16.6 us (1%)
    psum x1, waiting for transfers between devices, on_device(): lax.psum((in_grads[0], in_grads[1], in_grads[2], in_grads[3], in_grads[4]...  264 us
    unnamed x24, waiting for transfers between devices  216 us
    reduce_scatter x3, waiting for transfers between devices, col_scatter(): return lax.psum_scatter(values, 'col', scatter_dimension=1, tiled=True)  158 us
    reduce_scatter x4, waiting for transfers between devices, row_scatter(): return lax.psum_scatter(row_term(), 'row', scatter_dimension=0, tiled=True)  123 us
    all_gather x4, waiting for transfers between devices, col_gather(): return lax.all_gather(values, 'col', axis=1, tiled=True)  105 us
    all_gather x4, waiting for transfers between devices, row_gather(): return lax.all_gather(values, 'row', axis=0, tiled=True)  73.5 us
    unnamed x254, local copies, waits for them, and re-layouts  66.4 us
    psum x2, blocking collectives, grid_total(): return lax.psum(values, ('row', 'col'))  64.2 us
  transfers between devices with their start and end apart: 24, of which 22 were waited for; matrix products, arithmetic and copies ran while one was open for 14% of the time, Pallas kernels for 0%

commit v1 on v0

v1 whole, which is shorter than its diff:
```python
import types

import jax
import jax.numpy as jnp
import numpy as np
from jax import lax
from jax.experimental import pallas as pl
from jax.experimental.pallas import tpu as pltpu
from jax.sharding import PartitionSpec as P

D = 2048
HEADS = 48
HDIM = 64
STATE = 256
ADIM = 128
LEN = 1024
SPAN = 256
SIDE = 4
BLK = LEN // SIDE
HALO = 16
HH = 3
HW = HH * HDIM
EPSILON = 1e-05
ROPE_BASE = 100000000000.0
HIGHEST = lax.Precision.HIGHEST
NEGATIVE = -1e30
BF = jnp.bfloat16
F32 = jnp.float32
MESH = pl.DeviceIdType.MESH
SCALE = ADIM ** (-0.5)


def dot_nn(a, b, precision=None):
    return lax.dot_general(a, b, (((1,), (0,)), ((), ())), precision=precision, preferred_element_type=F32)


def dot_nt(a, b, precision=None):
    return lax.dot_general(a, b, (((1,), (1,)), ((), ())), precision=precision, preferred_element_type=F32)


def dot_tn(a, b, precision=None):
    return lax.dot_general(a, b, (((0,), (0,)), ((), ())), precision=precision, preferred_element_type=F32)


def sigmoid(v):
    return 1.0 / (1.0 + jnp.exp(-v))


def softplus(v):
    return jnp.maximum(v, 0.0) + jnp.log1p(jnp.exp(-jnp.abs(v)))


def iota(shape, axis):
    return lax.broadcasted_iota(jnp.int32, shape, axis)


def flip(v, d):
    v0, v1 = lax.rem(v, 2), lax.div(v, 2)
    if isinstance(d, int):
        d0, d1 = d % 2, d // 2
    else:
        d0, d1 = lax.rem(d, 2), lax.div(d, 2)
    return 2 * (v1 + d1 - 2 * v1 * d1) + (v0 + d0 - 2 * v0 * d0)


def here():
    return lax.axis_index("row"), lax.axis_index("col")


def greet(r, c, rows=False, cols=(), grid=False, dp=False):
    sem = pltpu.get_barrier_semaphore()
    peers = []
    if grid:
        for d in range(SIDE):
            for e in range(SIDE):
                if d or e:
                    peers.append({"row": flip(r, d), "col": flip(c, e)})
    else:
        if rows:
            peers += [{"row": flip(r, d)} for d in (1, 2, 3)]
        peers += [{"col": flip(c, e)} for e in cols]
    if dp:
        peers.append({"dp": 1 - lax.axis_index("dp")})
    for peer in peers:
        pl.semaphore_signal(sem, inc=1, device_id=peer, device_id_type=MESH)
    pl.semaphore_wait(sem, len(peers))


def hop(src, dst, ssem, rsem, **where):
    return pltpu.make_async_remote_copy(
        src_ref=src, dst_ref=dst, send_sem=ssem, recv_sem=rsem, device_id=where, device_id_type=MESH
    )


def rows_at(ref, block, pad=0):
    return ref.at[pl.ds(pl.multiple_of(block * BLK + pad, 16), BLK)]


def dma(*shape):
    return pltpu.SemaphoreType.DMA(shape)


def launch(body, ins, outs, scratch, cid, smem=None):
    smem = smem or {}
    shapes = []
    for item in scratch.values():
        shapes += list(item.values()) if isinstance(item, dict) else [item]

    def kernel(*refs):
        refs = list(refs)
        found = {}
        for key in (*ins, *smem, *outs):
            found[key] = refs.pop(0)
        for key, item in scratch.items():
            if isinstance(item, dict):
                found[key] = types.SimpleNamespace(**{name: refs.pop(0) for name in item})
            else:
                found[key] = refs.pop(0)
        body(types.SimpleNamespace(**found))

    vector = pl.BlockSpec(memory_space=pltpu.VMEM)
    results = pl.pallas_call(
        kernel,
        out_shape=[jax.ShapeDtypeStruct(*o) for o in outs.values()],
        in_specs=[vector] * len(ins) + [pl.BlockSpec(memory_space=pltpu.SMEM)] * len(smem),
        out_specs=[vector] * len(outs),
        scratch_shapes=shapes,
        compiler_params=pltpu.CompilerParams(
            collective_id=cid, has_side_effects=True, vmem_limit_bytes=58 << 20
        ),
        name=body.__name__,
    )(*ins.values(), *smem.values())
    return types.SimpleNamespace(**dict(zip(outs, results)))


def rows_scratch(padded=False):
    size = LEN + 2 * HALO if padded else LEN
    return dict(g=pltpu.VMEM((size, D // SIDE), BF), zs=dma(3), zr=dma(3))


def gather_rows(S, r, pad=0):
    own = rows_at(S.g, r, pad)
    for d in (1, 2, 3):
        hop(own, own, S.zs.at[d - 1], S.zr.at[d - 1], row=flip(r, d)).start()


def wait_rows(S, r, d, pad=0):
    block = flip(r, d)
    part = rows_at(S.g, block, pad)
    hop(part, part, S.zs.at[d - 1], S.zr.at[d - 1], row=block).wait_recv()


def wait_rows_sent(S, r, pad=0):
    own = rows_at(S.g, r, pad)
    for d in (1, 2, 3):
        hop(own, own, S.zs.at[d - 1], S.zr.at[d - 1], row=flip(r, d)).wait_send()


def cols_scratch(w):
    return dict(
        cs=pltpu.VMEM((SIDE, 2, BLK, w), F32),
        cr=pltpu.VMEM((SIDE, 2, BLK, w), F32),
        xs=pltpu.VMEM((SIDE, BLK, w), BF),
        xr=pltpu.VMEM((SIDE, BLK, w), BF),
        acc=pltpu.VMEM((SIDE, BLK, w), F32),
        mine=pltpu.VMEM((SIDE, BLK, w), F32),
        ks=dma(SIDE),
        kr=dma(SIDE),
        ss=dma(SIDE),
        sr=dma(SIDE),
    )


def scatter_cols(S, G, r, c, product, pad=0, finish=None, apart=False):
    cs, cr, xs, xr, acc = (S.cs, S.cr, S.xs, S.xr, S.acc)

    def core_hop(d):
        return hop(cs.at[d], cr.at[d], S.ks.at[d], S.kr.at[d], col=flip(c, 1))

    def x_hop(d):
        return hop(xs.at[d], xr.at[d], S.ss.at[d], S.sr.at[d], col=flip(c, 2))

    def first(d):
        @pl.when(d > 0)
        def _():
            wait_rows(G, r, d, pad)

        rows = rows_at(G.g, flip(r, d), pad)[...]
        cs[d, 1] = product(rows, flip(c, 3))
        cs[d, 0] = product(rows, flip(c, 1))
        core_hop(d).start()
        S.mine[d] = product(rows, flip(c, 2))
        acc[d] = product(rows, c)

    def second(d):
        core_hop(d).wait_recv()
        xs[d] = (S.mine[d] + cr[d, 1]).astype(BF)
        x_hop(d).start()
        acc[d] = acc[d] + cr[d, 0]

    def both(d, carry):
        first(d)
        second(d)
        return carry

    def only(phase):
        def step(d, carry):
            phase(d)
            return carry

        return step

    if apart:
        lax.fori_loop(0, SIDE, only(first), 0)
        lax.fori_loop(0, SIDE, only(second), 0)
    else:
        lax.fori_loop(0, SIDE, both, 0)

    def end(d, carry):
        x_hop(d).wait_recv()
        finish(flip(r, d), acc[d] + xr[d].astype(F32))
        x_hop(d).wait_send()
        core_hop(d).wait_send()
        return carry

    def close():
        lax.fori_loop(0, SIDE, end, 0)

    return close


def tokens_scratch(*shape, low=F32):
    return dict(
        cs=pltpu.VMEM((2, *shape), low),
        cr=pltpu.VMEM((2, *shape), low),
        xs=pltpu.VMEM(shape, low),
        xr=pltpu.VMEM(shape, low),
        acc=pltpu.VMEM(shape, F32),
        ks=dma(),
        kr=dma(),
        ss=dma(),
        sr=dma(),
    )


def scatter_tokens(S, c, product):
    low = S.xs.dtype
    core = hop(S.cs, S.cr, S.ks, S.kr, col=flip(c, 1))
    over = hop(S.xs, S.xr, S.ss, S.sr, col=flip(c, 2))
    S.cs[1] = product(flip(c, 3)).astype(low)
    S.cs[0] = product(flip(c, 1)).astype(low)
    core.start()
    mine = product(flip(c, 2))
    S.acc[...] = product(c)
    core.wait_recv()
    S.xs[...] = (mine + S.cr[1].astype(F32)).astype(low)
    over.start()
    S.acc[...] = S.acc[...] + S.cr[0].astype(F32)

    def close():
        over.wait_recv()
        total = S.acc[...] + S.xr[...].astype(F32)
        over.wait_send()
        core.wait_send()
        return total

    return close


def trio_scratch():
    return dict(xs=dma(), xr=dma(), ks=dma(), kr=dma(), fs=dma(), fr=dma())


def trio(S, c, part):
    own, over = part(c), part(flip(c, 2))
    return (
        hop(own, own, S.xs, S.xr, col=flip(c, 2)),
        hop(own, own, S.ks, S.kr, col=flip(c, 1)),
        hop(over, over, S.fs, S.fr, col=flip(c, 1)),
    )


def trio_end(hops):
    over, core, forward = hops
    over.wait_recv()
    forward.start()
    core.wait_recv()
    forward.wait_recv()


def gcols_scratch(w):
    return dict(
        g=pltpu.VMEM((SIDE, LEN, w), BF),
        xs=dma(SIDE),
        xr=dma(SIDE),
        ks=dma(SIDE),
        kr=dma(SIDE),
        fs=dma(SIDE),
        fr=dma(SIDE),
    )


def col_part(S, j, t):
    return S.g.at[j, pl.ds(pl.multiple_of(t * BLK, BLK), BLK)]


def col_hop(S, c, kind, t, d):
    part = col_part(S, flip(c, 2) if kind == "f" else c, t)
    to = flip(c, 2) if kind == "x" else flip(c, 1)
    return hop(part, part, getattr(S, kind + "s").at[d], getattr(S, kind + "r").at[d], col=to)


def gather_cols(S, r, c, order=(3, 2, 1, 0)):
    for d in order:
        t = flip(r, d)
        col_hop(S, c, "x", t, d).start()
        col_hop(S, c, "k", t, d).start()


def wait_cols(S, r, c, d):
    t = flip(r, d)
    col_hop(S, c, "x", t, d).wait_recv()
    col_hop(S, c, "f", t, d).start()
    col_hop(S, c, "k", t, d).wait_recv()
    col_hop(S, c, "f", t, d).wait_recv()


def wait_cols_sent(S, r, c):
    def step(d, carry):
        t = flip(r, d)
        for kind in "xkf":
            col_hop(S, c, kind, t, d).wait_send()
        return carry

    lax.fori_loop(0, SIDE, step, 0)


def srows_scratch():
    w = D // SIDE
    return dict(
        ps=pltpu.VMEM((3, BLK, w), BF),
        pr=pltpu.VMEM((3, BLK, w), BF),
        pa=pltpu.VMEM((BLK, w), F32),
        rs=dma(3),
        rr=dma(3),
    )


def scatter_rows(S, r, product, ready):
    ps, pr, acc = S.ps, S.pr, S.pa

    def row_hop(d):
        return hop(ps.at[d - 1], pr.at[d - 1], S.rs.at[d - 1], S.rr.at[d - 1], row=flip(r, d))

    def step(i, carry):
        d = 3 - i
        ready(d)
        acc[...] = product(flip(r, d))

        @pl.when(d > 0)
        def _():
            ps[d - 1] = acc[...].astype(BF)
            row_hop(d).start()

        return carry

    lax.fori_loop(0, SIDE, step, 0)

    def close():
        total = acc[...]
        for d in (1, 2, 3):
            row_hop(d).wait_recv()
            total = total + pr[d - 1].astype(F32)
        for d in (1, 2, 3):
            row_hop(d).wait_send()
        return total

    return close


def row_sums(v):
    return dot_nt(jnp.ones((8, v.shape[1]), F32), v, HIGHEST)


def stat_scratch():
    return dict(st=pltpu.VMEM((SIDE, 8, BLK), F32), sts=dma(3), str=dma(3))


def col_sum(S, c, v):
    st = S.st
    st[c] = v
    hops = [
        hop(st.at[c], st.at[c], S.sts.at[e - 1], S.str.at[e - 1], col=flip(c, e)) for e in (1, 2, 3)
    ]
    for one in hops:
        one.start()
    for one in hops:
        one.wait_recv()
    total = (st[0] + st[1]) + (st[2] + st[3])
    for one in hops:
        one.wait_send()
    return total


def grid_scratch():
    return dict(st=pltpu.VMEM((SIDE, SIDE, 8, BLK), F32), sts=dma(16), str=dma(16))


def grid_sum(S, r, c):
    st = S.st
    hops = []
    for d in range(SIDE):
        for e in range(SIDE):
            if d or e:
                k = SIDE * d + e
                hops.append(
                    hop(
                        st.at[r, c],
                        st.at[r, c],
                        S.sts.at[k],
                        S.str.at[k],
                        row=flip(r, d),
                        col=flip(c, e),
                    )
                )
    for one in hops:
        one.start()

    def close():
        for one in hops:
            one.wait_recv()
        total = jnp.zeros((8, BLK), F32)
        for d in range(SIDE):
            for e in range(SIDE):
                total = total + st[d, e]
        for one in hops:
            one.wait_send()
        return total

    return close


def to_column(v):
    return jnp.transpose(v)[:, :1]


def pick_column(v, b):
    return jnp.sum(jnp.where(iota(v.shape, 1) == b, v, 0.0), axis=1, keepdims=True)


def cut(v, j, w):
    return v[:, j * w : (j + 1) * w]


def cut(v, j, w):
    return v[:, j * w : (j + 1) * w]


def project_kernel(x, gain, wz, wx, wbc, wq, wkv, ws, cw):
    def project(R):
        r, c = here()
        greet(r, c, rows=True, cols=(1, 2, 3))
        tap_hops = [
            hop(R.taps.at[c], R.taps.at[c], R.tss.at[e - 1], R.tsr.at[e - 1], col=flip(c, e)) for e in (1, 2, 3)
        ]
        R.taps[c] = jnp.zeros((8, 128), F32)
        R.taps[c, 0:4, 0:32] = R.cw[...]
        for one in tap_hops:
            one.start()
        x = R.x[...].astype(F32)
        total = col_sum(R.n, c, row_sums(x * x))
        scale = to_column(lax.rsqrt(total / D + EPSILON))
        g = R.p.g
        g[pl.ds(0, HALO)] = jnp.zeros((HALO, D // SIDE), BF)
        g[pl.ds(LEN + HALO, HALO)] = jnp.zeros((HALO, D // SIDE), BF)
        rows_at(g, r, HALO)[...] = (x * scale * R.gain[...]).astype(BF)
        gather_rows(R.p, r, HALO)
        wa, wb = R.wa, R.wb
        for j in range(SIDE):
            wa[j, :, 0:HW] = cut(R.wz, j, HW)
            wa[j, :, HW : 2 * HW] = cut(R.wx, j, HW)
        wb[:, 0:128] = R.wbc[...]
        wb[:, 128:384] = R.wq[...]
        wb[:, 384:512] = R.wkv[...]

        def finish(block, v):
            at = pl.ds(pl.multiple_of(block * BLK, BLK), BLK)
            R.z[at] = v[:, 0:HW]
            R.xr[at] = v[:, HW : 2 * HW]

        close_a = scatter_cols(R.a, R.p, r, c, lambda rows, j: dot_nn(rows, wa[j]), HALO, finish)
        steps = dot_nt(R.ws[...], g[pl.ds(HALO, LEN)])
        for j in range(SIDE):
            R.ps[j] = steps[16 * j : 16 * j + 8]
        step_hops = [
            hop(
                R.ps.at[flip(c, e)],
                R.pr.at[e - 1],
                R.pss.at[e - 1],
                R.psr.at[e - 1],
                col=flip(c, e),
            )
            for e in (1, 2, 3)
        ]
        for one in step_hops:
            one.start()

        def token_rows(j):
            return dot_nn(g[pl.ds(pl.multiple_of(j * BLK, BLK), BLK + 2 * HALO)], wb[...])

        close_b = scatter_tokens(R.b, c, token_rows)
        R.n1[...] = g[pl.ds(HALO, LEN)]
        R.s1[...] = total
        R.wa_o[...] = wa[...]
        R.wb_o[...] = wb[...]
        close_a()
        for one in step_hops:
            one.wait_recv()
        R.sr[...] = (R.ps[c] + R.pr[0]) + (R.pr[1] + R.pr[2])
        for one in step_hops:
            one.wait_send()
        R.br[...] = close_b()
        for one in tap_hops:
            one.wait_recv()
        R.wcs[...] = jnp.concatenate([R.taps[j, 0:4, 0:32] for j in range(SIDE)], axis=1)
        for one in tap_hops:
            one.wait_send()
        wait_rows_sent(R.p, r, HALO)

    n = BLK + 2 * HALO
    scratch = dict(
        p=rows_scratch(True),
        n=stat_scratch(),
        a=cols_scratch(2 * HW),
        b=tokens_scratch(n, 512),
        wa=pltpu.VMEM((SIDE, 512, 2 * HW), BF),
        wb=pltpu.VMEM((512, 512), BF),
        ps=pltpu.VMEM((SIDE, 8, LEN), F32),
        pr=pltpu.VMEM((3, 8, LEN), F32),
        pss=dma(3),
        psr=dma(3),
        taps=pltpu.VMEM((SIDE, 8, 128), F32),
        tss=dma(3),
        tsr=dma(3),
    )
    outs = dict(
        n1=((LEN, 512), BF),
        s1=((8, BLK), F32),
        z=((LEN, HW), F32),
        xr=((LEN, HW), F32),
        br=((n, 512), F32),
        sr=((8, LEN), F32),
        wa_o=((SIDE, 512, 2 * HW), BF),
        wb_o=((512, 512), BF),
        wcs=((4, 128), F32),
    )
    ins = dict(x=x, gain=gain, wz=wz, wx=wx, wbc=wbc, wq=wq, wkv=wkv, ws=ws, cw=cw)
    return launch(project, ins, outs, scratch, 1)


SMALL = 32


def forward_kernel(m, o, x, gain, wo, wt, wg, wu, dh):
    def forward(R):
        r, c = here()
        greet(r, c, rows=True, cols=(1, 2, 3))
        R.mc.g[c] = R.m[...]
        og = R.og
        og[c] = R.o[...]
        o_hops = trio(R.ot, c, lambda j: og.at[j])
        o_hops[0].start()
        o_hops[1].start()
        gather_cols(R.mc, r, c)
        trio_end(o_hops)

        def product(t):
            total = dot_nn(og[t], R.wt[...])
            for j in range(SIDE):
                total = total + dot_nn(col_part(R.mc, j, t)[...], R.wo[j * HW : (j + 1) * HW])
            return total

        close = scatter_rows(R.s, r, product, lambda d: wait_cols(R.mc, r, c, d))
        R.m_all[...] = R.mc.g[...]
        R.o_all[...] = og[...]
        x1 = R.x[...].astype(F32) + close()
        R.x1[...] = x1
        total = col_sum(R.n, c, row_sums(x1 * x1))
        R.s2[...] = total
        scale = to_column(lax.rsqrt(total / D + EPSILON))
        rows_at(R.p.g, r)[...] = (R.x1[...] * scale * R.gain[...]).astype(BF)
        gather_rows(R.p, r)

        def gate_up(rows, j):
            at = pl.ds(pl.multiple_of(j * BLK, BLK), BLK)
            return jnp.concatenate([dot_nn(rows, R.wg[:, at]), dot_nn(rows, R.wu[:, at])], axis=1)

        def finish(block, v):
            at = pl.ds(pl.multiple_of(block * BLK, BLK), BLK)
            gate, up = v[:, :256], v[:, 256:]
            sig = sigmoid(gate)
            act = gate * sig
            dh = R.dh[at]
            R.hid[at] = (act * up).astype(BF)
            R.dgu[at, 0:256] = (dh * up * sig * (1.0 + gate * (1.0 - sig))).astype(BF)
            R.dgu[at, 256:512] = (dh * act).astype(BF)

        close = scatter_cols(R.a, R.p, r, c, gate_up, 0, finish)
        R.n2_all[...] = R.p.g[...]
        close()
        for one in o_hops:
            one.wait_send()
        wait_cols_sent(R.mc, r, c)
        wait_rows_sent(R.p, r)

    scratch = dict(
        mc=gcols_scratch(HW),
        s=srows_scratch(),
        n=stat_scratch(),
        og=pltpu.VMEM((SIDE, BLK, 256), BF),
        ot=trio_scratch(),
        p=rows_scratch(),
        a=cols_scratch(512),
    )
    outs = dict(
        x1=((BLK, 512), F32),
        s2=((8, BLK), F32),
        m_all=((SIDE, LEN, HW), BF),
        o_all=((SIDE, BLK, 256), BF),
        n2_all=((LEN, 512), BF),
        hid=((LEN, 256), BF),
        dgu=((LEN, 512), BF),
    )
    return launch(forward, dict(m=m, o=o, x=x, gain=gain, wo=wo, wt=wt, wg=wg, wu=wu, dh=dh), outs, scratch, 3)


def norm_back(S, c, dn, v, scale, gain):
    gain_grad = jnp.sum(dn * v * scale, axis=0, keepdims=True)
    weighted = dn * gain
    total = col_sum(S, c, row_sums(weighted * v))
    inner = to_column(total)
    return scale * weighted - v * (scale * scale * scale * inner / D), gain_grad


def backward_kernel(dgu, wg, wu, x1, s2, gain, cot, n2, wo, wt):
    def backward(R):
        r, c = here()
        greet(r, c, rows=True, cols=(1, 2, 3))
        R.gc.g[c] = R.dgu[...]
        gather_cols(R.gc, r, c)

        def product(t):
            total = jnp.zeros((BLK, 512), F32)
            for j in range(SIDE):
                part = col_part(R.gc, j, t)[...]
                total = total + dot_nt(part[:, :256], R.wg[:, 256 * j : 256 * j + 256])
                total = total + dot_nt(part[:, 256:], R.wu[:, 256 * j : 256 * j + 256])
            return total

        close = scatter_rows(R.s, r, product, lambda d: wait_cols(R.gc, r, c, d))

        def grads(j, carry):
            at = pl.ds(pl.multiple_of(j * BLK, BLK), BLK)
            both = dot_tn(R.n2[...], R.gc.g[j])
            R.gate_w[:, at] = both[:, :256].astype(BF)
            R.up_w[:, at] = both[:, 256:].astype(BF)
            return carry

        lax.fori_loop(0, SIDE, grads, 0)
        dn = close()
        scale = to_column(lax.rsqrt(R.s2[...] / D + EPSILON))
        dv, dgain = norm_back(R.n, c, dn, R.x1[...], scale, R.gain[...])
        dx1 = R.cot[...] + dv
        R.dx1[...] = dx1
        R.dgain[...] = dgain
        rows_at(R.p.g, r)[...] = dx1.astype(BF)
        gather_rows(R.p, r)

        def out_back(rows, j):
            return dot_nt(rows, R.wo[pl.ds(pl.multiple_of(j * HW, 64), HW)])

        def finish(block, v):
            R.dm[pl.ds(pl.multiple_of(block * BLK, BLK), BLK)] = v

        close_a = scatter_cols(R.a, R.p, r, c, out_back, 0, finish)
        close_b = scatter_tokens(R.b, c, lambda j: dot_nt(rows_at(R.p.g, j)[...], R.wt[...]))
        R.dx_all[...] = R.p.g[...]
        close_a()
        R.do[...] = close_b().astype(BF)
        wait_cols_sent(R.gc, r, c)
        wait_rows_sent(R.p, r)

    scratch = dict(
        gc=gcols_scratch(512),
        s=srows_scratch(),
        n=stat_scratch(),
        p=rows_scratch(),
        a=cols_scratch(HW),
        b=tokens_scratch(BLK, 256, low=BF),
    )
    outs = dict(
        gate_w=((512, 1024), BF),
        up_w=((512, 1024), BF),
        dx1=((BLK, 512), F32),
        dgain=((1, 512), F32),
        dx_all=((LEN, 512), BF),
        dm=((LEN, HW), F32),
        do=((BLK, 256), BF),
    )
    ins = dict(dgu=dgu, wg=wg, wu=wu, x1=x1, s2=s2, gain=gain, cot=cot, n2=n2, wo=wo, wt=wt)
    return launch(backward, ins, outs, scratch, 6)


def project_back_kernel(da, db, ds, wa, wb, ws, x, s1, gain, dx1, n1, ffn_grad, dconv, dgain, dhead, dstates):
    pair = lax.axis_size("dp") == 2

    def project_back(R):
        r, c = here()
        greet(r, c, rows=True, cols=(1, 2, 3), dp=pair)
        R.ac.g[c] = R.da[...]
        bg, sg, tg = R.bg, R.sg, R.tg
        bg[c] = R.db[...]
        sg[c] = R.ds[...]
        tg[c] = jnp.zeros((8, 128), F32)
        tg[c, 0:4] = R.dstates[...]
        b_hops = trio(R.bt, c, lambda j: bg.at[j])
        s_hops = []
        for e in (1, 2, 3):
            to = flip(c, e)
            s_hops.append(hop(sg.at[c], sg.at[c], R.sgs.at[e - 1], R.sgr.at[e - 1], col=to))
            s_hops.append(hop(tg.at[c], tg.at[c], R.tgs.at[e - 1], R.tgr.at[e - 1], col=to))
        b_hops[0].start()
        b_hops[1].start()
        for one in s_hops:
            one.start()
        gather_cols(R.ac, r, c)

        peer = 1 - lax.axis_index("dp")
        owns, theirs = (R.bw, R.sw, R.zw, R.xw), (R.bp, R.sp, R.zp, R.xp)
        w_hops = [hop(a, b, R.wss.at[k], R.wsr.at[k], dp=peer) for k, (a, b) in enumerate(zip(owns, theirs))]
        small_hop = hop(R.small, R.small_p, R.mss, R.msr, dp=peer)

        trio_end(b_hops)
        for one in s_hops:
            one.wait_recv()
        R.bw[...] = dot_tn(R.n1[...], bg[...].reshape(LEN, 512)).astype(BF)
        R.sw[...] = dot_nn(sg[...].reshape(16 * SIDE, LEN), R.n1[...]).astype(BF)
        if pair:
            w_hops[0].start()
            w_hops[1].start()

        def product(t):
            total = dot_nt(bg[t], R.wb[...])
            at = pl.ds(pl.multiple_of(t * BLK, BLK), BLK)
            for j in range(SIDE):
                total = total + dot_nt(col_part(R.ac, j, t)[...], R.wa[j])
                total = total + dot_tn(sg[j, :, at], R.ws[16 * j : 16 * j + 16])
            return total

        close = scatter_rows(R.s, r, product, lambda d: wait_cols(R.ac, r, c, d))
        for j in range(SIDE):
            both = dot_tn(R.n1[...], R.ac.g[j]).astype(BF)
            R.zw[:, j * HW : (j + 1) * HW] = both[:, :HW]
            R.xw[:, j * HW : (j + 1) * HW] = both[:, HW:]
        if pair:
            w_hops[2].start()
            w_hops[3].start()
        dn = close()
        scale = to_column(lax.rsqrt(R.s1[...] / D + EPSILON))
        dv, mixer_grad = norm_back(R.n, c, dn, R.x[...].astype(F32), scale, R.gain[...])
        gg = R.gg
        gg[r] = jnp.zeros((8, 512), F32)
        gg[r, 0:1] = mixer_grad
        gg[r, 1:2] = R.ffn_grad[...]
        g_hops = [hop(gg.at[r], gg.at[r], R.ggs.at[d - 1], R.ggr.at[d - 1], row=flip(r, d)) for d in (1, 2, 3)]
        for one in g_hops:
            one.start()
        R.dx[...] = R.dx1[...] + dv
        small = R.small
        small[...] = jnp.zeros((SMALL, 512), F32)
        small[8:12, 0:HW] = R.dconv[...]
        small[12:13, 0:HW] = R.dgain[...]
        small[16:24, 0:128] = R.dhead[...]
        small[24:32, 0:128] = (tg[0] + tg[1]) + (tg[2] + tg[3])
        for one in g_hops:
            one.wait_recv()
        small[0:8] = (gg[0] + gg[1]) + (gg[2] + gg[3])
        if pair:
            small_hop.start()
        for one in (*b_hops, *s_hops, *g_hops):
            one.wait_send()
        wait_cols_sent(R.ac, r, c)
        if pair:
            small_hop.wait_recv()
            R.total[...] = small[...] + R.small_p[...]
            small_hop.wait_send()
        else:
            R.total[...] = small[...]
        for own, their, one, out_own, out_their in zip(
            owns, theirs, w_hops, (R.bo, R.so, R.zo, R.xo), (R.bq, R.sq, R.zq, R.xq)
        ):
            out_own[...] = own[...]
            if pair:
                one.wait_recv()
                out_their[...] = their[...]
                one.wait_send()
            else:
                out_their[...] = jnp.zeros_like(out_their)

    low = dict(b=((512, 512), BF), s=((16 * SIDE, 512), BF), z=((512, 768), BF), x=((512, 768), BF))
    scratch = dict(
        ac=gcols_scratch(2 * HW),
        s=srows_scratch(),
        n=stat_scratch(),
        bt=trio_scratch(),
        bg=pltpu.VMEM((SIDE, BLK, 512), BF),
        sg=pltpu.VMEM((SIDE, 16, LEN), BF),
        sgs=dma(3),
        sgr=dma(3),
        tg=pltpu.VMEM((SIDE, 8, 128), F32),
        tgs=dma(3),
        tgr=dma(3),
        gg=pltpu.VMEM((SIDE, 8, 512), F32),
        ggs=dma(3),
        ggr=dma(3),
        bw=pltpu.VMEM(*low["b"]),
        bp=pltpu.VMEM(*low["b"]),
        sw=pltpu.VMEM(*low["s"]),
        sp=pltpu.VMEM(*low["s"]),
        zw=pltpu.VMEM(*low["z"]),
        zp=pltpu.VMEM(*low["z"]),
        xw=pltpu.VMEM(*low["x"]),
        xp=pltpu.VMEM(*low["x"]),
        wss=dma(4),
        wsr=dma(4),
        small=pltpu.VMEM((SMALL, 512), F32),
        small_p=pltpu.VMEM((SMALL, 512), F32),
        mss=dma(),
        msr=dma(),
    )
    outs = dict(
        dx=((BLK, 512), F32),
        total=((SMALL, 512), F32),
        bo=low["b"],
        bq=low["b"],
        so=low["s"],
        sq=low["s"],
        zo=low["z"],
        zq=low["z"],
        xo=low["x"],
        xq=low["x"],
    )
    ins = dict(da=da, db=db, ds=ds, wa=wa, wb=wb, ws=ws, x=x, s1=s1, gain=gain, dx1=dx1, n1=n1)
    ins.update(ffn_grad=ffn_grad, dconv=dconv, dgain=dgain, dhead=dhead, dstates=dstates)
    return launch(project_back, ins, outs, scratch, 8)


def per_head(values):
    lane = iota((1, HW), 1)
    first = jnp.where(lane < HDIM, values[0], values[1])
    return jnp.where(lane < 2 * HDIM, first, values[2])


def head_select():
    return jnp.where(iota((8, HW), 1) // HDIM == iota((8, HW), 0), 1.0, 0.0).astype(F32)


def scalar_rows(ref):
    sub = iota((8, 1), 0)
    return jnp.where(sub == 0, ref[0], jnp.where(sub == 1, ref[1], jnp.where(sub == 2, ref[2], 0.0)))


def triangle():
    return jnp.where(iota((BLK, BLK), 0) <= iota((BLK, BLK), 1), 1.0, 0.0).astype(F32)


def fill_padded(R):
    R.xpad[0:8] = jnp.zeros((8, HW), F32)
    R.xpad[8 : 8 + LEN] = R.xr[...]


def conv_block(R, b):
    start = pl.multiple_of(b * BLK, BLK)
    chunk = R.xpad[pl.ds(start, BLK + 8)]
    taps = [chunk[5 + j : 5 + j + BLK] for j in range(4)]
    pre = taps[0] * R.wc[0:1]
    for j in (1, 2, 3):
        pre = pre + taps[j] * R.wc[j : j + 1]
    return pre, taps


def step_block(R, b):
    at = pl.ds(pl.multiple_of(b * BLK, BLK), BLK)
    raw = R.sr[:, at] + scalar_rows(R.bias)
    dt = softplus(raw)
    rate = -dt * jnp.exp(scalar_rows(R.decay))
    within = dot_nn(rate, triangle(), HIGHEST)
    return raw, dt, rate, within, jnp.transpose(dt), jnp.transpose(within)


def rope_turn(v, cosine, sine):
    return v * cosine + pltpu.roll(v, ADIM // 2, axis=1) * sine


def rope_tables():
    half = ADIM // 2
    freqs = np.float32(ROPE_BASE) ** (-np.arange(half, dtype=np.float32) / np.float32(half))
    angles = np.arange(LEN, dtype=np.float32)[:, None] * freqs.astype(np.float32)
    angles = angles.astype(np.float32).astype(np.float64)
    cosine, sine = np.cos(angles), np.sin(angles)
    return (
        np.concatenate([cosine, cosine], axis=1).astype(np.float32),
        np.concatenate([-sine, sine], axis=1).astype(np.float32),
    )


def key_scores(q, keys, c):
    s = dot_nt(q, keys) * SCALE
    return jnp.where(iota(s.shape, 1) <= c * BLK + iota(s.shape, 0), s, NEGATIVE)


def state_cols(R, kind, b):
    g = R.g
    return jnp.concatenate([g[2 * kind, b], g[2 * kind + 1, b]], axis=1).astype(F32)


def lower_decay(within_c, within_r, h):
    gaps = within_c[:, h : h + 1] - within_r[h : h + 1]
    return jnp.exp(jnp.where(iota((BLK, BLK), 1) <= iota((BLK, BLK), 0), gaps, NEGATIVE))


def head_mask(v, h):
    return jnp.where(iota((1, HW), 1) // HDIM == h, v, jnp.zeros_like(v))


def column_heads(cols):
    return per_head([cols[:, h : h + 1] for h in range(HH)])


def mixers_kernel(z, xr, br, sr, wc, wcs, bias, decay, skip, gain, cosine, sine, cot, wd):
    def mixers(R):
        r, c = here()
        greet(r, c, grid=True)
        g = R.g
        br = R.br
        pre = br[13 : 13 + BLK, 0:128] * R.wcs[0:1]
        for j in (1, 2, 3):
            pre = pre + br[13 + j : 13 + j + BLK, 0:128] * R.wcs[j : j + 1]
        g[r, c] = (pre * sigmoid(pre)).astype(BF)
        at = pl.ds(pl.multiple_of(c * BLK, BLK), BLK)
        cos, sin = R.cos[at], R.sin[at]
        kv = br[HALO : HALO + BLK, 384:512].astype(BF)
        turned = rope_turn(kv.astype(F32), cos, sin).astype(BF)
        kind, head = lax.div(r, 2), lax.rem(r, 2)
        kvb = R.kvb
        kvb[...] = jnp.where(kind == 0, turned, kv)
        slot = SIDE + kind

        @pl.when(head == kind)
        def _():
            g[slot, c] = kvb[...]

        def bc_hop(d):
            return hop(g.at[r, c], g.at[r, c], R.zs.at[d - 1], R.zr.at[d - 1], row=flip(r, d))

        def kv_hop(d):
            return hop(kvb, g.at[slot, c], R.ys.at[d - 1], R.yr.at[d - 1], row=flip(r, d))

        for d in (1, 2, 3):
            bc_hop(d).start()

            @pl.when(lax.div(flip(r, d), 2) == head)
            def _():
                kv_hop(d).start()

        rows_at(R.p.g, r)[...] = R.cot[...].astype(BF)
        gather_rows(R.p, r)
        fill_padded(R)
        for d in (1, 2, 3):
            bc_hop(d).wait_recv()

            @pl.when(lax.rem(flip(r, d), 2) == kind)
            def _():
                kv_hop(d).wait_recv()

        g_hops = trio(R.gt, c, lambda j: g.at[:, j])
        g_hops[0].start()
        g_hops[1].start()
        for h in range(2):
            q = br[HALO : HALO + BLK, 128 + 128 * h : 256 + 128 * h].astype(BF).astype(F32)
            R.qr[h] = rope_turn(q, cos, sin).astype(BF)
        trio_end(g_hops)

        state = R.state
        state[...] = jnp.zeros_like(state)
        st = R.n.st
        st[r, c] = jnp.zeros((8, BLK), F32)
        skip_row = per_head([R.skip[h] for h in range(HH)])

        def block(b, carry):
            at = pl.ds(pl.multiple_of(b * BLK, BLK), BLK)
            pre, _ = conv_block(R, b)
            u = pre * sigmoid(pre)
            _, _, _, within, dt_c, within_c = step_block(R, b)
            bb, cb = state_cols(R, 0, b), state_cols(R, 1, b)
            x = u * column_heads(dt_c)
            xb = x
            scores = dot_nt(cb, bb, HIGHEST)
            y = jnp.exp(column_heads(within_c)) * dot_nn(cb, state[...], HIGHEST)
            for h in range(HH):
                a = (scores * lower_decay(within_c, within, h))
                y = y + dot_nn(a, head_mask(xb, h), HIGHEST)
            last = per_head([within[h : h + 1, BLK - 1 : BLK] for h in range(HH)])
            keep = jnp.exp(last - column_heads(within_c))
            R.states[b] = state[...]
            state[...] = state[...] * jnp.exp(last) + dot_tn(bb, (x * keep), HIGHEST)
            y = y + skip_row * u
            zb = R.z[at]
            gated = y * zb * sigmoid(zb)
            R.y[at] = y
            R.gs[at] = gated
            sums = row_sums(gated * gated)
            st[r, c] = jnp.where(iota((8, BLK), 0) == b, sums, st[r, c])
            return carry

        lax.fori_loop(0, SIDE, block, 0)
        close = grid_sum(R.n, r, c)

        def hidden_back(rows, j):
            return dot_nt(rows, R.wd[pl.ds(pl.multiple_of(j * BLK, BLK), BLK)])

        def finish(block, v):
            R.dh[pl.ds(pl.multiple_of(block * BLK, BLK), BLK)] = v

        close_h = scatter_cols(R.a, R.p, r, c, hidden_back, 0, finish, True)
        keys = g[4].reshape(LEN, ADIM)
        values = g[5].reshape(LEN, ADIM)
        for h in range(2):
            s = key_scores(R.qr[h], keys, c)
            top = jnp.max(s, axis=1, keepdims=True)
            lse = top + jnp.log(jnp.sum(jnp.exp(s - top), axis=1, keepdims=True))
            R.lse[h] = jnp.broadcast_to(lse, (BLK, 128))
            probs = jnp.exp(s - lse).astype(BF)
            R.o[:, 128 * h : 128 * h + 128] = dot_nn(probs, values).astype(BF)

        total = close()
        R.s3[...] = total
        scales = jnp.transpose(lax.rsqrt(total / (HEADS * HDIM) + EPSILON))

        def scaled(b, carry):
            at = pl.ds(pl.multiple_of(b * BLK, BLK), BLK)
            R.m[at] = (R.gs[at] * pick_column(scales, b) * R.gain[...]).astype(BF)
            return carry

        lax.fori_loop(0, SIDE, scaled, 0)
        R.g_o[...] = g[...]
        R.dy[...] = R.p.g[...]
        close_h()
        wait_rows_sent(R.p, r)
        for d in (1, 2, 3):
            bc_hop(d).wait_send()

            @pl.when(lax.div(flip(r, d), 2) == head)
            def _():
                kv_hop(d).wait_send()

        for one in g_hops:
            one.wait_send()

    scratch = dict(
        n=grid_scratch(),
        p=rows_scratch(),
        a=cols_scratch(256),
        g=pltpu.VMEM((6, SIDE, BLK, 128), BF),
        kvb=pltpu.VMEM((BLK, 128), BF),
        xpad=pltpu.VMEM((LEN + 8, HW), F32),
        gs=pltpu.VMEM((LEN, HW), F32),
        state=pltpu.VMEM((STATE, HW), F32),
        zs=dma(3),
        zr=dma(3),
        ys=dma(3),
        yr=dma(3),
        gt=trio_scratch(),
    )
    outs = dict(
        m=((LEN, HW), BF),
        o=((BLK, 256), BF),
        y=((LEN, HW), F32),
        s3=((8, BLK), F32),
        lse=((2, BLK, 128), F32),
        states=((SIDE, STATE, HW), F32),
        g_o=((6, SIDE, BLK, 128), BF),
        qr=((2, BLK, 128), BF),
        dy=((LEN, 512), BF),
        dh=((LEN, 256), F32),
    )
    ins = dict(z=z, xr=xr, br=br, sr=sr, wc=wc, wcs=wcs, gain=gain, cos=cosine, sin=sine, cot=cot, wd=wd)
    return launch(mixers, ins, outs, scratch, 9, dict(bias=bias, decay=decay, skip=skip))


def mixers_back_kernel(
    dm, do, z, xr, br, sr, y, s3, states, g, qr, lse, wc, wcs, bias, decay, skip, gain, cosine, sine, hid, wd, x1, dy, m, o, dx
):
    n = BLK + HALO

    def mixers_back(R):
        r, c = here()
        greet(r, c, grid=True)
        R.hc.g[c] = R.hid[...]
        gather_cols(R.hc, r, c)
        g = R.g
        fill_padded(R)
        st = R.n.st
        st[r, c] = jnp.zeros((8, BLK), F32)
        gain = R.gain[...]

        def inner(b, carry):
            at = pl.ds(pl.multiple_of(b * BLK, BLK), BLK)
            zb = R.z[at]
            sums = row_sums(R.dm[at] * gain * R.y[at] * zb * sigmoid(zb))
            st[r, c] = jnp.where(iota((8, BLK), 0) == b, sums, st[r, c])
            return carry

        lax.fori_loop(0, SIDE, inner, 0)
        close = grid_sum(R.n, r, c)

        tb = R.tb
        tb[:, pl.ds(LEN, HALO)] = jnp.zeros((6, HALO, 128), F32)
        keys = g[4].reshape(LEN, ADIM)
        values = g[5].reshape(LEN, ADIM)
        at = pl.ds(pl.multiple_of(c * BLK, BLK), BLK)
        cos, sin = R.cos[at], R.sin[at]
        for h in range(2):
            q = R.qr[h]
            dob = R.do[:, 128 * h : 128 * h + 128]
            p = jnp.exp(key_scores(q, keys, c) - R.lse[h][:, :1])
            dv = dot_tn(p.astype(BF), dob)
            dp = dot_nt(dob, values)
            ds = (p * (dp - jnp.sum(dp * p, axis=1, keepdims=True)) * SCALE).astype(BF)
            dk = dot_tn(ds, q)
            if h == 0:
                tb[4, 0:LEN] = dk
                tb[5, 0:LEN] = dv
            else:
                tb[4, 0:LEN] = tb[4, 0:LEN] + dk
                tb[5, 0:LEN] = tb[5, 0:LEN] + dv
            dq = dot_nn(ds, keys)
            R.db[:, 128 + 128 * h : 256 + 128 * h] = rope_turn(dq, cos, -sin).astype(BF)

        scales = jnp.transpose(lax.rsqrt(R.s3[...] / (HEADS * HDIM) + EPSILON))
        inners = jnp.transpose(close())

        def down(t):
            total = dot_nn(col_part(R.hc, 0, t)[...], R.wd[0:256])
            for j in (1, 2, 3):
                total = total + dot_nn(col_part(R.hc, j, t)[...], R.wd[256 * j : 256 * j + 256])
            return total

        close_d = scatter_rows(R.s, r, down, lambda d: wait_cols(R.hc, r, c, d))
        dstate, dpre_pad = R.dstate, R.dpre
        dstate[...] = jnp.zeros_like(dstate)
        dpre_pad[LEN : LEN + 8] = jnp.zeros((8, HW), F32)
        select = head_select()
        skip_row = per_head([R.skip[h] for h in range(HH)])
        rate_of = jnp.exp(scalar_rows(R.decay))
        for ref in (R.dgain, R.dskip, R.dconv, R.dhead, R.ds):
            ref[...] = jnp.zeros_like(ref)
        upto = jnp.where(iota((BLK, BLK), 0) >= iota((BLK, BLK), 1), 1.0, 0.0).astype(F32)

        def block(i, carry):
            b = 3 - i
            at = pl.ds(pl.multiple_of(b * BLK, BLK), BLK)
            pre, taps = conv_block(R, b)
            sig = sigmoid(pre)
            u = pre * sig
            raw, dt, rate, within, dt_c, within_c = step_block(R, b)
            bb, cb = state_cols(R, 0, b), state_cols(R, 1, b)
            zb, yb, dm = R.z[at], R.y[at], R.dm[at]
            zsig = sigmoid(zb)
            zact = zb * zsig
            gated = yb * zact
            scale = pick_column(scales, b)
            dgated = scale * dm * gain - gated * (scale * scale * scale * pick_column(inners, b) / (HEADS * HDIM))
            R.dgain[...] += jnp.sum(dm * gated * scale, axis=0, keepdims=True)
            dy = dgated * zact
            R.da[at, 0:HW] = (dgated * yb * zsig * (1.0 + zb * (1.0 - zsig))).astype(BF)
            R.dskip[...] += jnp.sum(dy * u, axis=0, keepdims=True)
            dyb = dy
            dyr = dyb.astype(F32)
            wide = column_heads(within_c)
            grow = jnp.exp(wide)
            last = per_head([within[h : h + 1, BLK - 1 : BLK] for h in range(HH)])
            keep = jnp.exp(last - wide)
            dt_w = column_heads(dt_c)
            x = u * dt_w
            xb = x
            scores = dot_nt(cb, bb, HIGHEST)
            state = R.states[b]
            stb = state
            yin = jnp.zeros((BLK, HW), F32)
            dx = jnp.zeros((BLK, HW), F32)
            dscores = jnp.zeros((BLK, BLK), F32)
            for h in range(HH):
                decay_h = lower_decay(within_c, within, h)
                a = (scores * decay_h)
                xh = head_mask(xb, h)
                yin = yin + dot_nn(a, xh, HIGHEST)
                dx = dx + dot_tn(a, head_mask(dyb, h), HIGHEST)
                dscores = dscores + dot_nt(dyb, xh, HIGHEST) * decay_h
            dsb = dscores
            dyg = dyr * grow
            dygb = dyg
            xk = x * keep
            dst = dstate[...]
            dstb = dst
            dc = dot_nn(dsb, bb, HIGHEST) + dot_nt(dygb, stb, HIGHEST)
            db = dot_tn(dsb, cb, HIGHEST) + dot_nt(xk, dstb, HIGHEST)
            tb[0, at] = db[:, :128]
            tb[1, at] = db[:, 128:]
            tb[2, at] = dc[:, :128]
            tb[3, at] = dc[:, 128:]
            dxk = dot_nn(bb, dstb, HIGHEST)
            carried = dxk * xk
            turn = dyr * yin - xb.astype(F32) * dx + dyg * dot_nn(cb, stb, HIGHEST) - carried
            dx = dx + dxk * keep
            elast = jnp.exp(last)
            ends = jnp.sum(carried, axis=0, keepdims=True) + jnp.sum(dst * state, axis=0, keepdims=True) * elast
            dlast = dot_nt(select, jnp.broadcast_to(ends, (8, HW)), HIGHEST)[:, :1]
            drate = dot_nn(dot_nt(select, turn, HIGHEST), upto, HIGHEST) + dlast
            ddt = dot_nt(select, dx * u, HIGHEST) - drate * rate_of
            draw = ddt * sigmoid(raw)
            R.ds[0:8, at] = draw.astype(BF)
            lane = iota((8, 128), 1)
            R.dhead[...] += jnp.where(
                lane == 0,
                jnp.sum(draw, axis=1, keepdims=True),
                jnp.where(lane == 1, jnp.sum(drate * rate, axis=1, keepdims=True), 0.0),
            )
            dstate[...] = dst * elast + dot_tn(cb, dygb, HIGHEST)
            du = dx * dt_w + dy * skip_row
            dpre = du * sig * (1.0 + pre * (1.0 - sig))
            dpre_pad[at] = dpre
            for j in range(4):
                R.dconv[j : j + 1] += jnp.sum(dpre * taps[j], axis=0, keepdims=True)
            chunk = dpre_pad[pl.ds(pl.multiple_of(b * BLK, BLK), BLK + 8)]
            dxr = chunk[3 : 3 + BLK] * R.wc[0:1]
            for j in (1, 2, 3):
                dxr = dxr + chunk[3 - j : 3 - j + BLK] * R.wc[j : j + 1]
            R.da[at, HW : 2 * HW] = dxr.astype(BF)
            return carry

        lax.fori_loop(0, SIDE, block, 0)
        R.dhead[...] += jnp.where(
            iota((8, 128), 1) == 2,
            dot_nt(select, jnp.broadcast_to(R.dskip[...], (8, HW)), HIGHEST)[:, :1],
            0.0,
        )

        def token_rows(j):
            return tb[:, pl.ds(pl.multiple_of(j * BLK, BLK), n)]

        close_t = scatter_tokens(R.t, c, token_rows)
        for j in range(SIDE):
            R.down_w[256 * j : 256 * j + 256] = dot_tn(R.hc.g[j], R.dy[...]).astype(BF)
        total = close_t()
        tob = R.tob
        tob[...] = total.astype(BF)
        mine = R.mine
        mine[...] = total
        kind, head = lax.div(r, 2), lax.rem(r, 2)

        def bc_hop(d):
            return hop(tob.at[flip(r, d)], R.zbr.at[d - 1], R.zs.at[d - 1], R.zr.at[d - 1], row=flip(r, d))

        def kv_hop(d):
            to = flip(r, d)
            return hop(
                tob.at[SIDE + lax.div(to, 2), pl.ds(0, BLK)],
                R.zkr.at[d - 1],
                R.ys.at[d - 1],
                R.yr.at[d - 1],
                row=to,
            )

        for d in (1, 2, 3):
            bc_hop(d).start()

            @pl.when(lax.rem(flip(r, d), 2) == kind)
            def _():
                kv_hop(d).start()

        for j in range(SIDE):
            R.out_w[HW * j : HW * j + HW] = dot_tn(R.m[j], R.dx[...]).astype(BF)
        R.attn_w[...] = dot_tn(R.o[...].reshape(LEN, 256), R.dx[...]).astype(BF)
        dpost = mine[r]
        dkv = R.dkv
        dkv[...] = jnp.zeros_like(dkv)

        @pl.when(head == kind)
        def _():
            dkv[...] = mine[SIDE + kind, 0:BLK]

        for d in (1, 2, 3):
            bc_hop(d).wait_recv()
            dpost = dpost + R.zbr[d - 1].astype(F32)

            @pl.when(lax.div(flip(r, d), 2) == head)
            def _():
                kv_hop(d).wait_recv()
                dkv[...] = dkv[...] + R.zkr[d - 1].astype(F32)

        br = R.br
        pre = br[13 : 13 + n, 0:128] * R.wcs[0:1]
        for j in (1, 2, 3):
            pre = pre + br[13 + j : 13 + j + n, 0:128] * R.wcs[j : j + 1]
        sig = sigmoid(pre)
        dpre = dpost * sig * (1.0 + pre * (1.0 - sig))
        dbc = dpre[3 : 3 + BLK] * R.wcs[0:1]
        for j in (1, 2, 3):
            dbc = dbc + dpre[3 - j : 3 - j + BLK] * R.wcs[j : j + 1]
        R.db[:, 0:128] = dbc.astype(BF)
        for j in range(4):
            R.dstates[j : j + 1] = jnp.sum(dpre[0:BLK] * br[13 + j : 13 + j + BLK, 0:128], axis=0, keepdims=True)
        R.out[...] = (R.x1[...] + close_d()).astype(BF)
        wait_cols_sent(R.hc, r, c)
        dkv_v = dkv[...]
        R.db[:, 384:512] = jnp.where(kind == 0, rope_turn(dkv_v, cos, -sin), dkv_v).astype(BF)
        for d in (1, 2, 3):
            bc_hop(d).wait_send()

            @pl.when(lax.rem(flip(r, d), 2) == kind)
            def _():
                kv_hop(d).wait_send()

    scratch = dict(
        n=grid_scratch(),
        hc=gcols_scratch(256),
        s=srows_scratch(),
        t=tokens_scratch(6, n, 128, low=BF),
        xpad=pltpu.VMEM((LEN + 8, HW), F32),
        dpre=pltpu.VMEM((LEN + 8, HW), F32),
        dstate=pltpu.VMEM((STATE, HW), F32),
        dskip=pltpu.VMEM((1, HW), F32),
        tb=pltpu.VMEM((6, LEN + HALO, 128), F32),
        tob=pltpu.VMEM((6, n, 128), BF),
        mine=pltpu.VMEM((6, n, 128), F32),
        dkv=pltpu.VMEM((BLK, 128), F32),
        zbr=pltpu.VMEM((3, n, 128), BF),
        zkr=pltpu.VMEM((3, BLK, 128), BF),
        zs=dma(3),
        zr=dma(3),
        ys=dma(3),
        yr=dma(3),
    )
    outs = dict(
        da=((LEN, 2 * HW), BF),
        db=((BLK, 512), BF),
        ds=((16, LEN), BF),
        dgain=((1, HW), F32),
        dconv=((4, HW), F32),
        dstates=((4, 128), F32),
        dhead=((8, 128), F32),
        out=((BLK, 512), BF),
        down_w=((LEN, 512), BF),
        out_w=((SIDE * HW, 512), BF),
        attn_w=((256, 512), BF),
    )
    ins = dict(dm=dm, do=do, z=z, xr=xr, br=br, sr=sr, y=y, s3=s3, states=states, g=g, qr=qr, lse=lse, wc=wc, wcs=wcs)
    ins.update(gain=gain, cos=cosine, sin=sine, hid=hid, wd=wd, x1=x1, dy=dy, m=m, o=o, dx=dx)
    return launch(mixers_back, ins, outs, scratch, 10, dict(bias=bias, decay=decay, skip=skip))


def dp_total(parts):
    if lax.axis_size("dp") == 2:
        peers = [lax.ppermute(p, "dp", ((0, 1), (1, 0))) for p in parts]
        return [p.astype(F32) + q.astype(F32) for p, q in zip(parts, peers)]
    return list(lax.psum(tuple(p.astype(F32) for p in parts), "dp"))


def on_device(
    block_input,
    mixer_gain,
    ssm_gate_weight,
    ssm_input_weight,
    ssm_bc_weight,
    ssm_step_weight,
    query_weight,
    keyval_weight,
    conv_input,
    conv_states,
    step_bias,
    decay_log,
    skip_gain,
    ssm_norm_gain,
    ssm_out_weight,
    attn_out_weight,
    ffn_gain,
    gate_up_weight,
    down_weight,
    cotangent,
):
    cosine, sine = (jnp.asarray(table) for table in rope_tables())
    step_w = jnp.pad(ssm_step_weight.T.reshape(SIDE, HH, -1), ((0, 0), (0, 16 - HH), (0, 0))).reshape(16 * SIDE, -1)
    wg, wu = gate_up_weight[:, 0], gate_up_weight[:, 1]
    mixer_row, ffn_row, ssm_row = mixer_gain[None], ffn_gain[None], ssm_norm_gain[None]
    wo, wt, wd = ssm_out_weight, attn_out_weight, down_weight

    p = project_kernel(
        block_input,
        mixer_row,
        ssm_gate_weight,
        ssm_input_weight,
        ssm_bc_weight,
        query_weight,
        keyval_weight,
        step_w,
        conv_states,
    )
    heads = (conv_input, p.wcs, step_bias, decay_log, skip_gain, ssm_row, cosine, sine)
    m = mixers_kernel(p.z, p.xr, p.br, p.sr, *heads, cotangent, wd)
    f = forward_kernel(m.m, m.o, block_input, ffn_row, wo, wt, wg, wu, m.dh)
    b = backward_kernel(f.dgu, wg, wu, f.x1, f.s2, ffn_row, cotangent, f.n2_all, wo, wt)
    gate_grad, up_grad = dp_total([b.gate_w, b.up_w])
    mixed = (p.z, p.xr, p.br, p.sr, m.y, m.s3, m.states, m.g_o, m.qr, m.lse)
    k = mixers_back_kernel(b.dm, b.do, *mixed, *heads, f.hid, wd, f.x1, m.dy, f.m_all, f.o_all, b.dx_all)
    down_grad, out_grad, attn_grad = dp_total([k.down_w, k.out_w, k.attn_w])
    q = project_back_kernel(
        k.da,
        k.db,
        k.ds,
        p.wa_o,
        p.wb_o,
        step_w,
        block_input,
        p.s1,
        mixer_row,
        b.dx1,
        p.n1,
        b.dgain,
        k.dconv,
        k.dgain,
        k.dhead,
        k.dstates,
    )
    pairs = ((q.zo, q.zq), (q.xo, q.xq), (q.bo, q.bq), (q.so, q.sq))
    sums = [own.astype(F32) + their.astype(F32) for own, their in pairs]
    total = q.total
    if lax.axis_size("dp") != 2:
        sums, total = lax.psum((sums, total), "dp")
    z_grad, x_grad, b_grad, step_grad = sums
    step_grad = step_grad.reshape(SIDE, 16, -1)[:, :HH].reshape(SIDE * HH, -1).T
    states_grad = lax.dynamic_slice(total, (24, lax.axis_index("col") * 32), (4, 32))
    return (
        k.out,
        q.dx,
        total[0],
        z_grad,
        x_grad,
        b_grad[:, 0:128],
        step_grad,
        b_grad[:, 128:384],
        b_grad[:, 384:512],
        total[8:12, 0:HW],
        states_grad,
        total[16 : 16 + HH, 0],
        total[16 : 16 + HH, 1],
        total[16 : 16 + HH, 2],
        total[12, 0:HW],
        out_grad,
        attn_grad,
        total[1],
        jnp.stack([gate_grad, up_grad], axis=1),
        down_grad,
    )


def solution(mesh):
    placed = (
        P(("dp", "row"), "col"),
        P("col"),
        P("col", "row"),
        P("col", "row"),
        P("col", "row"),
        P("col", "row"),
        P("col", "row"),
        P("col", "row"),
        P(None, ("row", "col")),
        P(None, ("row", "col")),
        P(("row", "col")),
        P(("row", "col")),
        P(("row", "col")),
        P(("row", "col")),
        P("row", "col"),
        P("row", "col"),
        P("col"),
        P("col", None, "row"),
        P("row", "col"),
        P(("dp", "row"), "col"),
    )
    return jax.shard_map(
        on_device,
        mesh=mesh,
        in_specs=placed,
        out_specs=(
            P(("dp", "row"), "col"),
            P(("dp", "row"), "col"),
            P("col"),
            P("col", "row"),
            P("col", "row"),
            P("col", "row"),
            P("col", "row"),
            P("col", "row"),
            P("col", "row"),
            P(None, ("row", "col")),
            P(None, ("row", "col")),
            P(("row", "col")),
            P(("row", "col")),
            P(("row", "col")),
            P(("row", "col")),
            P("row", "col"),
            P("row", "col"),
            P("col"),
            P("col", None, "row"),
            P("row", "col"),
        ),
        check_vma=False,
    )
```

time: 1640 us -> 537 us (0.33)
  waiting for transfers between devices: 960 us -> 0.01 us
  Pallas kernels: 0 us -> 484 us
  local copies, waits for them, and re-layouts: 251 us -> 24.9 us
  matrix products: 138 us -> 0 us
  blocking collectives: 133 us -> 0 us
  other arithmetic: 114 us -> 15.3 us
    pallas_call x0 -> x6, Pallas kernels: none -> 484 us  [launch(): pl.pallas_call(kernel, out_shape=[jax.ShapeDtypeStruct(*o) for o in outs....]
    reduce_scatter x7 -> x0, waiting for transfers between devices: 280 us -> none  [the longest x3 158 us: col_scatter(): return lax.psum_scatter(values, 'col', scatter_dimension=1, tiled=True)]
    psum x1 -> x0, waiting for transfers between devices: 264 us -> none  [on_device(): lax.psum((in_grads[0], in_grads[1], in_grads[2], in_grads[3], in_grads[4]...]
    unnamed x24 -> x0, waiting for transfers between devices: 216 us -> none
    all_gather x10 -> x0, waiting for transfers between devices: 184 us -> none  [the longest x4 105 us: col_gather(): return lax.all_gather(values, 'col', axis=1, tiled=True)]
    dot_general x74 -> x0, matrix products: 138 us -> none  [the longest x12 26.8 us: ssd_block(): jnp.einsum('sijh,sjhp->sihp', scores[..., None] * decay, xdt, precision=H...]
    psum x8 -> x0, blocking collectives: 122 us -> none  [the longest x2 64.2 us: grid_total(): return lax.psum(values, ('row', 'col'))]
    unnamed x254 -> x27, local copies, waits for them, and re-layouts: 66.4 us -> 6.79 us
  transfers between devices with their start and end apart: 24 -> 5, of which waited for: 22 -> 0; matrix products, arithmetic and copies ran while one was open for 14% -> 5% of each run, Pallas kernels for 0% -> 26%
where the time goes in v1:
time: 537 us; the launch traced here: 532 us
  Pallas kernels  484 us (90%)
  local copies, waits for them, and re-layouts  24.9 us (5%)
  other arithmetic  15.3 us (3%)
  starting transfers between devices  5.67 us (1%)
    pallas_call x6, Pallas kernels, launch(): pl.pallas_call(kernel, out_shape=[jax.ShapeDtypeStruct(*o) for o in outs....  484 us
  transfers between devices with their start and end apart: 5, of which 0 were waited for; matrix products, arithmetic and copies ran while one was open for 5% of the time, Pallas kernels for 26%

profile of v1, /device:TPU:0, one launch (start us, length us, event | category | flops | bytes accessed | tf_op | source)
XLA Modules:
  0.0 531.6 jit_solution(7217520001962600452)
XLA Ops:
  1.4 5.6 %fusion = (bf16[512,1,1024]{2,1,0:T(2,128)(2,1)S(1)}, bf16[512,1,1024]{2,1,0:T(2,128)(2,1)S(1)}) fusion(bf16[512,2,1024]{2,1,0:T(2,128)(2,1)} %param.39), kind=kLoop, calls=%fused_computation.16 | loop fusion | bytes 4194304 | tf_op jit(solution)/shard_map/slice | solution.py:1404
  7.6 2.1 copy_bitcast_fusion
  9.7 57.2 %project.1 = (bf16[1024,512]{1,0:T(8,128)(2,1)}, f32[8,256]{1,0:T(8,128)}, f32[1024,192]{1,0:T(8,128)}, f32[1024,192]{1,0:T(8,128)}, f32[288,512]{1,0:T(8,128)},...) custom-call(bf16[256,512]{1,0:T(8,128)(2,1)} %refs_6_.5, ...), custom_call_target="tpu_custom_call" | custom-call | tf_op jit(solution)/shard_map/project/pallas_call | solution.py:122
  67.0 57.4 %mixers.1 = (bf16[1024,192]{1,0:T(8,128)(2,1)}, bf16[256,256]{1,0:T(8,128)(2,1)}, f32[1024,192]{1,0:T(8,128)}, f32[8,256]{1,0:T(8,128)}, f32[2,256,128]{2,1,0:T(...) custom-call(f32[1024,192]{1,0:T(8,128)} %get-tuple-element.74.refs_0, ...), custom_call_target="tpu_custom_call" | custom-call | tf_op jit(solution)/shard_map/mixers/pallas_call | solution.py:122
  124.4 78.5 %forward.1 = (f32[256,512]{1,0:T(8,128)}, f32[8,256]{1,0:T(8,128)}, bf16[4,1024,192]{2,1,0:T(8,128)(2,1)}, bf16[4,256,256]{2,1,0:T(8,128)(2,1)}, bf16[1024,512]{...) custom-call(bf16[1024,192]{1,0:T(8,128)(2,1)} %get-tuple-element.79.refs_0_, ...), custom_call_target="tpu_custom_call" | custom-call | tf_op jit(solution)/shard_map/forward/pallas_call | solution.py:122
  202.9 73.6 %backward.1 = (bf16[512,1024]{1,0:T(8,128)(2,1)}, bf16[512,1024]{1,0:T(8,128)(2,1)}, f32[256,512]{1,0:T(8,128)}, f32[1,512]{1,0:T(1,128)}, bf16[1024,512]{1,0:T(...) custom-call(bf16[1024,512]{1,0:T(8,128)(2,1)} %get-tuple-element.82.refs_0_, ...), custom_call_target="tpu_custom_call" | custom-call | tf_op jit(solution)/shard_map/backward/pallas_call | solution.py:122
  276.5 80.8 %mixers_back.1 = (bf16[1024,384]{1,0:T(8,128)(2,1)}, bf16[256,512]{1,0:T(8,128)(2,1)}, bf16[16,1024]{1,0:T(8,128)(2,1)}, f32[1,192]{1,0:T(1,128)}, f32[4,192]{1,...) custom-call(f32[1024,192]{1,0:T(8,128)} %get-tuple-element.86.refs_0, ...), custom_call_target="tpu_custom_call" | custom-call | tf_op jit(solution)/shard_map/mixers_back/pallas_call | solution.py:122
  357.2 1.6 collective-permute-start.4
  359.3 1.6 collective-permute-start.3
  361.4 1.6 collective-permute-start
  362.9 137.0 %project_back.1 = (f32[256,512]{1,0:T(8,128)}, f32[32,512]{1,0:T(8,128)}, bf16[512,512]{1,0:T(8,128)(2,1)}, bf16[512,512]{1,0:T(8,128)(2,1)}, bf16[64,512]{1,0:T...) custom-call(bf16[1024,384]{1,0:T(8,128)(2,1)} %get-tuple-element.100, ...), custom_call_target="tpu_custom_call" | custom-call | tf_op jit(solution)/shard_map/project_back/pallas_call | solution.py:122
  499.9 1.5 convert_add_fusion.4
  502.2 1.3 convert_add_fusion.2
  503.6 1.3 convert_add_fusion.3
  504.9 1.4 fusion.2
  506.3 1.3 constant_dynamic-slice_fusion
  508.4 1.3 slice.46
  511.6 1.5 slice_reduce_fusion
  513.1 1.8 convert_add_fusion.5
  515.0 2.7 convert_add_fusion.1
  517.7 1.6 add_bitcast_fusion.1
  519.3 1.6 add_bitcast_fusion
  521.5 5.2 copy.47
  526.7 2.9 convert_add_fusion
  (42 shorter events, 8.0 us)
Async XLA Ops:
  276.5 82.4 %copy-start.1 = (bf16[512,1024]{1,0:T(8,128)(2,1)S(1)}, bf16[512,1024]{1,0:T(8,128)(2,1)}, u32[]{:S(2)}) copy-start(bf16[512,1024]{1,0:T(8,128)(2,1)} %get-tuple-element.125) | copy-start | bytes 3145732
  276.5 82.9 %copy-start = (bf16[512,1024]{1,0:T(8,128)(2,1)S(1)}, bf16[512,1024]{1,0:T(8,128)(2,1)}, u32[]{:S(2)}) copy-start(bf16[512,1024]{1,0:T(8,128)(2,1)} %get-tuple-element.126) | copy-start | bytes 3145732
  357.2 169.5 %collective-permute-start.4 = (bf16[1024,512]{1,0:T(8,128)(2,1)}, bf16[1024,512]{1,0:T(8,128)(2,1)}, u32[]{:S(2)}, u32[]{:S(2)}) collective-permute-start(bf16[1024,512]{1,0:T(8,128)(2,1)} %get-tuple-element.127), channel_id=1, source_target_pairs={{0,16},{16,0},{1,17},{17,1},{2,18},{18,2},{3,19},{19,3},{4,20},{20... | collective-permute-start | bytes 3145736 | tf_op jit(solution)/shard_map/ppermute | solution.py:1375
  358.9 158.9 %collective-permute-start.2 = (bf16[512,1024]{1,0:T(8,128)(2,1)S(1)}, bf16[512,1024]{1,0:T(8,128)(2,1)}, u32[]{:S(2)}, u32[]{:S(2)}) collective-permute-start(bf16[512,1024]{1,0:T(8,128)(2,1)S(1)} %copy-done.1), channel_id=1, source_target_pairs={{0,16},{16,0},{1,17},{17,1},{2,18},{18,2},{3,19},{19,3},{4,20},{20... | collective-permute-start | bytes 3145736 | tf_op jit(solution)/shard_map/ppermute | solution.py:1375
  359.3 160.0 %collective-permute-start.3 = (bf16[512,1024]{1,0:T(8,128)(2,1)S(1)}, bf16[512,1024]{1,0:T(8,128)(2,1)}, u32[]{:S(2)}, u32[]{:S(2)}) collective-permute-start(bf16[512,1024]{1,0:T(8,128)(2,1)S(1)} %copy-done), channel_id=1, source_target_pairs={{0,16},{16,0},{1,17},{17,1},{2,18},{18,2},{3,19},{19,3},{4,20},{20... | collective-permute-start | bytes 3145736 | tf_op jit(solution)/shard_map/ppermute | solution.py:1375
  360.9 152.2 %collective-permute-start.1 = (bf16[256,512]{1,0:T(8,128)(2,1)}, bf16[256,512]{1,0:T(8,128)(2,1)}, u32[]{:S(2)}, u32[]{:S(2)}) collective-permute-start(bf16[256,512]{1,0:T(8,128)(2,1)} %get-tuple-element.124), channel_id=1, source_target_pairs={{0,16},{16,0},{1,17},{17,1},{2,18},{18,2},{3,19},{19,3},{4,20},{20... | collective-permute-start | bytes 786440 | tf_op jit(solution)/shard_map/ppermute | solution.py:1375
  361.4 153.6 %collective-permute-start = (bf16[768,512]{1,0:T(8,128)(2,1)}, bf16[768,512]{1,0:T(8,128)(2,1)}, u32[]{:S(2)}, u32[]{:S(2)}) collective-permute-start(bf16[768,512]{1,0:T(8,128)(2,1)} %get-tuple-element.123), channel_id=1, source_target_pairs={{0,16},{16,0},{1,17},{17,1},{2,18},{18,2},{3,19},{19,3},{4,20},{20... | collective-permute-start | bytes 2359304 | tf_op jit(solution)/shard_map/ppermute | solution.py:1375
  499.9 2.3 copy-start.5
  499.9 2.3 copy-start.6
  501.4 2.2 copy-start.3
  501.4 2.2 copy-start.4
  503.5 1.3 copy-start.10
  503.5 1.3 copy-start.11
  503.6 9.6 %copy-start.9 = (bf16[256,512]{1,0:T(8,128)(2,1)S(1)}, bf16[256,512]{1,0:T(8,128)(2,1)}, u32[]{:S(2)}) copy-start(bf16[256,512]{1,0:T(8,128)(2,1)} %get-tuple-element.124) | copy-start | bytes 786436
  521.5 5.3 copy-start.2
  526.7 2.9 copy-start.8
  526.7 3.6 copy-start.7

commit v2 on v1

--- a/solution.py
+++ b/solution.py
@@ -24,6 +24,7 @@
 ROPE_BASE = 100000000000.0
 HIGHEST = lax.Precision.HIGHEST
 NEGATIVE = -1e30
+LETTERS = "abcd"
 BF = jnp.bfloat16
 F32 = jnp.float32
 MESH = pl.DeviceIdType.MESH
@@ -40,6 +41,22 @@
 
 def dot_tn(a, b, precision=None):
     return lax.dot_general(a, b, (((0,), (0,)), ((), ())), precision=precision, preferred_element_type=F32)
+
+
+def halves(v):
+    high = v.astype(BF)
+    return high, (v - high.astype(F32)).astype(BF)
+
+
+def fine(dot, a, b):
+    a = a if isinstance(a, tuple) else (a,)
+    b = b if isinstance(b, tuple) else (b,)
+    total = dot(a[0], b[0])
+    if len(b) > 1:
+        total = total + dot(a[0], b[1])
+    if len(a) > 1:
+        total = total + dot(a[1], b[0])
+    return total
 
 
 def sigmoid(v):
@@ -135,25 +152,53 @@
 
 def rows_scratch(padded=False):
     size = LEN + 2 * HALO if padded else LEN
-    return dict(g=pltpu.VMEM((size, D // SIDE), BF), zs=dma(3), zr=dma(3))
+    return dict(g=pltpu.VMEM((size, D // SIDE), BF), zs=dma(SIDE), zr=dma(3))
+
+
+def inner(r):
+    return lax.rem(r, 3) != 0
+
+
+def swapped(i):
+    return 2 * lax.rem(i, 2) + lax.div(i, 2)
+
+
+def row_hop(S, r, d, pad=0):
+    own = rows_at(S.g, r, pad)
+    return hop(own, own, S.zs.at[d - 1], S.zr.at[d - 1], row=flip(r, d))
+
+
+def pass_hop(S, r, pad=0):
+    part = rows_at(S.g, flip(r, 2), pad)
+    return hop(part, part, S.zs.at[3], S.zr.at[2], row=flip(r, 1))
 
 
 def gather_rows(S, r, pad=0):
-    own = rows_at(S.g, r, pad)
-    for d in (1, 2, 3):
-        hop(own, own, S.zs.at[d - 1], S.zr.at[d - 1], row=flip(r, d)).start()
+    row_hop(S, r, 2, pad).start()
+    row_hop(S, r, 1, pad).start()
+
+    @pl.when(inner(r))
+    def _():
+        row_hop(S, r, 3, pad).start()
 
 
 def wait_rows(S, r, d, pad=0):
-    block = flip(r, d)
-    part = rows_at(S.g, block, pad)
-    hop(part, part, S.zs.at[d - 1], S.zr.at[d - 1], row=block).wait_recv()
+    part = rows_at(S.g, flip(r, d), pad)
+    hop(part, part, S.zs.at[d - 1], S.zr.at[d - 1], row=flip(r, d)).wait_recv()
+
+    @pl.when((d == 2) & inner(r))
+    def _():
+        pass_hop(S, r, pad).start()
 
 
 def wait_rows_sent(S, r, pad=0):
-    own = rows_at(S.g, r, pad)
-    for d in (1, 2, 3):
-        hop(own, own, S.zs.at[d - 1], S.zr.at[d - 1], row=flip(r, d)).wait_send()
+    row_hop(S, r, 2, pad).wait_send()
+    row_hop(S, r, 1, pad).wait_send()
+
+    @pl.when(inner(r))
+    def _():
+        row_hop(S, r, 3, pad).wait_send()
+        pass_hop(S, r, pad).wait_send()
 
 
 def cols_scratch(w):
@@ -171,7 +216,7 @@
     )
 
 
-def scatter_cols(S, G, r, c, product, pad=0, finish=None, apart=False):
+def scatter_cols(S, G, r, c, product, finish, pad=0):
     cs, cr, xs, xr, acc = (S.cs, S.cr, S.xs, S.xr, S.acc)
 
     def core_hop(d):
@@ -180,8 +225,10 @@
     def x_hop(d):
         return hop(xs.at[d], xr.at[d], S.ss.at[d], S.sr.at[d], col=flip(c, 2))
 
-    def first(d):
-        @pl.when(d > 0)
+    def first(i):
+        d = swapped(i)
+
+        @pl.when(i > 0)
         def _():
             wait_rows(G, r, d, pad)
 
@@ -192,31 +239,15 @@
         S.mine[d] = product(rows, flip(c, 2))
         acc[d] = product(rows, c)
 
-    def second(d):
+    def second(i):
+        d = swapped(i)
         core_hop(d).wait_recv()
         xs[d] = (S.mine[d] + cr[d, 1]).astype(BF)
         x_hop(d).start()
         acc[d] = acc[d] + cr[d, 0]
 
-    def both(d, carry):
-        first(d)
-        second(d)
-        return carry
-
-    def only(phase):
-        def step(d, carry):
-            phase(d)
-            return carry
-
-        return step
-
-    if apart:
-        lax.fori_loop(0, SIDE, only(first), 0)
-        lax.fori_loop(0, SIDE, only(second), 0)
-    else:
-        lax.fori_loop(0, SIDE, both, 0)
-
-    def end(d, carry):
+    def end(i, carry):
+        d = swapped(i)
         x_hop(d).wait_recv()
         finish(flip(r, d), acc[d] + xr[d].astype(F32))
         x_hop(d).wait_send()
@@ -226,7 +257,16 @@
     def close():
         lax.fori_loop(0, SIDE, end, 0)
 
-    return close
+    return first, second, close
+
+
+def each(*phases):
+    def step(i, carry):
+        for phase in phases:
+            phase(i)
+        return carry
+
+    lax.fori_loop(0, SIDE, step, 0)
 
 
 def tokens_scratch(*shape, low=F32):
@@ -310,7 +350,7 @@
     return hop(part, part, getattr(S, kind + "s").at[d], getattr(S, kind + "r").at[d], col=to)
 
 
-def gather_cols(S, r, c, order=(3, 2, 1, 0)):
+def gather_cols(S, r, c, order=(3, 1, 2, 0)):
     for d in order:
         t = flip(r, d)
         col_hop(S, c, "x", t, d).start()
@@ -340,42 +380,78 @@
     return dict(
         ps=pltpu.VMEM((3, BLK, w), BF),
         pr=pltpu.VMEM((3, BLK, w), BF),
+        fr=pltpu.VMEM((BLK, w), BF),
         pa=pltpu.VMEM((BLK, w), F32),
         rs=dma(3),
         rr=dma(3),
+        frs=dma(),
     )
 
 
 def scatter_rows(S, r, product, ready):
     ps, pr, acc = S.ps, S.pr, S.pa
 
-    def row_hop(d):
+    def direct(d):
         return hop(ps.at[d - 1], pr.at[d - 1], S.rs.at[d - 1], S.rr.at[d - 1], row=flip(r, d))
 
-    def step(i, carry):
-        d = 3 - i
+    def aside():
+        return hop(ps.at[2], S.fr, S.rs.at[2], S.frs, row=flip(r, 1))
+
+    def step(i):
+        d = 3 - swapped(i)
         ready(d)
         acc[...] = product(flip(r, d))
+
+        @pl.when((d == 2) & inner(r))
+        def _():
+            aside().wait_recv()
+            acc[...] = acc[...] + S.fr[...].astype(F32)
 
         @pl.when(d > 0)
         def _():
             ps[d - 1] = acc[...].astype(BF)
-            row_hop(d).start()
-
-        return carry
-
-    lax.fori_loop(0, SIDE, step, 0)
+
+        @pl.when((d == 3) & jnp.logical_not(inner(r)))
+        def _():
+            aside().start()
+
+        @pl.when((d > 0) & ((d < 3) | inner(r)))
+        def _():
+            direct(d).start()
 
     def close():
-        total = acc[...]
+        for d in (1, 2):
+            direct(d).wait_recv()
+            acc[...] = acc[...] + pr[d - 1].astype(F32)
+
+        @pl.when(inner(r))
+        def _():
+            direct(3).wait_recv()
+            acc[...] = acc[...] + pr[2].astype(F32)
+
         for d in (1, 2, 3):
-            row_hop(d).wait_recv()
-            total = total + pr[d - 1].astype(F32)
-        for d in (1, 2, 3):
-            row_hop(d).wait_send()
-        return total
-
-    return close
+            direct(d).wait_send()
+        return acc[...]
+
+    return step, close
+
+
+def pair_scratch(*shapes):
+    found = dict(ss=dma(len(shapes)), sr=dma(len(shapes)))
+    for k, shape in enumerate(shapes):
+        found[LETTERS[k]] = pltpu.VMEM(shape, BF)
+        found[LETTERS[k].upper()] = pltpu.VMEM(shape, BF)
+    return found
+
+
+def pair_hop(S, k, own=None):
+    src = getattr(S, LETTERS[k]) if own is None else own
+    dst = getattr(S, LETTERS[k].upper())
+    return hop(src, dst, S.ss.at[k], S.sr.at[k], dp=1 - lax.axis_index("dp"))
+
+
+def paired():
+    return lax.axis_size("dp") == 2
 
 
 def row_sums(v):
@@ -488,7 +564,8 @@
             R.z[at] = v[:, 0:HW]
             R.xr[at] = v[:, HW : 2 * HW]
 
-        close_a = scatter_cols(R.a, R.p, r, c, lambda rows, j: dot_nn(rows, wa[j]), HALO, finish)
+        first, second, close_a = scatter_cols(R.a, R.p, r, c, lambda rows, j: dot_nn(rows, wa[j]), finish, HALO)
+        each(first, second)
         steps = dot_nt(R.ws[...], g[pl.ds(HALO, LEN)])
         for j in range(SIDE):
             R.ps[j] = steps[16 * j : 16 * j + 8]
@@ -580,7 +657,8 @@
                 total = total + dot_nn(col_part(R.mc, j, t)[...], R.wo[j * HW : (j + 1) * HW])
             return total
 
-        close = scatter_rows(R.s, r, product, lambda d: wait_cols(R.mc, r, c, d))
+        step, close = scatter_rows(R.s, r, product, lambda d: wait_cols(R.mc, r, c, d))
+        each(step)
         R.m_all[...] = R.mc.g[...]
         R.o_all[...] = og[...]
         x1 = R.x[...].astype(F32) + close()
@@ -605,7 +683,8 @@
             R.dgu[at, 0:256] = (dh * up * sig * (1.0 + gate * (1.0 - sig))).astype(BF)
             R.dgu[at, 256:512] = (dh * act).astype(BF)
 
-        close = scatter_cols(R.a, R.p, r, c, gate_up, 0, finish)
+        first, second, close = scatter_cols(R.a, R.p, r, c, gate_up, finish)
+        each(first, second)
         R.n2_all[...] = R.p.g[...]
         close()
         for one in o_hops:
@@ -642,11 +721,12 @@
     return scale * weighted - v * (scale * scale * scale * inner / D), gain_grad
 
 
-def backward_kernel(dgu, wg, wu, x1, s2, gain, cot, n2, wo, wt):
+def backward_kernel(dgu, wg, wu, x1, s2, gain, cot, n2, wo, wt, hid, wd, dy, m, o):
     def backward(R):
         r, c = here()
-        greet(r, c, rows=True, cols=(1, 2, 3))
+        greet(r, c, rows=True, cols=(1, 2, 3), dp=paired())
         R.gc.g[c] = R.dgu[...]
+        R.hc.g[c] = R.hid[...]
         gather_cols(R.gc, r, c)
 
         def product(t):
@@ -657,24 +737,45 @@
                 total = total + dot_nt(part[:, 256:], R.wu[:, 256 * j : 256 * j + 256])
             return total
 
-        close = scatter_rows(R.s, r, product, lambda d: wait_cols(R.gc, r, c, d))
-
-        def grads(j, carry):
+        step, close = scatter_rows(R.s, r, product, lambda d: wait_cols(R.gc, r, c, d))
+        each(step)
+        gather_cols(R.hc, r, c)
+
+        def grads(j):
             at = pl.ds(pl.multiple_of(j * BLK, BLK), BLK)
             both = dot_tn(R.n2[...], R.gc.g[j])
-            R.gate_w[:, at] = both[:, :256].astype(BF)
-            R.up_w[:, at] = both[:, 256:].astype(BF)
-            return carry
-
-        lax.fori_loop(0, SIDE, grads, 0)
+            R.y.a[:, at] = both[:, :256].astype(BF)
+            R.y.b[:, at] = both[:, 256:].astype(BF)
+
+        each(grads)
+        y_hops = [pair_hop(R.y, k) for k in range(2)] if paired() else []
+        for one in y_hops:
+            one.start()
+        R.gate_w[...] = R.y.a[...]
+        R.up_w[...] = R.y.b[...]
         dn = close()
         scale = to_column(lax.rsqrt(R.s2[...] / D + EPSILON))
         dv, dgain = norm_back(R.n, c, dn, R.x1[...], scale, R.gain[...])
         dx1 = R.cot[...] + dv
+        rows_at(R.p.g, r)[...] = dx1.astype(BF)
+        gather_rows(R.p, r)
         R.dx1[...] = dx1
         R.dgain[...] = dgain
-        rows_at(R.p.g, r)[...] = dx1.astype(BF)
-        gather_rows(R.p, r)
+
+        def down(i):
+            wait_cols(R.hc, r, c, 3 - swapped(i))
+            t = flip(r, 3 - swapped(i))
+            total = dot_nn(col_part(R.hc, 0, t)[...], R.wd[0:256])
+            for j in (1, 2, 3):
+                total = total + dot_nn(col_part(R.hc, j, t)[...], R.wd[256 * j : 256 * j + 256])
+            R.down[t] = total
+
+        each(down)
+
+        def down_grads(j):
+            R.down_w[pl.ds(pl.multiple_of(j * BLK, BLK), BLK)] = dot_tn(R.hc.g[j], R.dy[...]).astype(BF)
+
+        each(down_grads)
 
         def out_back(rows, j):
             return dot_nt(rows, R.wo[pl.ds(pl.multiple_of(j * HW, 64), HW)])
@@ -682,37 +783,56 @@
         def finish(block, v):
             R.dm[pl.ds(pl.multiple_of(block * BLK, BLK), BLK)] = v
 
-        close_a = scatter_cols(R.a, R.p, r, c, out_back, 0, finish)
+        first, second, close_a = scatter_cols(R.a, R.p, r, c, out_back, finish)
+        each(first, second)
         close_b = scatter_tokens(R.b, c, lambda j: dot_nt(rows_at(R.p.g, j)[...], R.wt[...]))
-        R.dx_all[...] = R.p.g[...]
+
+        def out_grads(j):
+            R.out_w[pl.ds(pl.multiple_of(j * HW, 64), HW)] = dot_tn(R.m[j], R.p.g[...]).astype(BF)
+
+        each(out_grads)
+        R.attn_w[...] = dot_tn(R.o[...].reshape(LEN, 256), R.p.g[...]).astype(BF)
         close_a()
         R.do[...] = close_b().astype(BF)
         wait_cols_sent(R.gc, r, c)
+        wait_cols_sent(R.hc, r, c)
         wait_rows_sent(R.p, r)
+        for one, theirs, out in zip(y_hops, (R.y.A, R.y.B), (R.gate_p, R.up_p) if y_hops else ()):
+            one.wait_recv()
+            out[...] = theirs[...]
+            one.wait_send()
 
     scratch = dict(
         gc=gcols_scratch(512),
+        hc=gcols_scratch(256),
         s=srows_scratch(),
         n=stat_scratch(),
         p=rows_scratch(),
         a=cols_scratch(HW),
         b=tokens_scratch(BLK, 256, low=BF),
+        y=pair_scratch((512, 1024), (512, 1024)),
     )
     outs = dict(
         gate_w=((512, 1024), BF),
         up_w=((512, 1024), BF),
         dx1=((BLK, 512), F32),
         dgain=((1, 512), F32),
-        dx_all=((LEN, 512), BF),
         dm=((LEN, HW), F32),
         do=((BLK, 256), BF),
-    )
+        down=((SIDE, BLK, 512), F32),
+        down_w=((LEN, 512), BF),
+        out_w=((SIDE * HW, 512), BF),
+        attn_w=((256, 512), BF),
+    )
+    if paired():
+        outs.update(gate_p=((512, 1024), BF), up_p=((512, 1024), BF))
     ins = dict(dgu=dgu, wg=wg, wu=wu, x1=x1, s2=s2, gain=gain, cot=cot, n2=n2, wo=wo, wt=wt)
+    ins.update(hid=hid, wd=wd, dy=dy, m=m, o=o)
     return launch(backward, ins, outs, scratch, 6)
 
 
 def project_back_kernel(da, db, ds, wa, wb, ws, x, s1, gain, dx1, n1, ffn_grad, dconv, dgain, dhead, dstates):
-    pair = lax.axis_size("dp") == 2
+    pair = paired()
 
     def project_back(R):
         r, c = here()
@@ -735,16 +855,14 @@
             one.start()
         gather_cols(R.ac, r, c)
 
-        peer = 1 - lax.axis_index("dp")
-        owns, theirs = (R.bw, R.sw, R.zw, R.xw), (R.bp, R.sp, R.zp, R.xp)
-        w_hops = [hop(a, b, R.wss.at[k], R.wsr.at[k], dp=peer) for k, (a, b) in enumerate(zip(owns, theirs))]
-        small_hop = hop(R.small, R.small_p, R.mss, R.msr, dp=peer)
+        y = R.y
+        w_hops = [pair_hop(y, k) for k in range(4)] if pair else []
 
         trio_end(b_hops)
         for one in s_hops:
             one.wait_recv()
-        R.bw[...] = dot_tn(R.n1[...], bg[...].reshape(LEN, 512)).astype(BF)
-        R.sw[...] = dot_nn(sg[...].reshape(16 * SIDE, LEN), R.n1[...]).astype(BF)
+        y.a[...] = dot_tn(R.n1[...], bg[...].reshape(LEN, 512)).astype(BF)
+        y.b[...] = dot_nn(sg[...].reshape(16 * SIDE, LEN), R.n1[...]).astype(BF)
         if pair:
             w_hops[0].start()
             w_hops[1].start()
@@ -757,11 +875,12 @@
                 total = total + dot_tn(sg[j, :, at], R.ws[16 * j : 16 * j + 16])
             return total
 
-        close = scatter_rows(R.s, r, product, lambda d: wait_cols(R.ac, r, c, d))
+        step, close = scatter_rows(R.s, r, product, lambda d: wait_cols(R.ac, r, c, d))
+        each(step)
         for j in range(SIDE):
             both = dot_tn(R.n1[...], R.ac.g[j]).astype(BF)
-            R.zw[:, j * HW : (j + 1) * HW] = both[:, :HW]
-            R.xw[:, j * HW : (j + 1) * HW] = both[:, HW:]
+            y.c[:, j * HW : (j + 1) * HW] = both[:, :HW]
+            y.d[:, j * HW : (j + 1) * HW] = both[:, HW:]
         if pair:
             w_hops[2].start()
             w_hops[3].start()
@@ -786,28 +905,36 @@
             one.wait_recv()
         small[0:8] = (gg[0] + gg[1]) + (gg[2] + gg[3])
         if pair:
+            small_hop = hop(small, R.small_p, R.mss, R.msr, dp=1 - lax.axis_index("dp"))
             small_hop.start()
         for one in (*b_hops, *s_hops, *g_hops):
             one.wait_send()
         wait_cols_sent(R.ac, r, c)
+        total = small[...]
         if pair:
             small_hop.wait_recv()
-            R.total[...] = small[...] + R.small_p[...]
+            total = total + R.small_p[...]
             small_hop.wait_send()
-        else:
-            R.total[...] = small[...]
-        for own, their, one, out_own, out_their in zip(
-            owns, theirs, w_hops, (R.bo, R.so, R.zo, R.xo), (R.bq, R.sq, R.zq, R.xq)
-        ):
-            out_own[...] = own[...]
-            if pair:
+        R.o_mixer[...] = total[0:1]
+        R.o_ffn[...] = total[1:2]
+        R.o_conv[...] = total[8:12, 0:HW]
+        R.o_gain[...] = total[12:13, 0:HW]
+        heads = jnp.transpose(total[16:24, 0:128])
+        R.o_bias[...] = heads[0:1, 0:HH]
+        R.o_decay[...] = heads[1:2, 0:HH]
+        R.o_skip[...] = heads[2:3, 0:HH]
+        taps = jnp.zeros((4, 32), F32)
+        for j in range(SIDE):
+            taps = taps + jnp.where(c == j, total[24:28, 32 * j : 32 * j + 32], 0.0)
+        R.o_states[...] = taps
+        for own, out in zip((y.a, y.b, y.c, y.d), (R.bo, R.so, R.zo, R.xo)):
+            out[...] = own[...]
+        if pair:
+            for one, theirs, out in zip(w_hops, (y.A, y.B, y.C, y.D), (R.bq, R.sq, R.zq, R.xq)):
                 one.wait_recv()
-                out_their[...] = their[...]
+                out[...] = theirs[...]
                 one.wait_send()
-            else:
-                out_their[...] = jnp.zeros_like(out_their)
-
-    low = dict(b=((512, 512), BF), s=((16 * SIDE, 512), BF), z=((512, 768), BF), x=((512, 768), BF))
+
     scratch = dict(
         ac=gcols_scratch(2 * HW),
         s=srows_scratch(),
@@ -823,16 +950,7 @@
         gg=pltpu.VMEM((SIDE, 8, 512), F32),
         ggs=dma(3),
         ggr=dma(3),
-        bw=pltpu.VMEM(*low["b"]),
-        bp=pltpu.VMEM(*low["b"]),
-        sw=pltpu.VMEM(*low["s"]),
-        sp=pltpu.VMEM(*low["s"]),
-        zw=pltpu.VMEM(*low["z"]),
-        zp=pltpu.VMEM(*low["z"]),
-        xw=pltpu.VMEM(*low["x"]),
-        xp=pltpu.VMEM(*low["x"]),
-        wss=dma(4),
-        wsr=dma(4),
+        y=pair_scratch((512, 512), (16 * SIDE, 512), (512, 768), (512, 768)),
         small=pltpu.VMEM((SMALL, 512), F32),
         small_p=pltpu.VMEM((SMALL, 512), F32),
         mss=dma(),
@@ -840,16 +958,21 @@
     )
     outs = dict(
         dx=((BLK, 512), F32),
-        total=((SMALL, 512), F32),
-        bo=low["b"],
-        bq=low["b"],
-        so=low["s"],
-        sq=low["s"],
-        zo=low["z"],
-        zq=low["z"],
-        xo=low["x"],
-        xq=low["x"],
-    )
+        o_mixer=((1, 512), F32),
+        o_ffn=((1, 512), F32),
+        o_conv=((4, HW), F32),
+        o_gain=((1, HW), F32),
+        o_bias=((1, HH), F32),
+        o_decay=((1, HH), F32),
+        o_skip=((1, HH), F32),
+        o_states=((4, 32), F32),
+        bo=((512, 512), BF),
+        so=((16 * SIDE, 512), BF),
+        zo=((512, 768), BF),
+        xo=((512, 768), BF),
+    )
+    if pair:
+        outs.update(bq=((512, 512), BF), sq=((16 * SIDE, 512), BF), zq=((512, 768), BF), xq=((512, 768), BF))
     ins = dict(da=da, db=db, ds=ds, wa=wa, wb=wb, ws=ws, x=x, s1=s1, gain=gain, dx1=dx1, n1=n1)
     ins.update(ffn_grad=ffn_grad, dconv=dconv, dgain=dgain, dhead=dhead, dstates=dstates)
     return launch(project_back, ins, outs, scratch, 8)
@@ -921,7 +1044,7 @@
 
 def state_cols(R, kind, b):
     g = R.g
-    return jnp.concatenate([g[2 * kind, b], g[2 * kind + 1, b]], axis=1).astype(F32)
+    return jnp.concatenate([g[2 * kind, b], g[2 * kind + 1, b]], axis=1)
 
 
 def lower_decay(within_c, within_r, h):
@@ -931,6 +1054,10 @@
 
 def head_mask(v, h):
     return jnp.where(iota((1, HW), 1) // HDIM == h, v, jnp.zeros_like(v))
+
+
+def head_masks(v, h):
+    return head_mask(v[0], h), head_mask(v[1], h)
 
 
 def column_heads(cols):
@@ -997,23 +1124,32 @@
         st[r, c] = jnp.zeros((8, BLK), F32)
         skip_row = per_head([R.skip[h] for h in range(HH)])
 
+        def hidden_back(rows, j):
+            return dot_nt(rows, R.wd[pl.ds(pl.multiple_of(j * BLK, BLK), BLK)])
+
+        def finish(block, v):
+            R.dh[pl.ds(pl.multiple_of(block * BLK, BLK), BLK)] = v
+
+        first, second, close_h = scatter_cols(R.a, R.p, r, c, hidden_back, finish)
+
         def block(b, carry):
+            first(b)
             at = pl.ds(pl.multiple_of(b * BLK, BLK), BLK)
             pre, _ = conv_block(R, b)
             u = pre * sigmoid(pre)
             _, _, _, within, dt_c, within_c = step_block(R, b)
             bb, cb = state_cols(R, 0, b), state_cols(R, 1, b)
             x = u * column_heads(dt_c)
-            xb = x
-            scores = dot_nt(cb, bb, HIGHEST)
-            y = jnp.exp(column_heads(within_c)) * dot_nn(cb, state[...], HIGHEST)
+            xb = halves(x)
+            scores = dot_nt(cb, bb)
+            y = jnp.exp(column_heads(within_c)) * fine(dot_nn, cb, halves(state[...]))
             for h in range(HH):
-                a = (scores * lower_decay(within_c, within, h))
-                y = y + dot_nn(a, head_mask(xb, h), HIGHEST)
+                a = halves(scores * lower_decay(within_c, within, h))
+                y = y + fine(dot_nn, a, head_masks(xb, h))
             last = per_head([within[h : h + 1, BLK - 1 : BLK] for h in range(HH)])
             keep = jnp.exp(last - column_heads(within_c))
             R.states[b] = state[...]
-            state[...] = state[...] * jnp.exp(last) + dot_tn(bb, (x * keep), HIGHEST)
+            state[...] = state[...] * jnp.exp(last) + fine(dot_tn, bb, halves(x * keep))
             y = y + skip_row * u
             zb = R.z[at]
             gated = y * zb * sigmoid(zb)
@@ -1021,18 +1157,12 @@
             R.gs[at] = gated
             sums = row_sums(gated * gated)
             st[r, c] = jnp.where(iota((8, BLK), 0) == b, sums, st[r, c])
+            second(b)
             return carry
 
         lax.fori_loop(0, SIDE, block, 0)
         close = grid_sum(R.n, r, c)
 
-        def hidden_back(rows, j):
-            return dot_nt(rows, R.wd[pl.ds(pl.multiple_of(j * BLK, BLK), BLK)])
-
-        def finish(block, v):
-            R.dh[pl.ds(pl.multiple_of(block * BLK, BLK), BLK)] = v
-
-        close_h = scatter_cols(R.a, R.p, r, c, hidden_back, 0, finish, True)
         keys = g[4].reshape(LEN, ADIM)
         values = g[5].reshape(LEN, ADIM)
         for h in range(2):
@@ -1099,15 +1229,18 @@
 
 
 def mixers_back_kernel(
-    dm, do, z, xr, br, sr, y, s3, states, g, qr, lse, wc, wcs, bias, decay, skip, gain, cosine, sine, hid, wd, x1, dy, m, o, dx
+    dm, do, z, xr, br, sr, y, s3, states, g, qr, lse, wc, wcs, bias, decay, skip, gain, cosine, sine, x1, down, down_w, out_w, attn_w
 ):
     n = BLK + HALO
 
     def mixers_back(R):
         r, c = here()
-        greet(r, c, grid=True)
-        R.hc.g[c] = R.hid[...]
-        gather_cols(R.hc, r, c)
+        greet(r, c, grid=True, dp=paired())
+        y_hops = []
+        if paired():
+            y_hops = [pair_hop(R.yy, k, own) for k, own in enumerate((R.down_w, R.out_w, R.attn_w))]
+        for one in y_hops:
+            one.start()
         g = R.g
         fill_padded(R)
         st = R.n.st
@@ -1150,13 +1283,7 @@
         scales = jnp.transpose(lax.rsqrt(R.s3[...] / (HEADS * HDIM) + EPSILON))
         inners = jnp.transpose(close())
 
-        def down(t):
-            total = dot_nn(col_part(R.hc, 0, t)[...], R.wd[0:256])
-            for j in (1, 2, 3):
-                total = total + dot_nn(col_part(R.hc, j, t)[...], R.wd[256 * j : 256 * j + 256])
-            return total
-
-        close_d = scatter_rows(R.s, r, down, lambda d: wait_cols(R.hc, r, c, d))
+        step, close_d = scatter_rows(R.s, r, lambda t: R.down[t], lambda d: None)
         dstate, dpre_pad = R.dstate, R.dpre
         dstate[...] = jnp.zeros_like(dstate)
         dpre_pad[LEN : LEN + 8] = jnp.zeros((8, HW), F32)
@@ -1168,6 +1295,7 @@
         upto = jnp.where(iota((BLK, BLK), 0) >= iota((BLK, BLK), 1), 1.0, 0.0).astype(F32)
 
         def block(i, carry):
+            step(i)
             b = 3 - i
             at = pl.ds(pl.multiple_of(b * BLK, BLK), BLK)
             pre, taps = conv_block(R, b)
@@ -1185,43 +1313,42 @@
             dy = dgated * zact
             R.da[at, 0:HW] = (dgated * yb * zsig * (1.0 + zb * (1.0 - zsig))).astype(BF)
             R.dskip[...] += jnp.sum(dy * u, axis=0, keepdims=True)
-            dyb = dy
-            dyr = dyb.astype(F32)
+            dyb = halves(dy)
             wide = column_heads(within_c)
             grow = jnp.exp(wide)
             last = per_head([within[h : h + 1, BLK - 1 : BLK] for h in range(HH)])
             keep = jnp.exp(last - wide)
             dt_w = column_heads(dt_c)
             x = u * dt_w
-            xb = x
-            scores = dot_nt(cb, bb, HIGHEST)
+            xb = halves(x)
+            scores = dot_nt(cb, bb)
             state = R.states[b]
-            stb = state
+            stb = halves(state)
             yin = jnp.zeros((BLK, HW), F32)
             dx = jnp.zeros((BLK, HW), F32)
             dscores = jnp.zeros((BLK, BLK), F32)
             for h in range(HH):
                 decay_h = lower_decay(within_c, within, h)
-                a = (scores * decay_h)
-                xh = head_mask(xb, h)
-                yin = yin + dot_nn(a, xh, HIGHEST)
-                dx = dx + dot_tn(a, head_mask(dyb, h), HIGHEST)
-                dscores = dscores + dot_nt(dyb, xh, HIGHEST) * decay_h
-            dsb = dscores
-            dyg = dyr * grow
-            dygb = dyg
+                a = halves(scores * decay_h)
+                xh = head_masks(xb, h)
+                yin = yin + fine(dot_nn, a, xh)
+                dx = dx + fine(dot_tn, a, head_masks(dyb, h))
+                dscores = dscores + fine(dot_nt, dyb, xh) * decay_h
+            dsb = halves(dscores)
+            dyg = dy * grow
+            dygb = halves(dyg)
             xk = x * keep
             dst = dstate[...]
-            dstb = dst
-            dc = dot_nn(dsb, bb, HIGHEST) + dot_nt(dygb, stb, HIGHEST)
-            db = dot_tn(dsb, cb, HIGHEST) + dot_nt(xk, dstb, HIGHEST)
+            dstb = halves(dst)
+            dc = fine(dot_nn, dsb, bb) + fine(dot_nt, dygb, stb)
+            db = fine(dot_tn, dsb, cb) + fine(dot_nt, halves(xk), dstb)
             tb[0, at] = db[:, :128]
             tb[1, at] = db[:, 128:]
             tb[2, at] = dc[:, :128]
             tb[3, at] = dc[:, 128:]
-            dxk = dot_nn(bb, dstb, HIGHEST)
+            dxk = fine(dot_nn, bb, dstb)
             carried = dxk * xk
-            turn = dyr * yin - xb.astype(F32) * dx + dyg * dot_nn(cb, stb, HIGHEST) - carried
+            turn = dy * yin - x * dx + dyg * fine(dot_nn, cb, stb) - carried
             dx = dx + dxk * keep
             elast = jnp.exp(last)
             ends = jnp.sum(carried, axis=0, keepdims=True) + jnp.sum(dst * state, axis=0, keepdims=True) * elast
@@ -1236,7 +1363,7 @@
                 jnp.sum(draw, axis=1, keepdims=True),
                 jnp.where(lane == 1, jnp.sum(drate * rate, axis=1, keepdims=True), 0.0),
             )
-            dstate[...] = dst * elast + dot_tn(cb, dygb, HIGHEST)
+            dstate[...] = dst * elast + fine(dot_tn, cb, dygb)
             du = dx * dt_w + dy * skip_row
             dpre = du * sig * (1.0 + pre * (1.0 - sig))
             dpre_pad[at] = dpre
@@ -1260,8 +1387,6 @@
             return tb[:, pl.ds(pl.multiple_of(j * BLK, BLK), n)]
 
         close_t = scatter_tokens(R.t, c, token_rows)
-        for j in range(SIDE):
-            R.down_w[256 * j : 256 * j + 256] = dot_tn(R.hc.g[j], R.dy[...]).astype(BF)
         total = close_t()
         tob = R.tob
         tob[...] = total.astype(BF)
@@ -1289,9 +1414,6 @@
             def _():
                 kv_hop(d).start()
 
-        for j in range(SIDE):
-            R.out_w[HW * j : HW * j + HW] = dot_tn(R.m[j], R.dx[...]).astype(BF)
-        R.attn_w[...] = dot_tn(R.o[...].reshape(LEN, 256), R.dx[...]).astype(BF)
         dpost = mine[r]
         dkv = R.dkv
         dkv[...] = jnp.zeros_like(dkv)
@@ -1322,7 +1444,6 @@
         for j in range(4):
             R.dstates[j : j + 1] = jnp.sum(dpre[0:BLK] * br[13 + j : 13 + j + BLK, 0:128], axis=0, keepdims=True)
         R.out[...] = (R.x1[...] + close_d()).astype(BF)
-        wait_cols_sent(R.hc, r, c)
         dkv_v = dkv[...]
         R.db[:, 384:512] = jnp.where(kind == 0, rope_turn(dkv_v, cos, -sin), dkv_v).astype(BF)
         for d in (1, 2, 3):
@@ -1332,10 +1453,15 @@
             def _():
                 kv_hop(d).wait_send()
 
+        for one, theirs, out in zip(y_hops, (R.yy.A, R.yy.B, R.yy.C), (R.down_p, R.out_p, R.attn_p) if y_hops else ()):
+            one.wait_recv()
+            out[...] = theirs[...]
+            one.wait_send()
+
     scratch = dict(
         n=grid_scratch(),
-        hc=gcols_scratch(256),
         s=srows_scratch(),
+        yy=pair_scratch((LEN, 512), (SIDE * HW, 512), (256, 512)),
         t=tokens_scratch(6, n, 128, low=BF),
         xpad=pltpu.VMEM((LEN + 8, HW), F32),
         dpre=pltpu.VMEM((LEN + 8, HW), F32),
@@ -1361,20 +1487,18 @@
         dstates=((4, 128), F32),
         dhead=((8, 128), F32),
         out=((BLK, 512), BF),
-        down_w=((LEN, 512), BF),
-        out_w=((SIDE * HW, 512), BF),
-        attn_w=((256, 512), BF),
-    )
+    )
+    if paired():
+        outs.update(down_p=((LEN, 512), BF), out_p=((SIDE * HW, 512), BF), attn_p=((256, 512), BF))
     ins = dict(dm=dm, do=do, z=z, xr=xr, br=br, sr=sr, y=y, s3=s3, states=states, g=g, qr=qr, lse=lse, wc=wc, wcs=wcs)
-    ins.update(gain=gain, cos=cosine, sin=sine, hid=hid, wd=wd, x1=x1, dy=dy, m=m, o=o, dx=dx)
+    ins.update(gain=gain, cos=cosine, sin=sine, x1=x1, down=down, down_w=down_w, out_w=out_w, attn_w=attn_w)
     return launch(mixers_back, ins, outs, scratch, 10, dict(bias=bias, decay=decay, skip=skip))
 
 
-def dp_total(parts):
-    if lax.axis_size("dp") == 2:
-        peers = [lax.ppermute(p, "dp", ((0, 1), (1, 0))) for p in parts]
-        return [p.astype(F32) + q.astype(F32) for p, q in zip(parts, peers)]
-    return list(lax.psum(tuple(p.astype(F32) for p in parts), "dp"))
+def dp_total(own, theirs):
+    if theirs is not None:
+        return own.astype(F32) + theirs.astype(F32)
+    return lax.psum(own.astype(F32), "dp")
 
 
 def on_device(
@@ -1419,11 +1543,11 @@
     heads = (conv_input, p.wcs, step_bias, decay_log, skip_gain, ssm_row, cosine, sine)
     m = mixers_kernel(p.z, p.xr, p.br, p.sr, *heads, cotangent, wd)
     f = forward_kernel(m.m, m.o, block_input, ffn_row, wo, wt, wg, wu, m.dh)
-    b = backward_kernel(f.dgu, wg, wu, f.x1, f.s2, ffn_row, cotangent, f.n2_all, wo, wt)
-    gate_grad, up_grad = dp_total([b.gate_w, b.up_w])
+    b = backward_kernel(
+        f.dgu, wg, wu, f.x1, f.s2, ffn_row, cotangent, f.n2_all, wo, wt, f.hid, wd, m.dy, f.m_all, f.o_all
+    )
     mixed = (p.z, p.xr, p.br, p.sr, m.y, m.s3, m.states, m.g_o, m.qr, m.lse)
-    k = mixers_back_kernel(b.dm, b.do, *mixed, *heads, f.hid, wd, f.x1, m.dy, f.m_all, f.o_all, b.dx_all)
-    down_grad, out_grad, attn_grad = dp_total([k.down_w, k.out_w, k.attn_w])
+    k = mixers_back_kernel(b.dm, b.do, *mixed, *heads, f.x1, b.down, b.down_w, b.out_w, b.attn_w)
     q = project_back_kernel(
         k.da,
         k.db,
@@ -1442,33 +1566,34 @@
         k.dhead,
         k.dstates,
     )
-    pairs = ((q.zo, q.zq), (q.xo, q.xq), (q.bo, q.bq), (q.so, q.sq))
-    sums = [own.astype(F32) + their.astype(F32) for own, their in pairs]
-    total = q.total
-    if lax.axis_size("dp") != 2:
-        sums, total = lax.psum((sums, total), "dp")
-    z_grad, x_grad, b_grad, step_grad = sums
+    pair = paired()
+    gate_grad = dp_total(b.gate_w, b.gate_p if pair else None)
+    up_grad = dp_total(b.up_w, b.up_p if pair else None)
+    down_grad = dp_total(b.down_w, k.down_p if pair else None)
+    out_grad = dp_total(b.out_w, k.out_p if pair else None)
+    attn_grad = dp_total(b.attn_w, k.attn_p if pair else None)
+    z_grad = dp_total(q.zo, q.zq if pair else None)
+    x_grad = dp_total(q.xo, q.xq if pair else None)
+    b_grad = dp_total(q.bo, q.bq if pair else None)
+    step_grad = dp_total(q.so, q.sq if pair else None)
     step_grad = step_grad.reshape(SIDE, 16, -1)[:, :HH].reshape(SIDE * HH, -1).T
-    states_grad = lax.dynamic_slice(total, (24, lax.axis_index("col") * 32), (4, 32))
+    small = [q.o_mixer[0], q.o_conv, q.o_states, q.o_bias[0], q.o_decay[0], q.o_skip[0], q.o_gain[0], q.o_ffn[0]]
+    if not pair:
+        small = lax.psum(small, "dp")
     return (
         k.out,
         q.dx,
-        total[0],
+        small[0],
         z_grad,
         x_grad,
         b_grad[:, 0:128],
         step_grad,
         b_grad[:, 128:384],
         b_grad[:, 384:512],
-        total[8:12, 0:HW],
-        states_grad,
-        total[16 : 16 + HH, 0],
-        total[16 : 16 + HH, 1],
-        total[16 : 16 + HH, 2],
-        total[12, 0:HW],
+        *small[1:7],
         out_grad,
         attn_grad,
-        total[1],
+        small[7],
         jnp.stack([gate_grad, up_grad], axis=1),
         down_grad,
     )

time: 537 us -> 463 us (0.86)
  Pallas kernels: 484 us -> 417 us
  starting transfers between devices: 5.67 us -> 0 us
    pallas_call x6, Pallas kernels: 484 us -> 417 us  [launch(): pl.pallas_call(kernel, out_shape=[jax.ShapeDtypeStruct(*o) for o in outs....]
    unnamed x27 -> x55, local copies, waits for them, and re-layouts: 6.79 us -> 13.2 us
    ppermute x5 -> x0, starting transfers between devices: 5.67 us -> none  [dp_total(): peers = [lax.ppermute(p, 'dp', ((0, 1), (1, 0))) for p in parts]]
    slice x4 -> x0, local copies, waits for them, and re-layouts: 5.45 us -> none  [the longest x1 1.52 us: on_device(): total[16:16 + HH, 2]]
  transfers between devices with their start and end apart: 5 -> 0, of which waited for: 0 -> 0; matrix products, arithmetic and copies ran while one was open for 5% -> 0% of each run, Pallas kernels for 26% -> 0%
where the time goes in v2:
time: 463 us; the launch traced here: 455 us
  Pallas kernels  417 us (90%)
  local copies, waits for them, and re-layouts  24.5 us (5%)
  other arithmetic  12.3 us (3%)
    pallas_call x6, Pallas kernels, launch(): pl.pallas_call(kernel, out_shape=[jax.ShapeDtypeStruct(*o) for o in outs....  417 us
    unnamed x55, local copies, waits for them, and re-layouts  13.2 us
    add x7, other arithmetic, dp_total(): return own.astype(F32) + theirs.astype(F32)  11.1 us

profile of v2, /device:TPU:0, one launch (start us, length us, event | category | flops | bytes accessed | tf_op | source)
XLA Modules:
  0.0 454.7 jit_solution(1633808836392872526)
XLA Ops:
  0.7 0.7 reshape.52
  1.4 0.6 pad.4
  2.0 5.5 %fusion = (bf16[512,1,1024]{2,1,0:T(2,128)(2,1)S(1)}, bf16[512,1,1024]{2,1,0:T(2,128)(2,1)S(1)}) fusion(bf16[512,2,1024]{2,1,0:T(2,128)(2,1)} %param.39), kind=kLoop, calls=%fused_computation.12 | loop fusion | bytes 4194304 | tf_op jit(solution)/shard_map/slice | solution.py:1528
  7.6 2.1 copy_bitcast_fusion
  9.7 56.7 %project.1 = (bf16[1024,512]{1,0:T(8,128)(2,1)}, f32[8,256]{1,0:T(8,128)}, f32[1024,192]{1,0:T(8,128)}, f32[1024,192]{1,0:T(8,128)}, f32[288,512]{1,0:T(8,128)},...) custom-call(bf16[256,512]{1,0:T(8,128)(2,1)} %refs_6_.5, ...), custom_call_target="tpu_custom_call" | custom-call | tf_op jit(solution)/shard_map/project/pallas_call | solution.py:139
  66.4 56.0 %mixers.1 = (bf16[1024,192]{1,0:T(8,128)(2,1)}, bf16[256,256]{1,0:T(8,128)(2,1)}, f32[1024,192]{1,0:T(8,128)}, f32[8,256]{1,0:T(8,128)}, f32[2,256,128]{2,1,0:T(...) custom-call(f32[1024,192]{1,0:T(8,128)} %get-tuple-element.86.refs_0, ...), custom_call_target="tpu_custom_call" | custom-call | tf_op jit(solution)/shard_map/mixers/pallas_call | solution.py:139
  122.4 74.0 %forward.1 = (f32[256,512]{1,0:T(8,128)}, f32[8,256]{1,0:T(8,128)}, bf16[4,1024,192]{2,1,0:T(8,128)(2,1)}, bf16[4,256,256]{2,1,0:T(8,128)(2,1)}, bf16[1024,512]{...) custom-call(bf16[1024,192]{1,0:T(8,128)(2,1)} %get-tuple-element.91.refs_0_, ...), custom_call_target="tpu_custom_call" | custom-call | tf_op jit(solution)/shard_map/forward/pallas_call | solution.py:139
  196.4 88.7 %backward.1 = (bf16[512,1024]{1,0:T(8,128)(2,1)}, bf16[512,1024]{1,0:T(8,128)(2,1)}, f32[256,512]{1,0:T(8,128)}, f32[1,512]{1,0:T(1,128)}, f32[1024,192]{1,0:T(8...) custom-call(bf16[1024,512]{1,0:T(8,128)(2,1)} %get-tuple-element.94., ...), custom_call_target="tpu_custom_call" | custom-call | tf_op jit(solution)/shard_map/backward/pallas_call | solution.py:139
  285.1 65.3 %mixers_back.1 = (bf16[1024,384]{1,0:T(8,128)(2,1)}, bf16[256,512]{1,0:T(8,128)(2,1)}, bf16[16,1024]{1,0:T(8,128)(2,1)}, f32[1,192]{1,0:T(1,128)}, f32[4,192]{1,...) custom-call(f32[1024,192]{1,0:T(8,128)} %get-tuple-element.102.refs_, ...), custom_call_target="tpu_custom_call" | custom-call | tf_op jit(solution)/shard_map/mixers_back/pallas_call | solution.py:139
  350.4 2.0 convert_add_fusion.5
  352.4 2.5 convert_add_fusion.1
  354.9 1.6 convert_add_fusion
  356.5 76.1 %project_back.1 = (f32[256,512]{1,0:T(8,128)}, f32[1,512]{1,0:T(1,128)}, f32[1,512]{1,0:T(1,128)}, f32[4,192]{1,0:T(4,128)}, f32[1,192]{1,0:T(1,128)}, /*index=5...) custom-call(bf16[1024,384]{1,0:T(8,128)(2,1)} %get-tuple-element.115, ...), custom_call_target="tpu_custom_call" | custom-call | tf_op jit(solution)/shard_map/project_back/pallas_call | solution.py:139
  432.6 0.9 convert_add_fusion.6
  433.5 0.6 reshape.55
  434.2 1.5 convert_add_fusion.4
  435.6 0.8 slice.26
  436.5 0.8 fusion.1
  437.3 1.3 convert_add_fusion.3
  438.6 1.3 convert_add_fusion.2
  441.1 0.8 copy-done.3
  443.3 5.2 %copy.47 = f32[512,2,1024]{2,1,0:T(2,128)} copy(f32[512,2,1024]{2,0,1:T(8,128)S(1)} %pad_maximum_fusion) | data formatting | bytes 8388608
  448.5 0.7 copy.62
  449.2 0.8 copy.63
  (55 shorter events, 6.9 us)
Async XLA Ops:
  285.0 65.3 %copy-start.2 = (bf16[256,512]{1,0:T(8,128)(2,1)S(1)}, bf16[256,512]{1,0:T(8,128)(2,1)}, u32[]{:S(2)}) copy-start(bf16[256,512]{1,0:T(8,128)(2,1)} %get-tuple-element.113.refs_21_) | copy-start | bytes 786436
  285.0 67.3 %copy-start.1 = (bf16[768,512]{1,0:T(8,128)(2,1)S(1)}, bf16[768,512]{1,0:T(8,128)(2,1)}, u32[]{:S(2)}) copy-start(bf16[768,512]{1,0:T(8,128)(2,1)} %get-tuple-element.112.refs_20_) | copy-start | bytes 2359300
  350.4 4.5 copy-start
  350.4 4.5 copy-start.7
  434.2 3.1 copy-start.10
  434.2 3.1 copy-start.11
  436.5 2.1 copy-start.8
  436.5 2.1 copy-start.9
  438.6 1.6 copy-start.5
  438.6 2.1 copy-start.6
  440.7 1.2 copy-start.3
  440.7 1.5 copy-start.4
  443.2 5.4 %copy-start.13 = (bf16[256,512]{1,0:T(8,128)(2,1)S(1)}, bf16[256,512]{1,0:T(8,128)(2,1)}, u32[]{:S(2)}) copy-start(bf16[256,512]{1,0:T(8,128)(2,1)} %get-tuple-element.218) | copy-start | bytes 786436
  443.2 6.0 %copy-start.12 = (f32[256,512]{1,0:T(8,128)S(1)}, f32[256,512]{1,0:T(8,128)}, u32[]{:S(2)}) copy-start(f32[256,512]{1,0:T(8,128)} %get-tuple-element.219) | copy-start | bytes 1572868
  443.2 6.8 %copy-start.17 = (f32[1,512]{1,0:T(1,128)S(1)}, f32[1,512]{1,0:T(1,128)}, u32[]{:S(2)}) copy-start(f32[1,512]{1,0:T(1,128)} %get-tuple-element.129) | copy-start | bytes 6148
  443.2 7.4 %copy-start.14 = (f32[4,192]{1,0:T(4,128)S(1)}, f32[4,192]{1,0:T(4,128)}, u32[]{:S(2)}) copy-start(f32[4,192]{1,0:T(4,128)} %get-tuple-element.227) | copy-start | bytes 9220
  443.2 8.0 %copy-start.16 = (f32[4,32]{1,0:T(4,128)S(1)}, f32[4,32]{1,0:T(4,128)}, u32[]{:S(2)}) copy-start(f32[4,32]{1,0:T(4,128)} %get-tuple-element.228) | copy-start | bytes 1540
  443.2 8.6 %copy-start.21 = (f32[1,3]{1,0:T(1,128)S(1)}, f32[1,3]{1,0:T(1,128)}, u32[]{:S(2)}) copy-start(f32[1,3]{1,0:T(1,128)} %get-tuple-element.140) | copy-start | bytes 40
  443.2 9.1 %copy-start.20 = (f32[1,3]{1,0:T(1,128)S(1)}, f32[1,3]{1,0:T(1,128)}, u32[]{:S(2)}) copy-start(f32[1,3]{1,0:T(1,128)} %get-tuple-element.141) | copy-start | bytes 40
  443.2 9.6 %copy-start.19 = (f32[1,3]{1,0:T(1,128)S(1)}, f32[1,3]{1,0:T(1,128)}, u32[]{:S(2)}) copy-start(f32[1,3]{1,0:T(1,128)} %get-tuple-element.142) | copy-start | bytes 40
  443.3 10.1 %copy-start.18 = (f32[1,192]{1,0:T(1,128)S(1)}, f32[1,192]{1,0:T(1,128)}, u32[]{:S(2)}) copy-start(f32[1,192]{1,0:T(1,128)} %get-tuple-element.143) | copy-start | bytes 2308
  443.3 10.6 %copy-start.15 = (f32[1,512]{1,0:T(1,128)S(1)}, f32[1,512]{1,0:T(1,128)}, u32[]{:S(2)}) copy-start(f32[1,512]{1,0:T(1,128)} %get-tuple-element.146) | copy-start | bytes 6148

commit v3 on v2

--- a/solution.py
+++ b/solution.py
@@ -117,37 +117,68 @@
     return pltpu.SemaphoreType.DMA(shape)
 
 
-def launch(body, ins, outs, scratch, cid, smem=None):
-    smem = smem or {}
-    shapes = []
+def launch(body, ins, outs, scratch, cid, smem=None, late=None, early=None):
+    smem, late, early = smem or {}, late or {}, early or {}
+    shapes = [pltpu.VMEM(v.shape, v.dtype) for v in late.values()]
+    shapes += [dma(max(len(late), 1)), dma(max(len(early), 1))]
     for item in scratch.values():
         shapes += list(item.values()) if isinstance(item, dict) else [item]
 
     def kernel(*refs):
         refs = list(refs)
         found = {}
-        for key in (*ins, *smem, *outs):
+        for key in (*ins, *smem):
             found[key] = refs.pop(0)
+        sources = [refs.pop(0) for _ in late]
+        for key in (*outs, *early):
+            found[key] = refs.pop(0)
+        places = [refs.pop(0) for _ in late]
+        late_sems, early_sems = refs.pop(0), refs.pop(0)
+        incoming, outgoing = [], []
+        for k, (key, src, dst) in enumerate(zip(late, sources, places)):
+            found[key] = dst
+            incoming.append((dst, pltpu.make_async_copy(src, dst, late_sems.at[k])))
+            incoming[-1][1].start()
         for key, item in scratch.items():
             if isinstance(item, dict):
                 found[key] = types.SimpleNamespace(**{name: refs.pop(0) for name in item})
             else:
                 found[key] = refs.pop(0)
-        body(types.SimpleNamespace(**found))
+
+        def arrive(*wanted):
+            for one in wanted:
+                for k, (dst, copy) in enumerate(incoming):
+                    if dst is one:
+                        copy.wait()
+                        del incoming[k]
+                        break
+
+        def leave(dst, src):
+            outgoing.append(pltpu.make_async_copy(src, dst, early_sems.at[len(outgoing)]))
+            outgoing[-1].start()
+
+        body(types.SimpleNamespace(arrive=arrive, leave=leave, **found))
+        for _, copy in incoming:
+            copy.wait()
+        for copy in outgoing:
+            copy.wait()
 
     vector = pl.BlockSpec(memory_space=pltpu.VMEM)
+    anywhere = pl.BlockSpec(memory_space=pl.ANY)
     results = pl.pallas_call(
         kernel,
-        out_shape=[jax.ShapeDtypeStruct(*o) for o in outs.values()],
-        in_specs=[vector] * len(ins) + [pl.BlockSpec(memory_space=pltpu.SMEM)] * len(smem),
-        out_specs=[vector] * len(outs),
+        out_shape=[jax.ShapeDtypeStruct(*o) for o in (*outs.values(), *early.values())],
+        in_specs=[vector] * len(ins)
+        + [pl.BlockSpec(memory_space=pltpu.SMEM)] * len(smem)
+        + [anywhere] * len(late),
+        out_specs=[vector] * len(outs) + [anywhere] * len(early),
         scratch_shapes=shapes,
         compiler_params=pltpu.CompilerParams(
             collective_id=cid, has_side_effects=True, vmem_limit_bytes=58 << 20
         ),
         name=body.__name__,
-    )(*ins.values(), *smem.values())
-    return types.SimpleNamespace(**dict(zip(outs, results)))
+    )(*ins.values(), *smem.values(), *late.values())
+    return types.SimpleNamespace(**dict(zip((*outs, *early), results)))
 
 
 def rows_scratch(padded=False):
@@ -186,7 +217,7 @@
     part = rows_at(S.g, flip(r, d), pad)
     hop(part, part, S.zs.at[d - 1], S.zr.at[d - 1], row=flip(r, d)).wait_recv()
 
-    @pl.when((d == 2) & inner(r))
+    @pl.when(jnp.logical_and(d == 2, inner(r)))
     def _():
         pass_hop(S, r, pad).start()
 
@@ -216,7 +247,7 @@
     )
 
 
-def scatter_cols(S, G, r, c, product, finish, pad=0):
+def scatter_cols(S, G, r, c, product, finish, pad=0, moving=True):
     cs, cr, xs, xr, acc = (S.cs, S.cr, S.xs, S.xr, S.acc)
 
     def core_hop(d):
@@ -228,9 +259,11 @@
     def first(i):
         d = swapped(i)
 
-        @pl.when(i > 0)
-        def _():
-            wait_rows(G, r, d, pad)
+        if moving:
+
+            @pl.when(i > 0)
+            def _():
+                wait_rows(G, r, d, pad)
 
         rows = rows_at(G.g, flip(r, d), pad)[...]
         cs[d, 1] = product(rows, flip(c, 3))
@@ -246,18 +279,25 @@
         x_hop(d).start()
         acc[d] = acc[d] + cr[d, 0]
 
-    def end(i, carry):
+    def end(i):
         d = swapped(i)
         x_hop(d).wait_recv()
         finish(flip(r, d), acc[d] + xr[d].astype(F32))
-        x_hop(d).wait_send()
-        core_hop(d).wait_send()
-        return carry
+
+    def sent(i):
+        x_hop(swapped(i)).wait_send()
+        core_hop(swapped(i)).wait_send()
+
+    def before(i):
+        @pl.when(i > 0)
+        def _():
+            end(i - 1)
 
     def close():
-        lax.fori_loop(0, SIDE, end, 0)
-
-    return first, second, close
+        end(SIDE - 1)
+        each(sent)
+
+    return first, second, before, close
 
 
 def each(*phases):
@@ -444,9 +484,11 @@
     return found
 
 
-def pair_hop(S, k, own=None):
+def pair_hop(S, k, own=None, rows=None):
     src = getattr(S, LETTERS[k]) if own is None else own
     dst = getattr(S, LETTERS[k].upper())
+    if rows is not None:
+        src, dst = src.at[rows], dst.at[rows]
     return hop(src, dst, S.ss.at[k], S.sr.at[k], dp=1 - lax.axis_index("dp"))
 
 
@@ -532,7 +574,7 @@
     return v[:, j * w : (j + 1) * w]
 
 
-def project_kernel(x, gain, wz, wx, wbc, wq, wkv, ws, cw):
+def project_kernel(x, gain, wz, wx, wbc, wq, wkv, ws, cw, cot):
     def project(R):
         r, c = here()
         greet(r, c, rows=True, cols=(1, 2, 3))
@@ -552,20 +594,27 @@
         rows_at(g, r, HALO)[...] = (x * scale * R.gain[...]).astype(BF)
         gather_rows(R.p, r, HALO)
         wa, wb = R.wa, R.wb
+        R.arrive(R.wz, R.wx, R.wbc, R.wq, R.wkv)
         for j in range(SIDE):
             wa[j, :, 0:HW] = cut(R.wz, j, HW)
             wa[j, :, HW : 2 * HW] = cut(R.wx, j, HW)
         wb[:, 0:128] = R.wbc[...]
         wb[:, 128:384] = R.wq[...]
         wb[:, 384:512] = R.wkv[...]
+        R.leave(R.wb_o, wb)
 
         def finish(block, v):
             at = pl.ds(pl.multiple_of(block * BLK, BLK), BLK)
-            R.z[at] = v[:, 0:HW]
-            R.xr[at] = v[:, HW : 2 * HW]
-
-        first, second, close_a = scatter_cols(R.a, R.p, r, c, lambda rows, j: dot_nn(rows, wa[j]), finish, HALO)
-        each(first, second)
+            R.zs[at] = v[:, 0:HW]
+            R.xs[at] = v[:, HW : 2 * HW]
+
+        first, second, before, close_a = scatter_cols(R.a, R.p, r, c, lambda rows, j: dot_nn(rows, wa[j]), finish, HALO)
+        each(first, second, before)
+        R.leave(R.n1, g.at[pl.ds(HALO, LEN)])
+        R.arrive(R.cot)
+        rows_at(R.h.g, r)[...] = R.cot[...].astype(BF)
+        gather_rows(R.h, r)
+        R.arrive(R.ws)
         steps = dot_nt(R.ws[...], g[pl.ds(HALO, LEN)])
         for j in range(SIDE):
             R.ps[j] = steps[16 * j : 16 * j + 8]
@@ -586,11 +635,11 @@
             return dot_nn(g[pl.ds(pl.multiple_of(j * BLK, BLK), BLK + 2 * HALO)], wb[...])
 
         close_b = scatter_tokens(R.b, c, token_rows)
-        R.n1[...] = g[pl.ds(HALO, LEN)]
         R.s1[...] = total
-        R.wa_o[...] = wa[...]
-        R.wb_o[...] = wb[...]
+        wait_rows(R.h, r, 2)
         close_a()
+        R.leave(R.z, R.zs)
+        R.leave(R.xr, R.xs)
         for one in step_hops:
             one.wait_recv()
         R.sr[...] = (R.ps[c] + R.pr[0]) + (R.pr[1] + R.pr[2])
@@ -602,11 +651,16 @@
         R.wcs[...] = jnp.concatenate([R.taps[j, 0:4, 0:32] for j in range(SIDE)], axis=1)
         for one in tap_hops:
             one.wait_send()
+        wait_rows(R.h, r, 1)
+        wait_rows(R.h, r, 3)
+        R.leave(R.dy, R.h.g)
         wait_rows_sent(R.p, r, HALO)
+        wait_rows_sent(R.h, r)
 
     n = BLK + 2 * HALO
     scratch = dict(
         p=rows_scratch(True),
+        h=rows_scratch(),
         n=stat_scratch(),
         a=cols_scratch(2 * HW),
         b=tokens_scratch(n, 512),
@@ -617,22 +671,22 @@
         pss=dma(3),
         psr=dma(3),
         taps=pltpu.VMEM((SIDE, 8, 128), F32),
+        zs=pltpu.VMEM((LEN, HW), F32),
+        xs=pltpu.VMEM((LEN, HW), F32),
         tss=dma(3),
         tsr=dma(3),
     )
-    outs = dict(
+    outs = dict(s1=((8, BLK), F32), br=((n, 512), F32), sr=((8, LEN), F32), wcs=((4, 128), F32))
+    early = dict(
         n1=((LEN, 512), BF),
-        s1=((8, BLK), F32),
         z=((LEN, HW), F32),
         xr=((LEN, HW), F32),
-        br=((n, 512), F32),
-        sr=((8, LEN), F32),
-        wa_o=((SIDE, 512, 2 * HW), BF),
+        dy=((LEN, 512), BF),
         wb_o=((512, 512), BF),
-        wcs=((4, 128), F32),
-    )
-    ins = dict(x=x, gain=gain, wz=wz, wx=wx, wbc=wbc, wq=wq, wkv=wkv, ws=ws, cw=cw)
-    return launch(project, ins, outs, scratch, 1)
+    )
+    ins = dict(x=x, gain=gain, cw=cw)
+    late = dict(wz=wz, wx=wx, wbc=wbc, wq=wq, wkv=wkv, ws=ws, cot=cot)
+    return launch(project, ins, outs, scratch, 1, late=late, early=early)
 
 
 SMALL = 32
@@ -649,6 +703,7 @@
         o_hops[0].start()
         o_hops[1].start()
         gather_cols(R.mc, r, c)
+        R.arrive(R.wo, R.wt)
         trio_end(o_hops)
 
         def product(t):
@@ -659,8 +714,9 @@
 
         step, close = scatter_rows(R.s, r, product, lambda d: wait_cols(R.mc, r, c, d))
         each(step)
-        R.m_all[...] = R.mc.g[...]
-        R.o_all[...] = og[...]
+        R.leave(R.m_all, R.mc.g)
+        R.leave(R.o_all, og)
+        R.arrive(R.x, R.wg, R.wu, R.dh)
         x1 = R.x[...].astype(F32) + close()
         R.x1[...] = x1
         total = col_sum(R.n, c, row_sums(x1 * x1))
@@ -683,9 +739,9 @@
             R.dgu[at, 0:256] = (dh * up * sig * (1.0 + gate * (1.0 - sig))).astype(BF)
             R.dgu[at, 256:512] = (dh * act).astype(BF)
 
-        first, second, close = scatter_cols(R.a, R.p, r, c, gate_up, finish)
-        each(first, second)
-        R.n2_all[...] = R.p.g[...]
+        first, second, before, close = scatter_cols(R.a, R.p, r, c, gate_up, finish)
+        each(first, second, before)
+        R.leave(R.n2_all, R.p.g)
         close()
         for one in o_hops:
             one.wait_send()
@@ -701,16 +757,10 @@
         p=rows_scratch(),
         a=cols_scratch(512),
     )
-    outs = dict(
-        x1=((BLK, 512), F32),
-        s2=((8, BLK), F32),
-        m_all=((SIDE, LEN, HW), BF),
-        o_all=((SIDE, BLK, 256), BF),
-        n2_all=((LEN, 512), BF),
-        hid=((LEN, 256), BF),
-        dgu=((LEN, 512), BF),
-    )
-    return launch(forward, dict(m=m, o=o, x=x, gain=gain, wo=wo, wt=wt, wg=wg, wu=wu, dh=dh), outs, scratch, 3)
+    outs = dict(x1=((BLK, 512), F32), s2=((8, BLK), F32), hid=((LEN, 256), BF), dgu=((LEN, 512), BF))
+    early = dict(m_all=((SIDE, LEN, HW), BF), o_all=((SIDE, BLK, 256), BF), n2_all=((LEN, 512), BF))
+    late = dict(wo=wo, wt=wt, x=x, wg=wg, wu=wu, dh=dh)
+    return launch(forward, dict(m=m, o=o, gain=gain), outs, scratch, 3, late=late, early=early)
 
 
 def norm_back(S, c, dn, v, scale, gain):
@@ -726,19 +776,20 @@
         r, c = here()
         greet(r, c, rows=True, cols=(1, 2, 3), dp=paired())
         R.gc.g[c] = R.dgu[...]
-        R.hc.g[c] = R.hid[...]
         gather_cols(R.gc, r, c)
+        R.arrive(R.wg, R.wu)
+        for j in range(SIDE):
+            R.wgu[:, 512 * j : 512 * j + 256] = R.wg[:, 256 * j : 256 * j + 256]
+            R.wgu[:, 512 * j + 256 : 512 * j + 512] = R.wu[:, 256 * j : 256 * j + 256]
 
         def product(t):
-            total = jnp.zeros((BLK, 512), F32)
-            for j in range(SIDE):
-                part = col_part(R.gc, j, t)[...]
-                total = total + dot_nt(part[:, :256], R.wg[:, 256 * j : 256 * j + 256])
-                total = total + dot_nt(part[:, 256:], R.wu[:, 256 * j : 256 * j + 256])
-            return total
+            parts = [col_part(R.gc, j, t)[...] for j in range(SIDE)]
+            return dot_nt(jnp.concatenate(parts, axis=1), R.wgu[...])
 
         step, close = scatter_rows(R.s, r, product, lambda d: wait_cols(R.gc, r, c, d))
         each(step)
+        R.arrive(R.hid, R.n2)
+        R.hc.g[c] = R.hid[...]
         gather_cols(R.hc, r, c)
 
         def grads(j):
@@ -748,11 +799,14 @@
             R.y.b[:, at] = both[:, 256:].astype(BF)
 
         each(grads)
-        y_hops = [pair_hop(R.y, k) for k in range(2)] if paired() else []
+        y_hops = []
+        if paired():
+            y_hops = [pair_hop(R.y, 0), pair_hop(R.y, 1, R.y.b.at[pl.ds(0, 256)])]
         for one in y_hops:
             one.start()
-        R.gate_w[...] = R.y.a[...]
-        R.up_w[...] = R.y.b[...]
+        R.leave(R.gate_w, R.y.a)
+        R.leave(R.up_w, R.y.b)
+        R.arrive(R.x1, R.cot)
         dn = close()
         scale = to_column(lax.rsqrt(R.s2[...] / D + EPSILON))
         dv, dgain = norm_back(R.n, c, dn, R.x1[...], scale, R.gain[...])
@@ -762,20 +816,25 @@
         R.dx1[...] = dx1
         R.dgain[...] = dgain
 
+        R.arrive(R.wd, R.dy)
+
         def down(i):
             wait_cols(R.hc, r, c, 3 - swapped(i))
             t = flip(r, 3 - swapped(i))
             total = dot_nn(col_part(R.hc, 0, t)[...], R.wd[0:256])
             for j in (1, 2, 3):
                 total = total + dot_nn(col_part(R.hc, j, t)[...], R.wd[256 * j : 256 * j + 256])
-            R.down[t] = total
+            R.down_s[t] = total
 
         each(down)
 
         def down_grads(j):
-            R.down_w[pl.ds(pl.multiple_of(j * BLK, BLK), BLK)] = dot_tn(R.hc.g[j], R.dy[...]).astype(BF)
+            R.down_ws[pl.ds(pl.multiple_of(j * BLK, BLK), BLK)] = dot_tn(R.hc.g[j], R.dy[...]).astype(BF)
 
         each(down_grads)
+        R.leave(R.down, R.down_s)
+        R.leave(R.down_w, R.down_ws)
+        R.arrive(R.wo, R.wt)
 
         def out_back(rows, j):
             return dot_nt(rows, R.wo[pl.ds(pl.multiple_of(j * HW, 64), HW)])
@@ -783,14 +842,17 @@
         def finish(block, v):
             R.dm[pl.ds(pl.multiple_of(block * BLK, BLK), BLK)] = v
 
-        first, second, close_a = scatter_cols(R.a, R.p, r, c, out_back, finish)
-        each(first, second)
+        first, second, before, close_a = scatter_cols(R.a, R.p, r, c, out_back, finish)
+        each(first, second, before)
         close_b = scatter_tokens(R.b, c, lambda j: dot_nt(rows_at(R.p.g, j)[...], R.wt[...]))
 
+        R.arrive(R.m, R.o)
+
         def out_grads(j):
-            R.out_w[pl.ds(pl.multiple_of(j * HW, 64), HW)] = dot_tn(R.m[j], R.p.g[...]).astype(BF)
+            R.out_ws[pl.ds(pl.multiple_of(j * HW, 64), HW)] = dot_tn(R.m[j], R.p.g[...]).astype(BF)
 
         each(out_grads)
+        R.leave(R.out_w, R.out_ws)
         R.attn_w[...] = dot_tn(R.o[...].reshape(LEN, 256), R.p.g[...]).astype(BF)
         close_a()
         R.do[...] = close_b().astype(BF)
@@ -799,7 +861,7 @@
         wait_rows_sent(R.p, r)
         for one, theirs, out in zip(y_hops, (R.y.A, R.y.B), (R.gate_p, R.up_p) if y_hops else ()):
             one.wait_recv()
-            out[...] = theirs[...]
+            R.leave(out, theirs)
             one.wait_send()
 
     scratch = dict(
@@ -810,28 +872,35 @@
         p=rows_scratch(),
         a=cols_scratch(HW),
         b=tokens_scratch(BLK, 256, low=BF),
-        y=pair_scratch((512, 1024), (512, 1024)),
+        y=dict(pair_scratch((512, 1024), (256, 1024)), b=pltpu.VMEM((512, 1024), BF)),
+        wgu=pltpu.VMEM((512, 2048), BF),
+        down_s=pltpu.VMEM((SIDE, BLK, 512), F32),
+        down_ws=pltpu.VMEM((LEN, 512), BF),
+        out_ws=pltpu.VMEM((SIDE * HW, 512), BF),
     )
     outs = dict(
-        gate_w=((512, 1024), BF),
-        up_w=((512, 1024), BF),
         dx1=((BLK, 512), F32),
         dgain=((1, 512), F32),
         dm=((LEN, HW), F32),
         do=((BLK, 256), BF),
+        attn_w=((256, 512), BF),
+    )
+    early = dict(
+        gate_w=((512, 1024), BF),
+        up_w=((512, 1024), BF),
         down=((SIDE, BLK, 512), F32),
         down_w=((LEN, 512), BF),
         out_w=((SIDE * HW, 512), BF),
-        attn_w=((256, 512), BF),
     )
     if paired():
-        outs.update(gate_p=((512, 1024), BF), up_p=((512, 1024), BF))
-    ins = dict(dgu=dgu, wg=wg, wu=wu, x1=x1, s2=s2, gain=gain, cot=cot, n2=n2, wo=wo, wt=wt)
-    ins.update(hid=hid, wd=wd, dy=dy, m=m, o=o)
-    return launch(backward, ins, outs, scratch, 6)
-
-
-def project_back_kernel(da, db, ds, wa, wb, ws, x, s1, gain, dx1, n1, ffn_grad, dconv, dgain, dhead, dstates):
+        early.update(gate_p=((512, 1024), BF), up_p=((256, 1024), BF))
+    late = dict(wg=wg, wu=wu, hid=hid, n2=n2, x1=x1, cot=cot, wd=wd, dy=dy, wo=wo, wt=wt, m=m, o=o)
+    return launch(backward, dict(dgu=dgu, s2=s2, gain=gain), outs, scratch, 6, late=late, early=early)
+
+
+def project_back_kernel(
+    da, db, ds, wz, wx, wb, ws, x, s1, gain, dx1, n1, ffn_grad, dconv, dgain, dhead, dstates, dz, z_w
+):
     pair = paired()
 
     def project_back(R):
@@ -856,34 +925,38 @@
         gather_cols(R.ac, r, c)
 
         y = R.y
-        w_hops = [pair_hop(y, k) for k in range(4)] if pair else []
+        w_hops = []
+        if pair:
+            w_hops = [pair_hop(y, 0, R.z_w), *(pair_hop(y, k) for k in (1, 2, 3))]
+            R.arrive(R.z_w)
+            w_hops[0].start()
 
         trio_end(b_hops)
         for one in s_hops:
             one.wait_recv()
-        y.a[...] = dot_tn(R.n1[...], bg[...].reshape(LEN, 512)).astype(BF)
-        y.b[...] = dot_nn(sg[...].reshape(16 * SIDE, LEN), R.n1[...]).astype(BF)
+        R.arrive(R.n1, R.wb, R.wx, R.wz, R.ws, R.dz)
+        y.b[...] = dot_tn(R.n1[...], bg[...].reshape(LEN, 512)).astype(BF)
+        y.c[...] = dot_nn(sg[...].reshape(16 * SIDE, LEN), R.n1[...]).astype(BF)
         if pair:
-            w_hops[0].start()
             w_hops[1].start()
+            w_hops[2].start()
 
         def product(t):
-            total = dot_nt(bg[t], R.wb[...])
             at = pl.ds(pl.multiple_of(t * BLK, BLK), BLK)
-            for j in range(SIDE):
-                total = total + dot_nt(col_part(R.ac, j, t)[...], R.wa[j])
-                total = total + dot_tn(sg[j, :, at], R.ws[16 * j : 16 * j + 16])
-            return total
+            total = dot_nt(bg[t], R.wb[...]) + dot_nt(R.dz[at], R.wz[...])
+            total = total + dot_tn(sg[:, :, at].reshape(16 * SIDE, BLK), R.ws[...])
+            joined = jnp.concatenate([col_part(R.ac, j, t)[...] for j in range(SIDE)], axis=1)
+            R.dx_all[at] = joined
+            return total + dot_nt(joined, R.wx[...])
 
         step, close = scatter_rows(R.s, r, product, lambda d: wait_cols(R.ac, r, c, d))
         each(step)
-        for j in range(SIDE):
-            both = dot_tn(R.n1[...], R.ac.g[j]).astype(BF)
-            y.c[:, j * HW : (j + 1) * HW] = both[:, :HW]
-            y.d[:, j * HW : (j + 1) * HW] = both[:, HW:]
+        y.d[...] = dot_tn(R.n1[...], R.dx_all[...]).astype(BF)
         if pair:
-            w_hops[2].start()
             w_hops[3].start()
+        for out, own in zip((R.bo, R.so, R.xo), (y.b, y.c, y.d)):
+            R.leave(out, own)
+        R.arrive(R.x, R.dx1)
         dn = close()
         scale = to_column(lax.rsqrt(R.s1[...] / D + EPSILON))
         dv, mixer_grad = norm_back(R.n, c, dn, R.x[...].astype(F32), scale, R.gain[...])
@@ -927,16 +1000,15 @@
         for j in range(SIDE):
             taps = taps + jnp.where(c == j, total[24:28, 32 * j : 32 * j + 32], 0.0)
         R.o_states[...] = taps
-        for own, out in zip((y.a, y.b, y.c, y.d), (R.bo, R.so, R.zo, R.xo)):
-            out[...] = own[...]
         if pair:
-            for one, theirs, out in zip(w_hops, (y.A, y.B, y.C, y.D), (R.bq, R.sq, R.zq, R.xq)):
+            for one, theirs, out in zip(w_hops, (y.A, y.B, y.C, y.D), (R.zq, R.bq, R.sq, R.xq)):
                 one.wait_recv()
-                out[...] = theirs[...]
+                R.leave(out, theirs)
                 one.wait_send()
 
     scratch = dict(
-        ac=gcols_scratch(2 * HW),
+        ac=gcols_scratch(HW),
+        dx_all=pltpu.VMEM((LEN, 768), BF),
         s=srows_scratch(),
         n=stat_scratch(),
         bt=trio_scratch(),
@@ -950,7 +1022,7 @@
         gg=pltpu.VMEM((SIDE, 8, 512), F32),
         ggs=dma(3),
         ggr=dma(3),
-        y=pair_scratch((512, 512), (16 * SIDE, 512), (512, 768), (512, 768)),
+        y=pair_scratch((512, 768), (512, 512), (16 * SIDE, 512), (512, 768)),
         small=pltpu.VMEM((SMALL, 512), F32),
         small_p=pltpu.VMEM((SMALL, 512), F32),
         mss=dma(),
@@ -966,16 +1038,19 @@
         o_decay=((1, HH), F32),
         o_skip=((1, HH), F32),
         o_states=((4, 32), F32),
+    )
+    early = dict(
         bo=((512, 512), BF),
         so=((16 * SIDE, 512), BF),
-        zo=((512, 768), BF),
         xo=((512, 768), BF),
     )
     if pair:
-        outs.update(bq=((512, 512), BF), sq=((16 * SIDE, 512), BF), zq=((512, 768), BF), xq=((512, 768), BF))
-    ins = dict(da=da, db=db, ds=ds, wa=wa, wb=wb, ws=ws, x=x, s1=s1, gain=gain, dx1=dx1, n1=n1)
+        early.update(zq=((512, 768), BF), bq=((512, 512), BF))
+        early.update(sq=((16 * SIDE, 512), BF), xq=((512, 768), BF))
+    ins = dict(da=da, db=db, ds=ds, s1=s1, gain=gain)
     ins.update(ffn_grad=ffn_grad, dconv=dconv, dgain=dgain, dhead=dhead, dstates=dstates)
-    return launch(project_back, ins, outs, scratch, 8)
+    late = dict(z_w=z_w, n1=n1, wb=wb, wx=wx, wz=wz, ws=ws, dz=dz, x=x, dx1=dx1)
+    return launch(project_back, ins, outs, scratch, 8, late=late, early=early)
 
 
 def per_head(values):
@@ -997,19 +1072,30 @@
     return jnp.where(iota((BLK, BLK), 0) <= iota((BLK, BLK), 1), 1.0, 0.0).astype(F32)
 
 
+def silu_pair(v):
+    sig = sigmoid(v)
+    return v * sig, sig * (1.0 + v * (1.0 - sig))
+
+
 def fill_padded(R):
     R.xpad[0:8] = jnp.zeros((8, HW), F32)
     R.xpad[8 : 8 + LEN] = R.xr[...]
 
 
-def conv_block(R, b):
-    start = pl.multiple_of(b * BLK, BLK)
-    chunk = R.xpad[pl.ds(start, BLK + 8)]
-    taps = [chunk[5 + j : 5 + j + BLK] for j in range(4)]
-    pre = taps[0] * R.wc[0:1]
-    for j in (1, 2, 3):
-        pre = pre + taps[j] * R.wc[j : j + 1]
-    return pre, taps
+def prepare(R):
+    fill_padded(R)
+    for b in range(SIDE):
+        at = pl.ds(b * BLK, BLK)
+        pre = R.xpad[5 + b * BLK : 5 + (b + 1) * BLK] * R.wc[0:1]
+        for j in (1, 2, 3):
+            pre = pre + R.xpad[5 + j + b * BLK : 5 + j + (b + 1) * BLK] * R.wc[j : j + 1]
+        R.u_[at], R.du_[at] = silu_pair(pre)
+        R.za_[at], R.dza_[at] = silu_pair(R.z[at])
+        _, _, _, within, dt_c, within_c = step_block(R, b)
+        R.xdt[at] = R.u_[at] * column_heads(dt_c)
+        R.wr[b] = within
+        R.wide[at] = column_heads(within_c)
+        R.wcol[b] = within_c
 
 
 def step_block(R, b):
@@ -1064,7 +1150,7 @@
     return per_head([cols[:, h : h + 1] for h in range(HH)])
 
 
-def mixers_kernel(z, xr, br, sr, wc, wcs, bias, decay, skip, gain, cosine, sine, cot, wd):
+def mixers_kernel(z, xr, br, sr, wc, wcs, bias, decay, skip, gain, cosine, sine, dy, wd):
     def mixers(R):
         r, c = here()
         greet(r, c, grid=True)
@@ -1100,9 +1186,18 @@
             def _():
                 kv_hop(d).start()
 
-        rows_at(R.p.g, r)[...] = R.cot[...].astype(BF)
-        gather_rows(R.p, r)
-        fill_padded(R)
+        R.arrive(R.wd, R.dy)
+
+        def hidden_back(rows, j):
+            return dot_nt(rows, R.wd[pl.ds(pl.multiple_of(j * BLK, BLK), BLK)])
+
+        def finish(block, v):
+            R.dh[pl.ds(pl.multiple_of(block * BLK, BLK), BLK)] = v
+
+        first, second, before, close_h = scatter_cols(
+            R.a, types.SimpleNamespace(g=R.dy), r, c, hidden_back, finish, moving=False
+        )
+        each(first)
         for d in (1, 2, 3):
             bc_hop(d).wait_recv()
 
@@ -1116,6 +1211,11 @@
         for h in range(2):
             q = br[HALO : HALO + BLK, 128 + 128 * h : 256 + 128 * h].astype(BF).astype(F32)
             R.qr[h] = rope_turn(q, cos, sin).astype(BF)
+        each(second)
+        R.arrive(R.xr, R.z, R.sr)
+        prepare(R)
+        for out, own in zip((R.u, R.du, R.za, R.dza), (R.u_, R.du_, R.za_, R.dza_)):
+            R.leave(out, own)
         trio_end(g_hops)
 
         state = R.state
@@ -1124,44 +1224,35 @@
         st[r, c] = jnp.zeros((8, BLK), F32)
         skip_row = per_head([R.skip[h] for h in range(HH)])
 
-        def hidden_back(rows, j):
-            return dot_nt(rows, R.wd[pl.ds(pl.multiple_of(j * BLK, BLK), BLK)])
-
-        def finish(block, v):
-            R.dh[pl.ds(pl.multiple_of(block * BLK, BLK), BLK)] = v
-
-        first, second, close_h = scatter_cols(R.a, R.p, r, c, hidden_back, finish)
-
         def block(b, carry):
-            first(b)
             at = pl.ds(pl.multiple_of(b * BLK, BLK), BLK)
-            pre, _ = conv_block(R, b)
-            u = pre * sigmoid(pre)
-            _, _, _, within, dt_c, within_c = step_block(R, b)
+            within, within_c, wide = R.wr[b], R.wcol[b], R.wide[at]
             bb, cb = state_cols(R, 0, b), state_cols(R, 1, b)
-            x = u * column_heads(dt_c)
+            x = R.xdt[at]
             xb = halves(x)
             scores = dot_nt(cb, bb)
-            y = jnp.exp(column_heads(within_c)) * fine(dot_nn, cb, halves(state[...]))
+            y = jnp.exp(wide) * fine(dot_nn, cb, halves(state[...]))
             for h in range(HH):
                 a = halves(scores * lower_decay(within_c, within, h))
                 y = y + fine(dot_nn, a, head_masks(xb, h))
             last = per_head([within[h : h + 1, BLK - 1 : BLK] for h in range(HH)])
-            keep = jnp.exp(last - column_heads(within_c))
-            R.states[b] = state[...]
+            keep = jnp.exp(last - wide)
+            R.states_[b] = state[...]
             state[...] = state[...] * jnp.exp(last) + fine(dot_tn, bb, halves(x * keep))
-            y = y + skip_row * u
-            zb = R.z[at]
-            gated = y * zb * sigmoid(zb)
-            R.y[at] = y
+            y = y + skip_row * R.u_[at]
+            gated = y * R.za_[at]
+            R.ys_[at] = y
             R.gs[at] = gated
             sums = row_sums(gated * gated)
             st[r, c] = jnp.where(iota((8, BLK), 0) == b, sums, st[r, c])
-            second(b)
+            before(b)
             return carry
 
         lax.fori_loop(0, SIDE, block, 0)
         close = grid_sum(R.n, r, c)
+        R.leave(R.g_o, g)
+        R.leave(R.y, R.ys_)
+        R.leave(R.states, R.states_)
 
         keys = g[4].reshape(LEN, ADIM)
         values = g[5].reshape(LEN, ADIM)
@@ -1183,10 +1274,7 @@
             return carry
 
         lax.fori_loop(0, SIDE, scaled, 0)
-        R.g_o[...] = g[...]
-        R.dy[...] = R.p.g[...]
         close_h()
-        wait_rows_sent(R.p, r)
         for d in (1, 2, 3):
             bc_hop(d).wait_send()
 
@@ -1199,11 +1287,13 @@
 
     scratch = dict(
         n=grid_scratch(),
-        p=rows_scratch(),
         a=cols_scratch(256),
         g=pltpu.VMEM((6, SIDE, BLK, 128), BF),
         kvb=pltpu.VMEM((BLK, 128), BF),
         xpad=pltpu.VMEM((LEN + 8, HW), F32),
+        wr=pltpu.VMEM((SIDE, 8, BLK), F32),
+        wcol=pltpu.VMEM((SIDE, BLK, 8), F32),
+        **{key: pltpu.VMEM((LEN, HW), F32) for key in ("u_", "du_", "za_", "dza_", "xdt", "wide")},
         gs=pltpu.VMEM((LEN, HW), F32),
         state=pltpu.VMEM((STATE, HW), F32),
         zs=dma(3),
@@ -1211,25 +1301,34 @@
         ys=dma(3),
         yr=dma(3),
         gt=trio_scratch(),
+        ys_=pltpu.VMEM((LEN, HW), F32),
+        states_=pltpu.VMEM((SIDE, STATE, HW), F32),
     )
     outs = dict(
         m=((LEN, HW), BF),
         o=((BLK, 256), BF),
-        y=((LEN, HW), F32),
         s3=((8, BLK), F32),
         lse=((2, BLK, 128), F32),
+        qr=((2, BLK, 128), BF),
+        dh=((LEN, 256), F32),
+    )
+    early = dict(
+        y=((LEN, HW), F32),
+        u=((LEN, HW), F32),
+        du=((LEN, HW), F32),
+        za=((LEN, HW), F32),
+        dza=((LEN, HW), F32),
         states=((SIDE, STATE, HW), F32),
         g_o=((6, SIDE, BLK, 128), BF),
-        qr=((2, BLK, 128), BF),
-        dy=((LEN, 512), BF),
-        dh=((LEN, 256), F32),
-    )
-    ins = dict(z=z, xr=xr, br=br, sr=sr, wc=wc, wcs=wcs, gain=gain, cos=cosine, sin=sine, cot=cot, wd=wd)
-    return launch(mixers, ins, outs, scratch, 9, dict(bias=bias, decay=decay, skip=skip))
+    )
+    ins = dict(br=br, wc=wc, wcs=wcs, gain=gain, cos=cosine, sin=sine)
+    late = dict(xr=xr, z=z, sr=sr, wd=wd, dy=dy)
+    smem = dict(bias=bias, decay=decay, skip=skip)
+    return launch(mixers, ins, outs, scratch, 9, smem, late, early)
 
 
 def mixers_back_kernel(
-    dm, do, z, xr, br, sr, y, s3, states, g, qr, lse, wc, wcs, bias, decay, skip, gain, cosine, sine, x1, down, down_w, out_w, attn_w
+    dm, do, u, du, za, dza, xr, br, sr, y, s3, states, g, qr, lse, wc, wcs, bias, decay, skip, gain, cosine, sine, x1, down, down_w, attn_w, up_w, n1, out_w
 ):
     n = BLK + HALO
 
@@ -1238,27 +1337,33 @@
         greet(r, c, grid=True, dp=paired())
         y_hops = []
         if paired():
-            y_hops = [pair_hop(R.yy, k, own) for k, own in enumerate((R.down_w, R.out_w, R.attn_w))]
+            y_hops = [
+                pair_hop(R.yy, 0, R.up_w.at[pl.ds(256, 256)]),
+                pair_hop(R.yy, 1, R.down_w),
+                pair_hop(R.yy, 2, R.attn_w),
+                pair_hop(R.yy, 3, R.out_w),
+            ]
+        R.arrive(R.up_w, R.down_w, R.attn_w, R.out_w)
         for one in y_hops:
             one.start()
         g = R.g
-        fill_padded(R)
         st = R.n.st
         st[r, c] = jnp.zeros((8, BLK), F32)
         gain = R.gain[...]
 
         def inner(b, carry):
             at = pl.ds(pl.multiple_of(b * BLK, BLK), BLK)
-            zb = R.z[at]
-            sums = row_sums(R.dm[at] * gain * R.y[at] * zb * sigmoid(zb))
+            sums = row_sums(R.dm[at] * gain * R.y[at] * R.za[at])
             st[r, c] = jnp.where(iota((8, BLK), 0) == b, sums, st[r, c])
             return carry
 
         lax.fori_loop(0, SIDE, inner, 0)
         close = grid_sum(R.n, r, c)
 
+        R.arrive(R.g, R.qr, R.lse, R.do)
         tb = R.tb
-        tb[:, pl.ds(LEN, HALO)] = jnp.zeros((6, HALO, 128), F32)
+        tb[:, pl.ds(LEN, HALO)] = jnp.zeros((4, HALO, 128), F32)
+        dkv_all = R.dkv_all
         keys = g[4].reshape(LEN, ADIM)
         values = g[5].reshape(LEN, ADIM)
         at = pl.ds(pl.multiple_of(c * BLK, BLK), BLK)
@@ -1272,16 +1377,34 @@
             ds = (p * (dp - jnp.sum(dp * p, axis=1, keepdims=True)) * SCALE).astype(BF)
             dk = dot_tn(ds, q)
             if h == 0:
-                tb[4, 0:LEN] = dk
-                tb[5, 0:LEN] = dv
+                dkv_all[0] = dk
+                dkv_all[1] = dv
             else:
-                tb[4, 0:LEN] = tb[4, 0:LEN] + dk
-                tb[5, 0:LEN] = tb[5, 0:LEN] + dv
+                dkv_all[0] = dkv_all[0] + dk
+                dkv_all[1] = dkv_all[1] + dv
             dq = dot_nn(ds, keys)
             R.db[:, 128 + 128 * h : 256 + 128 * h] = rope_turn(dq, cos, -sin).astype(BF)
 
+        R.arrive(R.xr, R.sr, R.states, R.down, R.u, R.du, R.dza)
+        fill_padded(R)
+        close_kv = scatter_tokens(R.kv, c, lambda j: dkv_all[:, pl.ds(pl.multiple_of(j * BLK, BLK), BLK)])
         scales = jnp.transpose(lax.rsqrt(R.s3[...] / (HEADS * HDIM) + EPSILON))
         inners = jnp.transpose(close())
+        for ref in (R.dgain, R.dskip, R.dconv, R.dhead, R.ds):
+            ref[...] = jnp.zeros_like(ref)
+
+        def through_norm(b):
+            at = pl.ds(pl.multiple_of(b * BLK, BLK), BLK)
+            yb, dm, zact = R.y[at], R.dm[at], R.za[at]
+            gated = yb * zact
+            scale = pick_column(scales, b)
+            dgated = scale * dm * gain - gated * (scale * scale * scale * pick_column(inners, b) / (HEADS * HDIM))
+            R.dgain[...] += jnp.sum(dm * gated * scale, axis=0, keepdims=True)
+            R.dy[at] = dgated * zact
+            R.zc.g[c, at] = (dgated * yb * R.dza[at]).astype(BF)
+
+        each(through_norm)
+        gather_cols(R.zc, r, c)
 
         step, close_d = scatter_rows(R.s, r, lambda t: R.down[t], lambda d: None)
         dstate, dpre_pad = R.dstate, R.dpre
@@ -1290,28 +1413,47 @@
         select = head_select()
         skip_row = per_head([R.skip[h] for h in range(HH)])
         rate_of = jnp.exp(scalar_rows(R.decay))
-        for ref in (R.dgain, R.dskip, R.dconv, R.dhead, R.ds):
-            ref[...] = jnp.zeros_like(ref)
         upto = jnp.where(iota((BLK, BLK), 0) >= iota((BLK, BLK), 1), 1.0, 0.0).astype(F32)
+
+        t = R.t
+
+        def t_rows(b):
+            return tb[:, pl.ds(pl.multiple_of(b * BLK, BLK), n)]
+
+        def t_core(slot):
+            return hop(t.cs.at[slot], t.cr.at[slot], t.ks.at[slot], t.kr.at[slot], col=flip(c, 1))
+
+        t_over = hop(t.xs, t.xr, t.ss, t.sr, col=flip(c, 2))
+
+        def leave_block(b):
+            e = flip(c, b)
+
+            @pl.when(lax.rem(e, 2) == 1)
+            def _():
+                slot = lax.div(e, 2)
+                t.cs[slot] = t_rows(b).astype(BF)
+                t_core(slot).start()
+
+        def pass_block(b):
+            @pl.when(flip(c, b) == 2)
+            def _():
+                t_core(1).wait_recv()
+                t.xs[...] = (t_rows(b) + t.cr[1].astype(F32)).astype(BF)
+                t_over.start()
 
         def block(i, carry):
             step(i)
             b = 3 - i
+
+            @pl.when(i > 0)
+            def _():
+                pass_block(b + 1)
+
             at = pl.ds(pl.multiple_of(b * BLK, BLK), BLK)
-            pre, taps = conv_block(R, b)
-            sig = sigmoid(pre)
-            u = pre * sig
+            u = R.u[at]
             raw, dt, rate, within, dt_c, within_c = step_block(R, b)
             bb, cb = state_cols(R, 0, b), state_cols(R, 1, b)
-            zb, yb, dm = R.z[at], R.y[at], R.dm[at]
-            zsig = sigmoid(zb)
-            zact = zb * zsig
-            gated = yb * zact
-            scale = pick_column(scales, b)
-            dgated = scale * dm * gain - gated * (scale * scale * scale * pick_column(inners, b) / (HEADS * HDIM))
-            R.dgain[...] += jnp.sum(dm * gated * scale, axis=0, keepdims=True)
-            dy = dgated * zact
-            R.da[at, 0:HW] = (dgated * yb * zsig * (1.0 + zb * (1.0 - zsig))).astype(BF)
+            dy = R.dy[at]
             R.dskip[...] += jnp.sum(dy * u, axis=0, keepdims=True)
             dyb = halves(dy)
             wide = column_heads(within_c)
@@ -1365,63 +1507,75 @@
             )
             dstate[...] = dst * elast + fine(dot_tn, cb, dygb)
             du = dx * dt_w + dy * skip_row
-            dpre = du * sig * (1.0 + pre * (1.0 - sig))
-            dpre_pad[at] = dpre
-            for j in range(4):
-                R.dconv[j : j + 1] += jnp.sum(dpre * taps[j], axis=0, keepdims=True)
-            chunk = dpre_pad[pl.ds(pl.multiple_of(b * BLK, BLK), BLK + 8)]
-            dxr = chunk[3 : 3 + BLK] * R.wc[0:1]
-            for j in (1, 2, 3):
-                dxr = dxr + chunk[3 - j : 3 - j + BLK] * R.wc[j : j + 1]
-            R.da[at, HW : 2 * HW] = dxr.astype(BF)
+            dpre_pad[at] = du * R.du[at]
+            leave_block(b)
+            wait_cols(R.zc, r, c, 3 - swapped(i))
             return carry
 
         lax.fori_loop(0, SIDE, block, 0)
+        total_kv = close_kv()
+        R.kvb[...] = total_kv.astype(BF)
+        kvb = R.kvb
+        kind, head = lax.div(r, 2), lax.rem(r, 2)
+
+        def kv_hop(d):
+            to = flip(r, d)
+            return hop(
+                kvb.at[lax.div(to, 2)], R.zkr.at[d - 1], R.ys.at[d - 1], R.yr.at[d - 1], row=to
+            )
+
+        for d in (1, 2, 3):
+
+            @pl.when(lax.rem(flip(r, d), 2) == kind)
+            def _():
+                kv_hop(d).start()
+
+        dkv = R.dkv
+        dkv[...] = jnp.zeros_like(dkv)
+
+        @pl.when(head == kind)
+        def _():
+            dkv[...] = jnp.where(kind == 0, total_kv[0], total_kv[1])
+
+        pass_block(0)
         R.dhead[...] += jnp.where(
             iota((8, 128), 1) == 2,
             dot_nt(select, jnp.broadcast_to(R.dskip[...], (8, HW)), HIGHEST)[:, :1],
             0.0,
         )
 
-        def token_rows(j):
-            return tb[:, pl.ds(pl.multiple_of(j * BLK, BLK), n)]
-
-        close_t = scatter_tokens(R.t, c, token_rows)
-        total = close_t()
+        for b in range(SIDE):
+            dpre = dpre_pad[b * BLK : (b + 1) * BLK]
+            dxr = jnp.zeros((BLK, HW), F32)
+            for j in range(4):
+                dxr = dxr + dpre_pad[3 - j + b * BLK : 3 - j + (b + 1) * BLK] * R.wc[j : j + 1]
+                R.dconv[j : j + 1] += jnp.sum(
+                    dpre * R.xpad[5 + j + b * BLK : 5 + j + (b + 1) * BLK], axis=0, keepdims=True
+                )
+            R.dxs[...] = dxr
+            R.da[b * BLK : (b + 1) * BLK] = R.dxs[...].astype(BF)
+
+        R.arrive(R.n1)
+        for j in range(SIDE):
+            R.dz_all[:, j * HW : (j + 1) * HW] = R.zc.g[j]
+        R.zw[...] = dot_tn(R.n1[...], R.dz_all[...]).astype(BF)
+        R.leave(R.dz_o, R.dz_all)
+        R.leave(R.z_w, R.zw)
+        t_core(0).wait_recv()
+        t_over.wait_recv()
+        total = t_rows(c) + t.cr[0].astype(F32) + t.xr[...].astype(F32)
         tob = R.tob
         tob[...] = total.astype(BF)
         mine = R.mine
         mine[...] = total
-        kind, head = lax.div(r, 2), lax.rem(r, 2)
 
         def bc_hop(d):
             return hop(tob.at[flip(r, d)], R.zbr.at[d - 1], R.zs.at[d - 1], R.zr.at[d - 1], row=flip(r, d))
 
-        def kv_hop(d):
-            to = flip(r, d)
-            return hop(
-                tob.at[SIDE + lax.div(to, 2), pl.ds(0, BLK)],
-                R.zkr.at[d - 1],
-                R.ys.at[d - 1],
-                R.yr.at[d - 1],
-                row=to,
-            )
-
         for d in (1, 2, 3):
             bc_hop(d).start()
 
-            @pl.when(lax.rem(flip(r, d), 2) == kind)
-            def _():
-                kv_hop(d).start()
-
         dpost = mine[r]
-        dkv = R.dkv
-        dkv[...] = jnp.zeros_like(dkv)
-
-        @pl.when(head == kind)
-        def _():
-            dkv[...] = mine[SIDE + kind, 0:BLK]
-
         for d in (1, 2, 3):
             bc_hop(d).wait_recv()
             dpost = dpost + R.zbr[d - 1].astype(F32)
@@ -1431,6 +1585,7 @@
                 kv_hop(d).wait_recv()
                 dkv[...] = dkv[...] + R.zkr[d - 1].astype(F32)
 
+        R.arrive(R.br, R.x1)
         br = R.br
         pre = br[13 : 13 + n, 0:128] * R.wcs[0:1]
         for j in (1, 2, 3):
@@ -1446,6 +1601,10 @@
         R.out[...] = (R.x1[...] + close_d()).astype(BF)
         dkv_v = dkv[...]
         R.db[:, 384:512] = jnp.where(kind == 0, rope_turn(dkv_v, cos, -sin), dkv_v).astype(BF)
+        wait_cols_sent(R.zc, r, c)
+        t_core(0).wait_send()
+        t_core(1).wait_send()
+        t_over.wait_send()
         for d in (1, 2, 3):
             bc_hop(d).wait_send()
 
@@ -1453,23 +1612,40 @@
             def _():
                 kv_hop(d).wait_send()
 
-        for one, theirs, out in zip(y_hops, (R.yy.A, R.yy.B, R.yy.C), (R.down_p, R.out_p, R.attn_p) if y_hops else ()):
+        for one, theirs, out in zip(y_hops, (R.yy.A, R.yy.B, R.yy.C, R.yy.D), (R.up_p, R.down_p, R.attn_p, R.out_p) if y_hops else ()):
             one.wait_recv()
-            out[...] = theirs[...]
+            R.leave(out, theirs)
             one.wait_send()
 
     scratch = dict(
         n=grid_scratch(),
         s=srows_scratch(),
-        yy=pair_scratch((LEN, 512), (SIDE * HW, 512), (256, 512)),
-        t=tokens_scratch(6, n, 128, low=BF),
+        yy=pair_scratch((256, 1024), (LEN, 512), (256, 512), (SIDE * HW, 512)),
+        zc=gcols_scratch(HW),
+        dy=pltpu.VMEM((LEN, HW), F32),
+        dxs=pltpu.VMEM((BLK, HW), F32),
+        dz_all=pltpu.VMEM((LEN, 768), BF),
+        zw=pltpu.VMEM((512, 768), BF),
+        t=dict(
+            cs=pltpu.VMEM((2, 4, n, 128), BF),
+            cr=pltpu.VMEM((2, 4, n, 128), BF),
+            xs=pltpu.VMEM((4, n, 128), BF),
+            xr=pltpu.VMEM((4, n, 128), BF),
+            ks=dma(2),
+            kr=dma(2),
+            ss=dma(),
+            sr=dma(),
+        ),
+        kv=tokens_scratch(2, BLK, 128, low=BF),
+        dkv_all=pltpu.VMEM((2, LEN, 128), F32),
+        kvb=pltpu.VMEM((2, BLK, 128), BF),
         xpad=pltpu.VMEM((LEN + 8, HW), F32),
         dpre=pltpu.VMEM((LEN + 8, HW), F32),
         dstate=pltpu.VMEM((STATE, HW), F32),
         dskip=pltpu.VMEM((1, HW), F32),
-        tb=pltpu.VMEM((6, LEN + HALO, 128), F32),
-        tob=pltpu.VMEM((6, n, 128), BF),
-        mine=pltpu.VMEM((6, n, 128), F32),
+        tb=pltpu.VMEM((4, LEN + HALO, 128), F32),
+        tob=pltpu.VMEM((4, n, 128), BF),
+        mine=pltpu.VMEM((4, n, 128), F32),
         dkv=pltpu.VMEM((BLK, 128), F32),
         zbr=pltpu.VMEM((3, n, 128), BF),
         zkr=pltpu.VMEM((3, BLK, 128), BF),
@@ -1479,7 +1655,7 @@
         yr=dma(3),
     )
     outs = dict(
-        da=((LEN, 2 * HW), BF),
+        da=((LEN, HW), BF),
         db=((BLK, 512), BF),
         ds=((16, LEN), BF),
         dgain=((1, HW), F32),
@@ -1488,11 +1664,16 @@
         dhead=((8, 128), F32),
         out=((BLK, 512), BF),
     )
+    early = dict(dz_o=((LEN, 768), BF), z_w=((512, 768), BF))
     if paired():
-        outs.update(down_p=((LEN, 512), BF), out_p=((SIDE * HW, 512), BF), attn_p=((256, 512), BF))
-    ins = dict(dm=dm, do=do, z=z, xr=xr, br=br, sr=sr, y=y, s3=s3, states=states, g=g, qr=qr, lse=lse, wc=wc, wcs=wcs)
-    ins.update(gain=gain, cos=cosine, sin=sine, x1=x1, down=down, down_w=down_w, out_w=out_w, attn_w=attn_w)
-    return launch(mixers_back, ins, outs, scratch, 10, dict(bias=bias, decay=decay, skip=skip))
+        early.update(up_p=((256, 1024), BF), down_p=((LEN, 512), BF), attn_p=((256, 512), BF))
+        early.update(out_p=((SIDE * HW, 512), BF))
+    ins = dict(dm=dm, za=za, y=y, s3=s3, wc=wc, wcs=wcs, gain=gain, cos=cosine, sin=sine)
+    late = dict(g=g, qr=qr, lse=lse, do=do, down_w=down_w, up_w=up_w, attn_w=attn_w, out_w=out_w, n1=n1, xr=xr, sr=sr, states=states)
+    late.update(u=u, du=du, dza=dza)
+    late.update(down=down, br=br, x1=x1)
+    smem = dict(bias=bias, decay=decay, skip=skip)
+    return launch(mixers_back, ins, outs, scratch, 10, smem, late, early)
 
 
 def dp_total(own, theirs):
@@ -1539,20 +1720,22 @@
         keyval_weight,
         step_w,
         conv_states,
+        cotangent,
     )
     heads = (conv_input, p.wcs, step_bias, decay_log, skip_gain, ssm_row, cosine, sine)
-    m = mixers_kernel(p.z, p.xr, p.br, p.sr, *heads, cotangent, wd)
+    m = mixers_kernel(p.z, p.xr, p.br, p.sr, *heads, p.dy, wd)
     f = forward_kernel(m.m, m.o, block_input, ffn_row, wo, wt, wg, wu, m.dh)
     b = backward_kernel(
-        f.dgu, wg, wu, f.x1, f.s2, ffn_row, cotangent, f.n2_all, wo, wt, f.hid, wd, m.dy, f.m_all, f.o_all
-    )
-    mixed = (p.z, p.xr, p.br, p.sr, m.y, m.s3, m.states, m.g_o, m.qr, m.lse)
-    k = mixers_back_kernel(b.dm, b.do, *mixed, *heads, f.x1, b.down, b.down_w, b.out_w, b.attn_w)
+        f.dgu, wg, wu, f.x1, f.s2, ffn_row, cotangent, f.n2_all, wo, wt, f.hid, wd, p.dy, f.m_all, f.o_all
+    )
+    mixed = (m.u, m.du, m.za, m.dza, p.xr, p.br, p.sr, m.y, m.s3, m.states, m.g_o, m.qr, m.lse)
+    k = mixers_back_kernel(b.dm, b.do, *mixed, *heads, f.x1, b.down, b.down_w, b.attn_w, b.up_w, p.n1, b.out_w)
     q = project_back_kernel(
         k.da,
         k.db,
         k.ds,
-        p.wa_o,
+        ssm_gate_weight,
+        ssm_input_weight,
         p.wb_o,
         step_w,
         block_input,
@@ -1565,14 +1748,16 @@
         k.dgain,
         k.dhead,
         k.dstates,
+        k.dz_o,
+        k.z_w,
     )
     pair = paired()
     gate_grad = dp_total(b.gate_w, b.gate_p if pair else None)
-    up_grad = dp_total(b.up_w, b.up_p if pair else None)
+    up_grad = dp_total(b.up_w, jnp.concatenate([b.up_p, k.up_p]) if pair else None)
     down_grad = dp_total(b.down_w, k.down_p if pair else None)
     out_grad = dp_total(b.out_w, k.out_p if pair else None)
     attn_grad = dp_total(b.attn_w, k.attn_p if pair else None)
-    z_grad = dp_total(q.zo, q.zq if pair else None)
+    z_grad = dp_total(k.z_w, q.zq if pair else None)
     x_grad = dp_total(q.xo, q.xq if pair else None)
     b_grad = dp_total(q.bo, q.bq if pair else None)
     step_grad = dp_total(q.so, q.sq if pair else None)

time: 463 us -> 408 us (0.88)
  Pallas kernels: 417 us -> 367 us
    pallas_call x6, Pallas kernels: 417 us -> 367 us  [launch(): pl.pallas_call(kernel, out_shape=[jax.ShapeDtypeStruct(*o) for o in (*out...]
    unnamed x55 -> x59, local copies, waits for them, and re-layouts: 13.2 us -> 12 us
where the time goes in v3:
time: 408 us; the launch traced here: 404 us
  Pallas kernels  367 us (90%)
  local copies, waits for them, and re-layouts  23.4 us (6%)
  other arithmetic  12 us (3%)
    pallas_call x6, Pallas kernels, launch(): pl.pallas_call(kernel, out_shape=[jax.ShapeDtypeStruct(*o) for o in (*out...  367 us
    unnamed x59, local copies, waits for them, and re-layouts  12 us
    add x7, other arithmetic, dp_total(): return own.astype(F32) + theirs.astype(F32)  9.7 us

profile of v3, /device:TPU:0, one launch (start us, length us, event | category | flops | bytes accessed | tf_op | source)
XLA Modules:
  0.0 403.5 jit_solution(11676293609667596160)
XLA Ops:
  0.7 0.7 reshape.52
  1.4 0.6 pad.4
  2.0 5.7 %fusion = (bf16[512,1,1024]{2,1,0:T(2,128)(2,1)S(1)}, bf16[512,1,1024]{2,1,0:T(2,128)(2,1)S(1)}) fusion(bf16[512,2,1024]{2,1,0:T(2,128)(2,1)} %param.39), kind=kLoop, calls=%fused_computation.12 | loop fusion | bytes 4194304 | tf_op jit(solution)/shard_map/slice | solution.py:1709
  7.7 2.1 copy_bitcast_fusion
  9.8 57.3 %project.1 = (f32[8,256]{1,0:T(8,128)}, f32[288,512]{1,0:T(8,128)}, f32[8,1024]{1,0:T(8,128)}, f32[4,128]{1,0:T(4,128)}, bf16[1024,512]{1,0:T(8,128)(2,1)}, /*in...) custom-call(bf16[256,512]{1,0:T(8,128)(2,1)} %refs_17_.1, ...), custom_call_target="tpu_custom_call" | custom-call | tf_op jit(solution)/shard_map/project/pallas_call | solution.py:168
  67.1 40.1 %mixers.1 = (bf16[1024,192]{1,0:T(8,128)(2,1)}, bf16[256,256]{1,0:T(8,128)(2,1)}, f32[8,256]{1,0:T(8,128)}, f32[2,256,128]{2,1,0:T(8,128)}, bf16[2,256,128]{2,1,...) custom-call(f32[288,512]{1,0:T(8,128)} %get-tuple-element.91.refs_0_, ...), custom_call_target="tpu_custom_call" | custom-call | tf_op jit(solution)/shard_map/mixers/pallas_call | solution.py:168
  107.3 73.0 %forward.1 = (f32[256,512]{1,0:T(8,128)}, f32[8,256]{1,0:T(8,128)}, bf16[1024,256]{1,0:T(8,128)(2,1)}, bf16[1024,512]{1,0:T(8,128)(2,1)}, bf16[4,1024,192]{2,1,0...) custom-call(bf16[1024,192]{1,0:T(8,128)(2,1)} %get-tuple-element.97.refs_0_, ...), custom_call_target="tpu_custom_call" | custom-call | tf_op jit(solution)/shard_map/forward/pallas_call | solution.py:168
  180.3 75.1 %backward.1 = (f32[256,512]{1,0:T(8,128)}, f32[1,512]{1,0:T(1,128)}, f32[1024,192]{1,0:T(8,128)}, bf16[256,256]{1,0:T(8,128)(2,1)}, bf16[256,512]{1,0:T(8,128)(2...) custom-call(bf16[1024,512]{1,0:T(8,128)(2,1)} %get-tuple-element.100, ...), custom_call_target="tpu_custom_call" | custom-call | tf_op jit(solution)/shard_map/backward/pallas_call | solution.py:168
  255.4 66.7 %mixers_back.1 = (bf16[1024,192]{1,0:T(8,128)(2,1)}, bf16[256,512]{1,0:T(8,128)(2,1)}, bf16[16,1024]{1,0:T(8,128)(2,1)}, f32[1,192]{1,0:T(1,128)}, f32[4,192]{1,...) custom-call(f32[1024,192]{1,0:T(8,128)} %get-tuple-element.107.refs_, ...), custom_call_target="tpu_custom_call" | custom-call | tf_op jit(solution)/shard_map/mixers_back/pallas_call | solution.py:168
  322.1 1.8 convert_add_fusion.5
  324.0 1.5 add_bitcast_fusion
  325.5 1.4 convert_add_fusion.1
  326.9 0.7 copy-done.7
  327.6 1.6 convert_add_fusion
  329.3 54.5 %project_back.1 = (f32[256,512]{1,0:T(8,128)}, f32[1,512]{1,0:T(1,128)}, f32[1,512]{1,0:T(1,128)}, f32[4,192]{1,0:T(4,128)}, f32[1,192]{1,0:T(1,128)}, /*index=5...) custom-call(bf16[1024,192]{1,0:T(8,128)(2,1)} %get-tuple-element.126, ...), custom_call_target="tpu_custom_call" | custom-call | tf_op jit(solution)/shard_map/project_back/pallas_call | solution.py:168
  383.8 0.9 convert_add_fusion.6
  384.7 0.6 reshape.55
  385.4 2.5 convert_add_fusion.3
  388.0 0.8 slice.26
  388.9 0.8 fusion.1
  389.7 1.3 convert_add_fusion.2
  391.9 5.2 %copy.47 = f32[512,2,1024]{2,1,0:T(2,128)} copy(f32[512,2,1024]{2,0,1:T(8,128)S(1)} %pad_maximum_fusion) | data formatting | bytes 8388608
  397.1 0.7 copy.62
  397.8 0.8 copy.63
  (59 shorter events, 5.5 us)
Async XLA Ops:
  255.4 66.7 %copy-start.4 = (bf16[256,512]{1,0:T(8,128)(2,1)S(1)}, bf16[256,512]{1,0:T(8,128)(2,1)}, u32[]{:S(2)}) copy-start(bf16[256,512]{1,0:T(8,128)(2,1)} %get-tuple-element.117.refs_18_) | copy-start | bytes 786436
  255.4 68.6 %copy-start.1 = (bf16[512,1024]{1,0:T(8,128)(2,1)S(1)}, bf16[512,1024]{1,0:T(8,128)(2,1)}, u32[]{:S(2)}) copy-start(bf16[512,1024]{1,0:T(8,128)(2,1)} %get-tuple-element.116.refs_17_) | copy-start | bytes 3145732
  255.4 68.5 %copy-start.14 = (bf16[256,1024]{1,0:T(8,128)(2,1)S(1)}, bf16[256,1024]{1,0:T(8,128)(2,1)}, u32[]{:S(2)}) copy-start(bf16[256,1024]{1,0:T(8,128)(2,1)} %get-tuple-element.159) | copy-start | bytes 1572868
  324.0 1.6 copy-start.2
  324.0 1.6 copy-start.10
  325.5 1.4 copy-start
  325.5 2.1 copy-start.7
  329.3 56.1 %copy-start.3 = (bf16[512,768]{1,0:T(8,128)(2,1)S(1)}, bf16[512,768]{1,0:T(8,128)(2,1)}, u32[]{:S(2)}) copy-start(bf16[512,768]{1,0:T(8,128)(2,1)} %get-tuple-element.135.refs_10_) | copy-start | bytes 2359300
  383.7 4.1 %copy-start.12 = (bf16[512,512]{1,0:T(8,128)(2,1)S(1)}, bf16[512,512]{1,0:T(8,128)(2,1)}, u32[]{:S(2)}) copy-start(bf16[512,512]{1,0:T(8,128)(2,1)} %get-tuple-element.144) | copy-start | bytes 1572868
  385.4 2.5 copy-start.13
  387.9 1.8 copy-start.8
  387.9 1.8 copy-start.9
  388.8 2.1 copy-start.5
  388.8 2.1 copy-start.6
  391.8 5.4 %copy-start.15 = (bf16[256,512]{1,0:T(8,128)(2,1)S(1)}, bf16[256,512]{1,0:T(8,128)(2,1)}, u32[]{:S(2)}) copy-start(bf16[256,512]{1,0:T(8,128)(2,1)} %get-tuple-element.228) | copy-start | bytes 786436
  391.8 6.0 %copy-start.11 = (f32[256,512]{1,0:T(8,128)S(1)}, f32[256,512]{1,0:T(8,128)}, u32[]{:S(2)}) copy-start(f32[256,512]{1,0:T(8,128)} %get-tuple-element.229) | copy-start | bytes 1572868
  391.8 6.8 %copy-start.19 = (f32[1,512]{1,0:T(1,128)S(1)}, f32[1,512]{1,0:T(1,128)}, u32[]{:S(2)}) copy-start(f32[1,512]{1,0:T(1,128)} %get-tuple-element.140) | copy-start | bytes 6148
  391.8 7.4 %copy-start.16 = (f32[4,192]{1,0:T(4,128)S(1)}, f32[4,192]{1,0:T(4,128)}, u32[]{:S(2)}) copy-start(f32[4,192]{1,0:T(4,128)} %get-tuple-element.237) | copy-start | bytes 9220
  391.8 8.0 %copy-start.18 = (f32[4,32]{1,0:T(4,128)S(1)}, f32[4,32]{1,0:T(4,128)}, u32[]{:S(2)}) copy-start(f32[4,32]{1,0:T(4,128)} %get-tuple-element.238) | copy-start | bytes 1540
  391.8 8.6 %copy-start.23 = (f32[1,3]{1,0:T(1,128)S(1)}, f32[1,3]{1,0:T(1,128)}, u32[]{:S(2)}) copy-start(f32[1,3]{1,0:T(1,128)} %get-tuple-element.150) | copy-start | bytes 40
  391.8 9.1 %copy-start.22 = (f32[1,3]{1,0:T(1,128)S(1)}, f32[1,3]{1,0:T(1,128)}, u32[]{:S(2)}) copy-start(f32[1,3]{1,0:T(1,128)} %get-tuple-element.151) | copy-start | bytes 40
  391.8 9.6 %copy-start.21 = (f32[1,3]{1,0:T(1,128)S(1)}, f32[1,3]{1,0:T(1,128)}, u32[]{:S(2)}) copy-start(f32[1,3]{1,0:T(1,128)} %get-tuple-element.152) | copy-start | bytes 40
  391.9 10.1 %copy-start.20 = (f32[1,192]{1,0:T(1,128)S(1)}, f32[1,192]{1,0:T(1,128)}, u32[]{:S(2)}) copy-start(f32[1,192]{1,0:T(1,128)} %get-tuple-element.153) | copy-start | bytes 2308
  391.9 10.6 %copy-start.17 = (f32[1,512]{1,0:T(1,128)S(1)}, f32[1,512]{1,0:T(1,128)}, u32[]{:S(2)}) copy-start(f32[1,512]{1,0:T(1,128)} %get-tuple-element.156) | copy-start | bytes 6148
